TPU v7x, 128 devices: a whole 4x4x4 slice. The times are simulated.
128 devices in a mesh: row: 8 (over z, x_hi), col: 16 (over y, x_lo, core).
Axes of the slice: x: 4 (x_hi: 2, x_lo: 2; x = x_hi * 2 + x_lo), y: 4, z: 4, core: 2. Of those that a mesh axis runs over, the one named last changes fastest.
Arguments:
- object_now: float32 [2, 2048, 8192], P(None, 'row', 'col'), may hold values from -5 to 5
- object_prev: float32 [2, 2048, 8192], P(None, 'row', 'col'), may hold values from -5 to 5
- probe: float32 [2, 256, 256], replicated, may hold values from -4 to 4
- amplitudes: float32 [8, 16, 4, 256, 256], P('row', 'col'), may hold values from 0.2 to 3
- pos_row: int32 [8, 16, 4], P('row', 'col'), may hold values from 0 to 255
- pos_col: int32 [8, 16, 4], P('row', 'col'), may hold values from 0 to 511
- counts: int32 [8, 16], P('row', 'col'), may hold values from 1 to 4, as said below
Outputs:
- object_new: float32 [2, 2048, 8192], P(None, 'row', 'col')
- probe_new: float32 [2, 256, 256], replicated
Inputs may be any that keep to these rules, and one draw needn't show every extreme that they name: Tile (r, c) uses its first counts[r, c] slots; some tile uses all 4.
All inputs are finite; a program needn't handle non-finite values.
Results may differ from a plain program's by a relative error of at most 0.0003.
Values sent between devices are 32-bit elements; how exact they have to be, the bound alone decides.
No kernel may reach another device: no remote copies, remote signals or barrier semaphores. Data moves between devices by JAX's collectives and lax.ppermute only.
A program may use at most 384 MiB of HBM per device.

v0:
```python
import math

import jax
import jax.numpy as jnp
from jax import lax
from jax.sharding import PartitionSpec as P

LEVELS = 4


MOMENTUM = 0.6
STEP_OBJECT = 0.5
PROBE_STEP = 2.0
THRESHOLD = 0.3
FLOOR = 0.5


def extended_2(block, sides, width):
    for axis, dim in sides:
        count = lax.axis_size(axis)
        forward = [(i, i + 1) for i in range(count - 1)]
        backward = [(target, source) for source, target in forward]
        low = lax.ppermute(
            lax.slice_in_dim(block, block.shape[dim] - width, None, axis=dim), axis, forward
        )
        high = lax.ppermute(lax.slice_in_dim(block, 0, width, axis=dim), axis, backward)
        block = jnp.concatenate([low, block, high], axis=dim)
    return block


def dft_tables(length):
    points = jnp.arange(length, dtype=jnp.int32)
    phase_index = points[:, None] * points[None, :] % length
    angles = phase_index.astype(jnp.float32) * (-2.0 * math.pi / length)
    factor = 1.0 / math.sqrt(length)
    return (jnp.cos(angles) * factor, jnp.sin(angles) * factor)


def left_product(table, values):
    return jnp.einsum("jk,bkl->bjl", table, values, precision=lax.Precision.HIGHEST)


def right_product(values, table):
    return jnp.einsum("bjl,lm->bjm", values, table, precision=lax.Precision.HIGHEST)


def transform(real_part, imag_part, table_real, table_imag):
    left_real = left_product(table_real, real_part) - left_product(table_imag, imag_part)
    left_imag = left_product(table_real, imag_part) + left_product(table_imag, real_part)
    out_real = right_product(left_real, table_real) - right_product(left_imag, table_imag)
    out_imag = right_product(left_real, table_imag) + right_product(left_imag, table_real)
    return (out_real, out_imag)


def patch_gradients(windows, probe, amplitude, live_mask, table_real, table_imag):
    window_real = windows[:, 0]
    window_imag = windows[:, 1]
    probe_real = probe[0]
    probe_imag = probe[1]
    exit_real = probe_real * window_real - probe_imag * window_imag
    exit_imag = probe_real * window_imag + probe_imag * window_real
    far_real, far_imag = transform(exit_real, exit_imag, table_real, table_imag)
    modulus = jnp.sqrt(far_real * far_real + far_imag * far_imag)
    remain = 1.0 - amplitude / jnp.maximum(modulus, FLOOR)
    back_real, back_imag = transform(far_real * remain, far_imag * remain, table_real, -table_imag)
    weight = live_mask[:, None, None]
    back_real = back_real * weight
    back_imag = back_imag * weight
    object_real = probe_real * back_real + probe_imag * back_imag
    object_imag = probe_real * back_imag - probe_imag * back_real
    probe_real_term = jnp.sum(window_real * back_real + window_imag * back_imag, axis=0)
    probe_imag_term = jnp.sum(window_real * back_imag - window_imag * back_real, axis=0)
    return (
        jnp.stack([object_real, object_imag], axis=1),
        jnp.stack([probe_real_term, probe_imag_term]),
    )


def scatter_patches(gradient, terms, starts_row, starts_col):

    def add_patch(slot_index, running):
        corner = (jnp.int32(0), starts_row[slot_index], starts_col[slot_index])
        current = lax.dynamic_slice(running, corner, terms.shape[1:])
        return lax.dynamic_update_slice(running, current + terms[slot_index], corner)

    return lax.fori_loop(0, terms.shape[0], add_patch, gradient)


def shrink(detail):
    magnitude = jnp.sqrt(detail[0] * detail[0] + detail[1] * detail[1])
    factor = jnp.maximum(magnitude - THRESHOLD, 0.0) / jnp.maximum(magnitude, THRESHOLD)
    return detail * factor[None]


def haar_shrink(field, depth_left):
    if depth_left == 0:
        return field
    height = field.shape[1] // 2
    breadth = field.shape[2] // 2
    blocks = field.reshape(2, height, 2, breadth, 2)
    north_west = blocks[:, :, 0, :, 0]
    north_east = blocks[:, :, 0, :, 1]
    south_west = blocks[:, :, 1, :, 0]
    south_east = blocks[:, :, 1, :, 1]
    coarse = (north_west + north_east + south_west + south_east) * 0.5
    across = shrink((north_west - north_east + south_west - south_east) * 0.5)
    downward = shrink((north_west + north_east - south_west - south_east) * 0.5)
    diagonal = shrink((north_west - north_east - south_west + south_east) * 0.5)
    coarse = haar_shrink(coarse, depth_left - 1)
    corner_one = (coarse + across + downward + diagonal) * 0.5
    corner_two = (coarse - across + downward - diagonal) * 0.5
    corner_three = (coarse + across - downward - diagonal) * 0.5
    corner_four = (coarse - across - downward + diagonal) * 0.5
    upper_pair = jnp.stack([corner_one, corner_two], axis=-1)
    lower_pair = jnp.stack([corner_three, corner_four], axis=-1)
    return jnp.stack([upper_pair, lower_pair], axis=2).reshape(2, 2 * height, 2 * breadth)


def fold_rims(extended, axis_dim, margin):
    length = extended.shape[axis_dim] - 4 * margin
    interior = lax.slice_in_dim(extended, 2 * margin, 2 * margin + length, axis=axis_dim)
    leading = lax.slice_in_dim(extended, 0, margin, axis=axis_dim)
    trailing = lax.slice_in_dim(extended, length + 3 * margin, length + 4 * margin, axis=axis_dim)
    head_part = lax.slice_in_dim(interior, 0, margin, axis=axis_dim) + leading
    middle_part = lax.slice_in_dim(interior, margin, length - margin, axis=axis_dim)
    tail_part = lax.slice_in_dim(interior, length - margin, length, axis=axis_dim) + trailing
    return jnp.concatenate([head_part, middle_part, tail_part], axis=axis_dim)


def on_device(object_now, object_prev, probe, amplitudes, pos_row, pos_col, counts):
    momentum_point = object_now + MOMENTUM * (object_now - object_prev)
    patch_size = probe.shape[1]
    margin = patch_size // 2
    extended = extended_2(momentum_point, (("row", 1), ("col", 2)), margin)
    table_real, table_imag = dft_tables(patch_size)
    starts_row = pos_row[0, 0]
    starts_col = pos_col[0, 0]
    live_count = counts[0, 0]
    amplitude = amplitudes[0, 0]
    slot_total = starts_row.shape[0]
    windows = jax.vmap(
        lambda row_start, col_start: lax.dynamic_slice(
            extended, (jnp.int32(0), row_start, col_start), (2, patch_size, patch_size)
        )
    )(starts_row, starts_col)
    live_mask = (jnp.arange(slot_total, dtype=jnp.int32) < live_count).astype(jnp.float32)
    object_terms, probe_sum = patch_gradients(
        windows, probe, amplitude, live_mask, table_real, table_imag
    )
    gradient = scatter_patches(jnp.zeros_like(extended), object_terms, starts_row, starts_col)
    gathered = extended_2(gradient, (("row", 1), ("col", 2)), margin)
    tile_gradient = fold_rims(fold_rims(gathered, 1, margin), 2, margin)
    probe_total = lax.psum(probe_sum, ("row", "col"))
    devices = lax.axis_size("row") * lax.axis_size("col")
    object_new = haar_shrink(momentum_point - STEP_OBJECT * tile_gradient, LEVELS)
    probe_new = probe - PROBE_STEP / (slot_total * devices) * probe_total
    return (object_new, probe_new)


def solution(mesh):
    in_specs = (
        P(None, "row", "col"),
        P(None, "row", "col"),
        P(),
        P("row", "col", None, None, None),
        P("row", "col", None),
        P("row", "col", None),
        P("row", "col"),
    )
    out_specs = (P(None, "row", "col"), P())
    return jax.shard_map(
        on_device, mesh=mesh, in_specs=in_specs, out_specs=out_specs, check_vma=False
    )
```

profile of v0, /device:TPU:1, one launch (start us, length us, event | category | flops | bytes accessed | tf_op | source)
XLA Modules:
  0.0 833.0 jit_solution(7397219706093608372)
XLA Ops:
  9.1 5.6 collective-permute-start
  16.1 9.2 %collective-permute-done = f32[2,128,512]{2,1,0:T(8,128)S(1)} collective-permute-done((f32[2,128,512]{2,1,0:T(8,128)S(1)}, f32[2,128,512]{2,1,0:T(8,128)S(1)}, u32[]{:S(2)}, u32[]{:S(2)}) %collective-permute-start) | collective-permute-done | bytes 524320 | tf_op jit(solution)/shard_map/ppermute | solution.py:23
  25.3 13.5 %collective-permute-done.1 = f32[2,128,512]{2,1,0:T(8,128)S(1)} collective-permute-done((f32[2,128,512]{2,1,0:T(8,128)S(1)}, f32[2,128,512]{2,1,0:T(8,128)S(1)}, u32[]{:S(2)}, u32[]{:S(2)}) %collective-permute-start.1) | collective-permute-done | bytes 524320 | tf_op jit(solution)/shard_map/ppermute | solution.py:26
  39.9 4.5 collective-permute-start.2
  44.4 1.9 collective-permute-start.3
  47.2 3.6 collective-permute-done.2
  50.8 7.3 collective-permute-done.3
  58.2 3.1 pad_maximum_fusion
  61.3 16.3 %while.15 = (s32[]{:T(128)}, f32[2,512,768]{2,1,0:T(8,128)}, s32[4,3]{1,0:T(4,128)S(1)}, f32[4,2,256,256]{3,2,0,1:T(8,128)}, s32[]{:T(128)}) while((s32[]{:T(128)}, f32[2,512,768]{2,1,0:T(8,128)}, s32[4,3]{1,0:T(4,128)S(1)}, f32[4,2,256,256]{3,2,0,1:T(8,128)}, s32[]{:T(128)}) %tuple.124), condition=%wide.while_cond, body=%wide.while_body.sunk | while | flops 2 | bytes 1049717 | solution.py:142
  61.9 3.5 bitcast_dynamic-update-slice_fusion.2
  65.9 3.5 bitcast_dynamic-update-slice_fusion.2
  70.0 3.5 bitcast_dynamic-update-slice_fusion.2
  74.1 3.5 bitcast_dynamic-update-slice_fusion.2
  77.5 4.4 fusion.47
  82.0 2.8 fusion.5
  84.8 2.7 fusion.30
  87.5 2.7 fusion.45
  90.2 11.5 %fusion.43 = f32[4,256,256]{2,1,0:T(8,128)S(1)} fusion(f32[4,2,256,256]{3,2,0,1:T(8,128)S(1)} %copy-done.1, f32[256,256]{1,0:T(8,128)S(1)} %get-tuple-element.242, f32[256,256]{1,0:T(8,128)S(1)} %get-tuple-element.241), kind=kOutput, calls=%fused_computation.91 | convolution fusion | flops 807075840 | bytes 3670016 | tf_op jit(solution)/shard_map/jk,bkl->bjl/dot_general | solution.py:40
  101.8 2.8 fusion.4
  104.6 2.7 convolution_subtract_fusion.2
  107.3 3.2 fusion.18
  110.5 2.9 fusion.36
  113.4 2.7 fusion.40
  116.1 2.7 fusion.3
  118.8 2.7 fusion.25
  121.4 2.7 fusion.38
  124.1 3.1 fusion.2
  127.2 2.8 fusion.1
  130.0 3.4 fusion.15
  136.8 52.3 %while.14 = (s32[]{:T(128)}, f32[2,512,768]{2,1,0:T(8,128)}, s32[4]{0:T(128)S(1)}, s32[4]{0:T(128)S(1)}, f32[4,2,256,256]{3,2,0,1:T(8,128)}, /*index=5*/s32[]{:T(128)}, s32[]{:T(128)}, s32[]{:T(128)}, s32[]{:T(128)}) while((s32[]{:T(128)}, f32[2,512,768]{2,1,0:T(8,128)}, s32[4]{0:T(128)S(1)}, s32[4]{0:T(128)S(1)}, ...), condition=%wide.region_1.2_spmd, body=%wide.region_0.1_spmd.sunk | while | flops 131080 | bytes 2621649 | solution.py:86
  143.4 6.4 dynamic_update_slice.8
  156.4 6.5 dynamic_update_slice.8
  169.5 6.2 dynamic_update_slice.8
  182.3 6.8 dynamic_update_slice.8
  190.7 3.9 collective-permute-start.4
  196.0 7.6 collective-permute-done.4
  203.8 18.8 %collective-permute-done.5 = f32[2,128,768]{2,1,0:T(8,128)S(1)} collective-permute-done((f32[2,128,768]{2,1,0:T(8,128)S(1)}, f32[2,128,768]{2,1,0:T(8,128)S(1)}, u32[]{:S(2)}, u32[]{:S(2)}) %collective-permute-start.5) | collective-permute-done | bytes 786464 | tf_op jit(solution)/shard_map/ppermute | solution.py:26
  222.7 2.1 copy-done.2
  226.0 12.4 %collective-permute-start.6 = (f32[2,768,128]{2,1,0:T(8,128)}, f32[2,768,128]{2,1,0:T(8,128)S(1)}, u32[]{:S(2)}, u32[]{:S(2)}) collective-permute-start(f32[2,768,128]{2,1,0:T(8,128)} %get-tuple-element.208), channel_id=1, source_target_pairs={{0,1},{1,2},{2,3},{3,4},{4,5},{5,6},{6,7},{7,8},{8,9},{9,10},{10,1... | collective-permute-start | bytes 2359304 | tf_op jit(solution)/shard_map/ppermute | solution.py:23
  241.3 145.0 %all-reduce.2.cloned.1.call-done = f32[2,256,256]{2,1,0:T(8,128)} async-done(((f32[2,256,256]{2,1,0:T(8,128)}), f32[2,256,256]{2,1,0:T(8,128)}) %all-reduce.2.cloned.1.call-update) | async-done | bytes 524304 | tf_op jit(solution)/shard_map/psum | solution.py:153
  388.1 2.4 maximum_add_fusion
  390.8 68.5 %reshape.1319 = f32[2,128,2,256,2]{4,3,2,1,0:T(8,128)} reshape(f32[2,256,512]{2,1,0:T(8,128)S(1)} %fusion.9) | data formatting | bytes 2097152 | tf_op jit(solution)/shard_map/reshape | solution.py:100
  459.4 84.4 %fusion.171 = (f32[2,128,1,256,1]{4,3,2,1,0:T(8,128)}, f32[2,128,1,256,1]{4,3,2,1,0:T(8,128)}, f32[2,128,1,256,1]{4,3,2,1,0:T(8,128)}, f32[2,128,1,256,1]{4,3,2,1,0:T(8,128)}) fusion(f32[2,128,2,256,2]{4,3,2,1,0:T(8,128)} %reshape.1319), kind=kLoop, calls=%fused_computation.325 | loop fusion | bytes 2097152 | tf_op jit(solution)/shard_map/slice | solution.py:102
  543.7 19.4 %copy.205 = f32[2,128,1,256,1]{3,1,4,2,0:T(8,128)S(1)} copy(f32[2,128,1,256,1]{4,3,2,1,0:T(8,128)} %get-tuple-element.198) | data formatting | bytes 524288
  563.1 19.4 %copy.206 = f32[2,128,1,256,1]{3,1,4,2,0:T(8,128)S(1)} copy(f32[2,128,1,256,1]{4,3,2,1,0:T(8,128)} %get-tuple-element.199) | data formatting | bytes 524288
  582.5 19.4 %copy.204 = f32[2,128,1,256,1]{3,1,4,2,0:T(8,128)S(1)} copy(f32[2,128,1,256,1]{4,3,2,1,0:T(8,128)} %get-tuple-element.200) | data formatting | bytes 524288
  601.9 19.4 %copy.207 = f32[2,128,1,256,1]{3,1,4,2,0:T(8,128)S(1)} copy(f32[2,128,1,256,1]{4,3,2,1,0:T(8,128)} %get-tuple-element.201) | data formatting | bytes 524288
  623.8 18.0 %mul.1046 = f32[2,64,2,128,2]{4,3,2,1,0:T(8,128)} reshape(f32[2,128,1,256,1]{3,1,4,2,0:T(8,128)S(1)} %get-tuple-element.234) | data formatting | bytes 524288 | tf_op jit(solution)/shard_map/mul | solution.py:105
  641.9 24.3 %fusion.172 = (f32[2,64,1,128,1]{4,3,2,1,0:T(8,128)}, f32[2,64,1,128,1]{4,3,2,1,0:T(8,128)}, f32[2,64,1,128,1]{4,3,2,1,0:T(8,128)}, f32[2,64,1,128,1]{4,3,2,1,0:T(8,128)}) fusion(f32[2,64,2,128,2]{4,3,2,1,0:T(8,128)} %mul.1046), kind=kLoop, calls=%fused_computation.326 | loop fusion | bytes 524288 | tf_op jit(solution)/shard_map/slice | solution.py:102
  666.2 5.2 copy.209
  671.4 5.2 copy.210
  676.6 5.2 copy.208
  681.8 5.2 copy.211
  689.6 5.7 mul.1048
  695.3 7.6 fusion.174
  703.0 2.3 copy.213
  705.2 2.3 copy.214
  707.5 2.3 copy.212
  717.1 2.7 copy.182
  719.9 4.1 reshape.1321
  724.1 8.7 %copy.183 = f32[2,64,2,128,2]{4,3,2,1,0:T(8,128)} copy(f32[2,64,2,128,2]{3,1,0,4,2:T(8,128)S(1)} %pad_maximum_fusion.10) | data formatting | bytes 524288 | tf_op jit(solution)/shard_map/stack | solution.py:116
  732.8 12.8 %reshape.1322 = f32[2,128,256,1]{2,1,0,3:T(8,128)S(1)} reshape(f32[2,64,2,128,2]{4,3,2,1,0:T(8,128)} %copy.183) | data formatting | bytes 524288 | tf_op jit(solution)/shard_map/reshape | solution.py:116
  746.0 32.7 %copy.184 = f32[2,128,2,256,2]{4,3,2,1,0:T(8,128)} copy(f32[2,128,2,256,2]{3,1,0,4,2:T(8,128)S(1)} %pad_maximum_fusion.4) | data formatting | bytes 2097152 | tf_op jit(solution)/shard_map/stack | solution.py:116
  778.7 47.2 %reshape.1323 = f32[2,256,512]{2,1,0:T(8,128)} reshape(f32[2,128,2,256,2]{4,3,2,1,0:T(8,128)} %copy.184) | data formatting | bytes 2097152 | tf_op jit(solution)/shard_map/reshape | solution.py:116
  (123 shorter events, 43.2 us)
Async XLA Ops:
  7.2 379.1 %all-reduce.2.cloned.1.call-start = ((), (), s32[]{:S(2)}) async-start(), calls=%async_computation | async-start | bytes 1048576 | tf_op jit(solution)/shard_map/psum | solution.py:153
  9.0 37.4 %copy-start.14 = (s32[1,1,4]{2,1,0:T(1,128)S(1)}, s32[1,1,4]{2,1,0:T(1,128)}, u32[]{:S(2)}) copy-start(s32[1,1,4]{2,1,0:T(1,128)} %param.13) | copy-start | bytes 52
  9.0 37.4 %copy-start.15 = (s32[1,1,4]{2,1,0:T(1,128)S(1)}, s32[1,1,4]{2,1,0:T(1,128)}, u32[]{:S(2)}) copy-start(s32[1,1,4]{2,1,0:T(1,128)} %param.14) | copy-start | bytes 52
  9.0 38.2 %copy-start.3 = (f32[2,256,256]{2,1,0:T(8,128)S(1)}, f32[2,256,256]{2,1,0:T(8,128)}, u32[]{:S(2)}) copy-start(f32[2,256,256]{2,1,0:T(8,128)} %param.11) | copy-start | bytes 1572868
  9.1 16.2 %collective-permute-start = (f32[2,128,512]{2,1,0:T(8,128)S(1)}, f32[2,128,512]{2,1,0:T(8,128)S(1)}, u32[]{:S(2)}, u32[]{:S(2)}) collective-permute-start(f32[2,128,512]{2,1,0:T(8,128)S(1)} %get-tuple-element.239), channel_id=1, source_target_pairs={{0,16},{16,32},{32,48},{48,64},{64,80},{80,96},{96,112},{1,17},{17... | collective-permute-start | bytes 1572872 | tf_op jit(solution)/shard_map/ppermute | solution.py:23
  14.8 24.1 %collective-permute-start.1 = (f32[2,128,512]{2,1,0:T(8,128)S(1)}, f32[2,128,512]{2,1,0:T(8,128)S(1)}, u32[]{:S(2)}, u32[]{:S(2)}) collective-permute-start(f32[2,128,512]{2,1,0:T(8,128)S(1)} %get-tuple-element.240), channel_id=1, source_target_pairs={{16,0},{32,16},{48,32},{64,48},{80,64},{96,80},{112,96},{17,1},{33... | collective-permute-start | bytes 1572872 | tf_op jit(solution)/shard_map/ppermute | solution.py:26
  39.9 11.0 %collective-permute-start.2 = (f32[2,512,128]{2,1,0:T(8,128)}, f32[2,512,128]{2,1,0:T(8,128)}, u32[]{:S(2)}, u32[]{:S(2)}) collective-permute-start(f32[2,512,128]{2,1,0:T(8,128)} %get-tuple-element.224), channel_id=1, source_target_pairs={{0,1},{1,2},{2,3},{3,4},{4,5},{5,6},{6,7},{7,8},{8,9},{9,10},{10,1... | collective-permute-start | bytes 1572872 | tf_op jit(solution)/shard_map/ppermute | solution.py:23
  44.4 13.7 %collective-permute-start.3 = (f32[2,512,128]{2,1,0:T(8,128)}, f32[2,512,128]{2,1,0:T(8,128)}, u32[]{:S(2)}, u32[]{:S(2)}) collective-permute-start(f32[2,512,128]{2,1,0:T(8,128)} %get-tuple-element.225), channel_id=1, source_target_pairs={{1,0},{2,1},{3,2},{4,3},{5,4},{6,5},{7,6},{8,7},{9,8},{10,9},{11,1... | collective-permute-start | bytes 1572872 | tf_op jit(solution)/shard_map/ppermute | solution.py:26
  77.5 4.4 copy-start.1
  101.8 5.5 copy-start.16
  189.1 14.5 %copy-start = (f32[2,512,768]{2,1,0:T(8,128)S(1)}, f32[2,512,768]{2,1,0:T(8,128)}, u32[]{:S(2)}) copy-start(f32[2,512,768]{2,1,0:T(8,128)} %get-tuple-element.96) | copy-start | bytes 9437188
  190.7 12.8 %collective-permute-start.4 = (f32[2,128,768]{2,1,0:T(8,128)S(1)}, f32[2,128,768]{2,1,0:T(8,128)S(1)}, u32[]{:S(2)}, u32[]{:S(2)}) collective-permute-start(f32[2,128,768]{2,1,0:T(8,128)S(1)} %get-tuple-element.215), channel_id=1, source_target_pairs={{0,16},{16,32},{32,48},{48,64},{64,80},{80,96},{96,112},{1,17},{17... | collective-permute-start | bytes 2359304 | tf_op jit(solution)/shard_map/ppermute | solution.py:23
  194.7 27.9 %collective-permute-start.5 = (f32[2,128,768]{2,1,0:T(8,128)S(1)}, f32[2,128,768]{2,1,0:T(8,128)S(1)}, u32[]{:S(2)}, u32[]{:S(2)}) collective-permute-start(f32[2,128,768]{2,1,0:T(8,128)S(1)} %get-tuple-element.214), channel_id=1, source_target_pairs={{16,0},{32,16},{48,32},{64,48},{80,64},{96,80},{112,96},{17,1},{33... | collective-permute-start | bytes 2359304 | tf_op jit(solution)/shard_map/ppermute | solution.py:26
  222.7 2.1 copy-start.2
  226.0 162.1 %collective-permute-start.6 = (f32[2,768,128]{2,1,0:T(8,128)}, f32[2,768,128]{2,1,0:T(8,128)S(1)}, u32[]{:S(2)}, u32[]{:S(2)}) collective-permute-start(f32[2,768,128]{2,1,0:T(8,128)} %get-tuple-element.208), channel_id=1, source_target_pairs={{0,1},{1,2},{2,3},{3,4},{4,5},{5,6},{6,7},{7,8},{8,9},{9,10},{10,1... | collective-permute-start | bytes 2359304 | tf_op jit(solution)/shard_map/ppermute | solution.py:23
  238.5 149.7 %collective-permute-start.7 = (f32[2,768,128]{2,1,0:T(8,128)}, f32[2,768,128]{2,1,0:T(8,128)}, u32[]{:S(2)}, u32[]{:S(2)}) collective-permute-start(f32[2,768,128]{2,1,0:T(8,128)} %get-tuple-element.209), channel_id=1, source_target_pairs={{1,0},{2,1},{3,2},{4,3},{5,4},{6,5},{7,6},{8,7},{9,8},{10,9},{11,1... | collective-permute-start | bytes 2359304 | tf_op jit(solution)/shard_map/ppermute | solution.py:26
  719.9 4.1 copy-start.8
  719.9 4.1 copy-start.9
  719.9 4.1 copy-start.10
  719.9 4.1 copy-start.11
  719.9 4.1 copy-start.12
  719.9 4.1 copy-start.13
  732.8 12.8 %copy-start.4 = (f32[2,128,1,256,1]{3,1,4,2,0:T(8,128)S(1)}, f32[2,128,1,256,1]{3,1,4,2,0:T(8,128)}, u32[]{:S(2)}) copy-start(f32[2,128,1,256,1]{3,1,4,2,0:T(8,128)} %get-tuple-element.231) | copy-start | bytes 786436
  732.8 12.8 %copy-start.5 = (f32[2,128,1,256,1]{3,1,4,2,0:T(8,128)S(1)}, f32[2,128,1,256,1]{3,1,4,2,0:T(8,128)}, u32[]{:S(2)}) copy-start(f32[2,128,1,256,1]{3,1,4,2,0:T(8,128)} %get-tuple-element.233) | copy-start | bytes 786436
  732.8 12.8 %copy-start.6 = (f32[128,256]{1,0:T(8,128)S(1)}, f32[128,256]{1,0:T(8,128)}, u32[]{:S(2)}) copy-start(f32[128,256]{1,0:T(8,128)} %multiply_bitcast_fusion) | copy-start | bytes 393220
  732.8 12.8 %copy-start.7 = (f32[128,256]{1,0:T(8,128)S(1)}, f32[128,256]{1,0:T(8,128)}, u32[]{:S(2)}) copy-start(f32[128,256]{1,0:T(8,128)} %multiply_bitcast_fusion.1) | copy-start | bytes 393220
Sparse Core Ops, SparseCore 0:
  241.4 144.8 all-reduce.1
where the time goes:
time: 847 us; the launch traced here: 833 us
  local copies, waits for them, and re-layouts  481 us (57%)
  waiting for transfers between devices  205 us (24%)
  matrix products  55.7 us (7%)
  starting transfers between devices  33 us (4%)
  other arithmetic  27.4 us (3%)
  loops' own time  15.6 us (2%)
  between operations  15.6 us (2%)
    psum x1, waiting for transfers between devices, on_device(): probe_total = lax.psum(probe_sum, ('row', 'col'))  145 us
    slice x4, local copies, waits for them, and re-layouts, haar_shrink(): north_east = blocks[:, :, 0, :, 1]  117 us
    unnamed x53, local copies, waits for them, and re-layouts  110 us
    reshape x1, local copies, waits for them, and re-layouts, haar_shrink(): blocks = field.reshape(2, height, 2, breadth, 2)  68.5 us
    reshape x4, local copies, waits for them, and re-layouts, haar_shrink(): jnp.stack([upper_pair, lower_pair], axis=2)  64.7 us
    another operation x4, local copies, waits for them, and re-layouts, haar_shrink(): jnp.stack([upper_pair, lower_pair], axis=2)  44.6 us
    ppermute x4, waiting for transfers between devices, extended_2(): lax.ppermute(lax.slice_in_dim(block, 0, width, axis=dim), axis, backward)  39.6 us
    dot_general x8, matrix products, left_product(): jnp.einsum('jk,bkl->bjl', table, values, precision=lax.Precision.HIGHEST)  32.9 us
  transfers between devices with their start and end apart: 9, of which 7 were waited for; matrix products, arithmetic and copies ran while one was open for 0% of the time, Pallas kernels for 0%

commit v1 on v0

v1 whole, which is shorter than its diff:
```python
import math

import jax
import jax.numpy as jnp
import ml_dtypes
import numpy as np
from jax import lax
from jax.experimental import pallas as pl
from jax.experimental.pallas import tpu as pltpu
from jax.sharding import PartitionSpec as P

LEVELS = 4
MOMENTUM = 0.6
STEP_OBJECT = 0.5
PROBE_STEP = 2.0
THRESHOLD = 0.3
FLOOR = 0.5

AXES = ("row", "pair", "core")
CHIPS = ("row", "pair")
LANES = 128
TILE = 8
VMEM_LIMIT = 28 * 1024 * 1024


def split_table(table):
    high = table.astype(ml_dtypes.bfloat16)
    low = (table - high.astype(np.float64)).astype(ml_dtypes.bfloat16)
    return high, low


def dft_tables(length):
    half = length // 2
    points = np.arange(half)
    angles = (points[:, None] * points[None, :] % half) * (-2.0 * math.pi / half)
    real = np.cos(angles) / math.sqrt(length)
    imag = np.sin(angles) / math.sqrt(length)
    left_high, left_low = split_table(np.block([[real, -imag], [imag, real]]))
    right_high, right_low = split_table(np.block([[real, imag], [-imag, real]]))
    turn = points * (-2.0 * math.pi / length)
    twiddle = np.stack([np.cos(turn), np.sin(turn)]).astype(np.float32)
    return (
        np.concatenate([left_high, left_high, left_low], axis=1),
        np.concatenate([right_high, right_high, right_low], axis=0),
        np.repeat(twiddle[:, :, None], LANES, axis=2),
        np.repeat(twiddle[:, None, :], half, axis=1),
    )


def split_value(value):
    high = value.astype(jnp.bfloat16)
    low = (value - high.astype(jnp.float32)).astype(jnp.bfloat16)
    return high, low


def times(real, imag, twiddle):
    cosine, sine = twiddle
    return real * cosine - imag * sine, real * sine + imag * cosine


def left_product(blocks, table):
    half = blocks[0][0].shape[0]
    width = blocks[0][0].shape[1]
    value = jnp.concatenate(
        [jnp.concatenate([real, imag], axis=0) for real, imag in blocks], axis=1
    )
    high, low = split_value(value)
    out = jnp.dot(
        table[...],
        jnp.concatenate([high, low, high], axis=0),
        preferred_element_type=jnp.float32,
    )
    return [
        (out[:half, index * width : (index + 1) * width], out[half:, index * width : (index + 1) * width])
        for index in range(len(blocks))
    ]


def right_product(blocks, table):
    half = blocks[0][0].shape[1]
    value = jnp.concatenate(
        [jnp.concatenate([real, imag], axis=1) for real, imag in blocks], axis=0
    )
    high, low = split_value(value)
    out = jnp.dot(
        jnp.concatenate([high, low, high], axis=1),
        table[...],
        preferred_element_type=jnp.float32,
    )
    return [
        (out[index * half : (index + 1) * half, :half], out[index * half : (index + 1) * half, half:])
        for index in range(len(blocks))
    ]


def forward(real, imag, left_table, right_table, row_twiddle, lane_twiddle):
    half = real.shape[0] // 2
    wide_twiddle = [jnp.concatenate([part, part], axis=1) for part in row_twiddle]
    total = (real[:half] + real[half:], imag[:half] + imag[half:])
    gap = times(real[:half] - real[half:], imag[:half] - imag[half:], wide_twiddle)
    blocks = []
    for real, imag in left_product([total, gap], left_table):
        blocks.append((real[:, :half] + real[:, half:], imag[:, :half] + imag[:, half:]))
        blocks.append(
            times(real[:, :half] - real[:, half:], imag[:, :half] - imag[:, half:], lane_twiddle)
        )
    return right_product(blocks, right_table)


def backward(blocks, left_table, right_table, row_twiddle, lane_twiddle):
    blocks = right_product(blocks, right_table)
    wide_twiddle = [jnp.concatenate([part, part], axis=1) for part in row_twiddle]
    joined = []
    for parity in range(2):
        even_real, even_imag = blocks[2 * parity]
        odd_real, odd_imag = times(*blocks[2 * parity + 1], lane_twiddle)
        joined.append(
            (
                jnp.concatenate([even_real + odd_real, even_real - odd_real], axis=1),
                jnp.concatenate([even_imag + odd_imag, even_imag - odd_imag], axis=1),
            )
        )
    (even_real, even_imag), odd = left_product(joined, left_table)
    odd_real, odd_imag = times(*odd, wide_twiddle)
    return (
        jnp.concatenate([even_real + odd_real, even_real - odd_real], axis=0),
        jnp.concatenate([even_imag + odd_imag, even_imag - odd_imag], axis=0),
    )


def amplitude_kernel(amplitude, table, out, sorted_lanes):
    slots, size, _ = amplitude.shape
    half = size // 2
    for slot in range(slots):
        value = amplitude[slot]
        high = value.astype(jnp.bfloat16)
        rest = value - high.astype(jnp.float32)
        middle, low = split_value(rest)
        ordered = jnp.dot(
            jnp.concatenate([high, middle, low], axis=1),
            table[...],
            preferred_element_type=jnp.float32,
        )
        for index in range(2):
            sorted_lanes[slot, index] = ordered[:, index * half : (index + 1) * half]
            for parity in range(2):
                out[slot, 2 * parity + index] = sorted_lanes[slot, index, pl.ds(parity, half, stride=2), :]


def ordered_amplitude(amplitude):
    slots, size, _ = amplitude.shape
    half = size // 2
    table = np.zeros((size, size), np.float32)
    table[2 * np.arange(half), np.arange(half)] = 1
    table[2 * np.arange(half) + 1, half + np.arange(half)] = 1
    table = np.concatenate([table] * 3, axis=0).astype(ml_dtypes.bfloat16)
    vmem = pl.BlockSpec(memory_space=pltpu.VMEM)
    return pl.pallas_call(
        amplitude_kernel,
        out_shape=pltpu.VMEM((slots, 4, half, half), jnp.float32),
        in_specs=[vmem, vmem],
        out_specs=vmem,
        scratch_shapes=[pltpu.VMEM((slots, 2, size, half), jnp.float32)],
        compiler_params=pltpu.CompilerParams(vmem_limit_bytes=VMEM_LIMIT),
        cost_estimate=pl.CostEstimate(
            flops=2 * slots * size**3 * 3, bytes_accessed=8 * slots * size**2, transcendentals=0
        ),
        name="ordered_amplitude",
    )(amplitude, jnp.asarray(table))


def patch_kernel(
    counts,
    rows,
    cols,
    core,
    centre,
    top,
    bottom,
    near_mid,
    far_mid,
    near_corner,
    far_top,
    far_bottom,
    probe,
    amplitude,
    left_table,
    right_table,
    row_table,
    lane_table,
    inner_out,
    up_out,
    down_out,
    near_mid_out,
    far_mid_out,
    given_out,
    far_top_out,
    far_bottom_out,
    probe_out,
    extended,
    gradient,
    probe_sum,
    sems,
):
    size = probe.shape[1]
    margin = size // 2
    height, width = centre.shape[1:]
    inner = pl.ds(margin, width)
    near = pl.ds(pl.multiple_of((1 - core[0]) * (margin + width), LANES), margin)
    far = pl.ds(pl.multiple_of(core[0] * (margin + width), LANES), margin)
    head, middle, tail = pl.ds(0, margin), pl.ds(margin, height), pl.ds(margin + height, margin)
    moves = [
        (centre, extended.at[:, middle, inner]),
        (near_mid, extended.at[:, middle, near]),
        (far_mid, extended.at[:, middle, far]),
        (top, extended.at[:, head, inner]),
        (bottom, extended.at[:, tail, inner]),
        (far_top, extended.at[:, head, far]),
        (far_bottom, extended.at[:, tail, far]),
        (near_corner.at[:, head, :], extended.at[:, head, near]),
        (near_corner.at[:, pl.ds(margin, margin), :], extended.at[:, tail, near]),
    ]
    copies = [
        pltpu.make_async_copy(source, target, sems.at[index])
        for index, (source, target) in enumerate(moves)
    ]
    for copy in copies:
        copy.start()
    gradient[...] = jnp.zeros_like(gradient)
    probe_sum[...] = jnp.zeros_like(probe_sum)
    for copy in copies:
        copy.wait()
    tile = (1, TILE, LANES)
    lane = lax.broadcasted_iota(jnp.int32, tile, 2)
    sublane = lax.broadcasted_iota(jnp.int32, tile, 1)
    tiles = size // TILE
    pieces = size // LANES

    tables = (
        left_table,
        right_table,
        (row_table[0], row_table[1]),
        (lane_table[0], lane_table[1]),
    )

    def place(slot):
        row_shift = lax.rem(rows[slot], TILE)
        col_shift = lax.rem(cols[slot], LANES)
        row = pl.multiple_of(rows[slot] - row_shift, TILE)
        col = pl.multiple_of(cols[slot] - col_shift, LANES)
        areas = [
            (pl.ds(row, size + TILE), pl.ds(col + LANES * piece, LANES))
            for piece in range(pieces + 1)
        ]
        return row_shift, col_shift, areas

    def window(part, row_shift, col_shift, areas):
        columns = [
            pltpu.roll(
                extended[(part,) + area].reshape(tiles + 1, TILE, LANES),
                lax.rem(LANES - col_shift, LANES),
                2,
            )
            for area in areas
        ]
        result = []
        for piece in range(pieces):
            value = jnp.where(lane < LANES - col_shift, columns[piece], columns[piece + 1])
            value = pltpu.roll(value, lax.rem(TILE - row_shift, TILE), 1)
            value = jnp.where(sublane < TILE - row_shift, value[:tiles], value[1:])
            result.append(value.reshape(size, LANES))
        return jnp.concatenate(result, axis=1)

    def add_term(part, term, row_shift, col_shift, areas):
        columns = []
        ended = jnp.zeros(tile, jnp.float32)
        for piece in range(pieces):
            value = term[:, LANES * piece : LANES * (piece + 1)].reshape(tiles, TILE, LANES)
            value = pltpu.roll(value, row_shift, 1)
            value = jnp.where(
                sublane >= row_shift,
                jnp.concatenate([value, ended], axis=0),
                jnp.concatenate([ended, value], axis=0),
            )
            columns.append(pltpu.roll(value, col_shift, 2))
        ended = jnp.zeros_like(columns[0])
        columns = [ended] + columns + [ended]
        for piece, area in enumerate(areas):
            block = jnp.where(lane >= col_shift, columns[piece + 1], columns[piece])
            gradient[(part,) + area] += block.reshape(size + TILE, LANES)

    def some_patches(slots):
        places = [place(slot) for slot in slots]
        windows = [[window(part, *where) for part in range(2)] for where in places]
        probe_real = probe[0]
        probe_imag = probe[1]
        far_fields = [
            forward(
                probe_real * real - probe_imag * imag, probe_real * imag + probe_imag * real, *tables
            )
            for real, imag in windows
        ]
        residuals = []
        for slot, far_field in zip(slots, far_fields):
            residual = []
            for index, (real, imag) in enumerate(far_field):
                power = real * real + imag * imag
                remain = 1.0 - amplitude[slot, index] * lax.rsqrt(
                    jnp.maximum(power, FLOOR * FLOOR)
                )
                residual.append((real * remain, -imag * remain))
            residuals.append(residual)
        backs = [backward(residual, *tables) for residual in residuals]
        probe_terms = [0.0, 0.0]
        for where, (window_real, window_imag), (back_real, back_imag) in zip(places, windows, backs):
            back_imag = -back_imag
            probe_terms[0] += window_real * back_real + window_imag * back_imag
            probe_terms[1] += window_real * back_imag - window_imag * back_real
            add_term(0, probe_real * back_real + probe_imag * back_imag, *where)
            add_term(1, probe_real * back_imag - probe_imag * back_real, *where)
        for part, term in enumerate(probe_terms):
            for piece in range(pieces):
                probe_sum[part, piece] += term[:, LANES * piece : LANES * (piece + 1)]

    def two_patches(index, carry):
        some_patches([2 * index, 2 * index + 1])
        return carry

    count = counts[0]
    lax.fori_loop(0, count // 2, two_patches, 0)

    @pl.when(count % 2 == 1)
    def _():
        some_patches([count - 1])

    given_out[:, :margin] = gradient[:, head, near]
    given_out[:, margin : 2 * margin] = gradient[:, tail, near]
    for part in range(2):
        given_out[part, 2 * margin :] = probe_sum[part, 1 - core[0]]
        probe_out[part] = probe_sum[part, core[0]]
    inner_out[...] = gradient[:, middle, inner]
    up_out[...] = gradient[:, head, inner]
    down_out[...] = gradient[:, tail, inner]
    near_mid_out[...] = gradient[:, middle, near]
    far_mid_out[...] = gradient[:, middle, far]
    far_top_out[...] = gradient[:, head, far]
    far_bottom_out[...] = gradient[:, tail, far]


def patches(counts, rows, cols, core, pieces, probe, amplitude):
    size = probe.shape[1]
    margin = size // 2
    height, width = pieces[0].shape[1:]
    tall, wide = height + size, width + size
    smem = pl.BlockSpec(memory_space=pltpu.SMEM)
    vmem = pl.BlockSpec(memory_space=pltpu.VMEM)
    anywhere = pl.BlockSpec(memory_space=pl.ANY)
    shapes = [
        (height, width),
        (margin, width),
        (margin, width),
        (height, margin),
        (height, margin),
        (2 * margin + size, margin),
        (margin, margin),
        (margin, margin),
        (size, LANES),
    ]
    return pl.pallas_call(
        patch_kernel,
        out_shape=tuple(pltpu.VMEM((2,) + shape, jnp.float32) for shape in shapes),
        in_specs=[smem] * 4 + [anywhere] * 8 + [vmem] * 6,
        out_specs=[vmem] * 9,
        scratch_shapes=[
            pltpu.VMEM((2, tall, wide), jnp.float32),
            pltpu.VMEM((2, tall, wide), jnp.float32),
            pltpu.VMEM((2, size // LANES, size, LANES), jnp.float32),
            pltpu.SemaphoreType.DMA((9,)),
        ],
        compiler_params=pltpu.CompilerParams(vmem_limit_bytes=VMEM_LIMIT),
        name="patches",
    )(
        counts,
        rows,
        cols,
        core,
        *pieces,
        probe,
        amplitude,
        *(jnp.asarray(table) for table in dft_tables(size)),
    )


def haar_kernel(
    core,
    centre,
    inner,
    above,
    below,
    near_top,
    near_bottom,
    far_mid,
    far_top,
    far_bottom,
    out,
    *scratch,
):
    height, width = centre.shape[1:]
    margin = above.shape[1]
    levels = [scratch[level] for level in range(LEVELS)]
    details = [scratch[LEVELS + level] for level in range(LEVELS - 1)]
    columns = width // LANES
    work = levels[0]
    near = (1 - core[0]) * (columns - 1)
    far = core[0] * (columns - 1)
    for part in range(2):
        for column in range(columns):
            piece = part, slice(None), pl.ds(column * LANES, LANES)
            gathered = jnp.concatenate([above[piece], below[piece]], axis=0) + inner[piece]
            work[part, column] = centre[piece] - STEP_OBJECT * gathered
        sides = jnp.concatenate([near_top[part], near_bottom[part]], axis=0)
        work[part, near] -= STEP_OBJECT * sides
        corners = jnp.concatenate([far_top[part], far_bottom[part]], axis=0)
        work[part, far] -= STEP_OBJECT * (far_mid[part] + corners)

    lane = lax.broadcasted_iota(jnp.int32, (TILE, LANES), 1)

    def each(function, *parts):
        return [[function(*pair) for pair in zip(*rows)] for rows in zip(*parts)]

    def level_steps(level):
        stride = 1 << level
        active = lane % stride == 0
        second = lane % (2 * stride) == stride
        keep = jnp.where(active, jnp.where(second, -0.5, 0.5), 1.0).astype(jnp.float32)
        swap = jnp.where(active, 0.5, 0.0).astype(jnp.float32)

        def lane_step(values):
            after = each(lambda value: pltpu.roll(value, LANES - stride, 1), values)
            before = each(lambda value: pltpu.roll(value, stride, 1), values)
            return each(
                lambda value, high, low: value * keep + jnp.where(second, low, high) * swap,
                values,
                after,
                before,
            )

        def row_step(first, other):
            if level == 0:
                return each(jnp.add, first, other), each(jnp.subtract, first, other)
            return (
                each(lambda a, b: jnp.where(active, a + b, a), first, other),
                each(lambda a, b: jnp.where(active, a - b, b), first, other),
            )

        return lane_step, row_step

    def shrink(values, kept=None):
        factors = []
        for real, imag in zip(*values):
            power = real * real + imag * imag
            factor = jnp.maximum(
                1.0 - THRESHOLD * lax.rsqrt(jnp.maximum(power, THRESHOLD * THRESHOLD)), 0.0
            )
            factors.append(factor if kept is None else jnp.where(kept, 1.0, factor))
        return [[value * factor for value, factor in zip(row, factors)] for row in values]

    def load(ref, start, stride=None):
        where = pl.ds(start, TILE) if stride is None else pl.ds(start, TILE, stride=stride)
        return [[ref[part, column, where, :] for column in range(columns)] for part in range(2)]

    def save(ref, values, start, stride=None):
        where = pl.ds(start, TILE) if stride is None else pl.ds(start, TILE, stride=stride)
        for part in range(2):
            for column in range(columns):
                ref[part, column, where, :] = values[part][column]

    for level in range(LEVELS - 1):
        lane_step, row_step = level_steps(level)

        for index in range(height >> (level + 4)):
            base = index * 2 * TILE
            first = load(levels[level], base, 2)
            other = load(levels[level], base + 1, 2)
            low, high = row_step(first, other)
            save(levels[level + 1], lane_step(low), index * TILE)
            save(details[level], shrink(lane_step(high)), index * TILE)

    lane_step, row_step = level_steps(LEVELS - 1)
    coarsest = lane % (1 << LEVELS) == 0
    for index in range(height >> (LEVELS + 3)):
        base = index * 2 * TILE
        low, high = row_step(load(levels[-1], base, 2), load(levels[-1], base + 1, 2))
        low = lane_step(shrink(lane_step(low), coarsest))
        high = lane_step(shrink(lane_step(high)))
        first, other = row_step(low, high)
        save(levels[-1], first, base, 2)
        save(levels[-1], other, base + 1, 2)

    for level in range(LEVELS - 1)[::-1]:
        lane_step, row_step = level_steps(level)
        for index in range(height >> (level + 4)):
            low = lane_step(load(levels[level + 1], index * TILE))
            high = lane_step(load(details[level], index * TILE))
            first, other = row_step(low, high)
            base = index * 2 * TILE
            save(levels[level], first, base, 2)
            save(levels[level], other, base + 1, 2)
    for part in range(2):
        for column in range(columns):
            out[part, :, pl.ds(column * LANES, LANES)] = work[part, column]


def shrink_object(core, *pieces):
    smem = pl.BlockSpec(memory_space=pltpu.SMEM)
    vmem = pl.BlockSpec(memory_space=pltpu.VMEM)
    shape = pieces[0].shape
    sizes = [(2, shape[2] // LANES, shape[1] >> level, LANES) for level in range(LEVELS)]
    return pl.pallas_call(
        haar_kernel,
        out_shape=jax.ShapeDtypeStruct(shape, jnp.float32),
        in_specs=[smem] + [vmem] * len(pieces),
        out_specs=vmem,
        scratch_shapes=[pltpu.VMEM(size, jnp.float32) for size in sizes + sizes[1:]],
        compiler_params=pltpu.CompilerParams(vmem_limit_bytes=VMEM_LIMIT),
        name="haar",
    )(core, *pieces)


def permuted(value, move):
    rows, cols = lax.axis_size("row"), lax.axis_size(AXES[1:])
    pairs = []
    for source in range(rows * cols):
        row, col = move(source // cols, source % cols)
        if 0 <= row < rows and 0 <= col < cols:
            pairs.append((source, row * cols + col))
    return lax.ppermute(value, AXES, pairs)


def up_by(step):
    return lambda row, col: (row + step, col)


def near_to(row, col):
    return row, col ^ 1


def far_to(step):
    return lambda row, col: (row + step, col - 1 if col % 2 == 0 else col + 1)


def chip_tiles(half):
    return half.reshape(lax.axis_size(CHIPS), -1, LANES)


def handed_out(tile):
    tiles = jnp.broadcast_to(tile[None], (lax.axis_size(CHIPS),) + tile.shape)
    return lax.all_to_all(tiles, CHIPS, 0, 0, tiled=True)


def on_device(object_now, object_prev, probe, amplitudes, pos_row, pos_col, counts):
    centre = object_now + MOMENTUM * (object_now - object_prev)
    margin = probe.shape[1] // 2
    height, width = centre.shape[1:]
    slots = amplitudes.shape[2]
    core = lax.axis_index("core")
    core_word = core.reshape(1)
    devices = lax.axis_size(AXES)

    def sides(value):
        first, last = value[:, :, :margin], value[:, :, width - margin :]
        return jnp.where(core == 0, last, first), jnp.where(core == 0, first, last)

    near, far = sides(centre)
    top = permuted(centre[:, height - margin :], up_by(1))
    bottom = permuted(centre[:, :margin], up_by(-1))
    far_top = permuted(far[:, height - margin :], far_to(1))
    far_bottom = permuted(far[:, :margin], far_to(-1))
    far_mid = permuted(far, far_to(0))
    near_mid = permuted(near, near_to)
    near_corner, far_top, far_bottom, far_mid = lax.optimization_barrier(
        (
            jnp.concatenate([sides(top)[0], sides(bottom)[0]], axis=1),
            far_top,
            far_bottom,
            far_mid,
        )
    )
    near_corner = permuted(near_corner, near_to)
    (
        inner,
        up,
        down,
        near_mid,
        far_mid,
        given,
        far_top,
        far_bottom,
        probe_kept,
    ) = patches(
        counts.reshape(1),
        pos_row.reshape(slots),
        pos_col.reshape(slots),
        core_word,
        (centre, top, bottom, near_mid, far_mid, near_corner, far_top, far_bottom),
        probe,
        ordered_amplitude(amplitudes[0, 0]),
    )
    given = permuted(given, near_to)
    corner = given[:, : 2 * margin]
    shares = chip_tiles(probe_kept + given[:, 2 * margin :])

    def with_corner(strip, piece):
        none = jnp.zeros_like(piece)
        first = jnp.where(core == 0, none, piece)
        last = jnp.where(core == 0, piece, none)
        gap = jnp.zeros(piece.shape[:2] + (width - 2 * margin,), piece.dtype)
        return strip + jnp.concatenate([first, gap, last], axis=2)

    up = with_corner(up, corner[:, :margin])
    down = with_corner(down, corner[:, margin:])
    up, down, far_top, far_bottom, far_mid, near_mid, shares = lax.optimization_barrier(
        (up, down, far_top, far_bottom, far_mid, near_mid, shares)
    )
    shares = lax.all_to_all(shares, CHIPS, 0, 0, tiled=True)
    below = permuted(up, up_by(-1))
    above = permuted(down, up_by(1))
    far_below = permuted(far_top, far_to(-1))
    far_above = permuted(far_bottom, far_to(1))
    far_mid = permuted(far_mid, far_to(0))
    near_mid, above, below, far_below, far_above, far_mid = lax.optimization_barrier(
        (near_mid, above, below, far_below, far_above, far_mid)
    )
    near_top = permuted(near_mid[:, :margin], near_to)
    near_top, near_bottom = lax.optimization_barrier((near_top, near_mid[:, margin:]))
    near_bottom = permuted(near_bottom, near_to)
    columns = [probe[:, :, LANES * index : LANES * (index + 1)] for index in range(2)]
    tile = lax.dynamic_index_in_dim(
        chip_tiles(jnp.where(core == 0, *columns)), lax.axis_index(CHIPS), keepdims=False
    )
    tile = tile - PROBE_STEP / (slots * devices) * jnp.sum(shares, axis=0)
    mine = handed_out(tile).reshape(columns[0].shape)
    other = permuted(mine, near_to)
    probe_new = jnp.concatenate(
        [jnp.where(core == 0, mine, other), jnp.where(core == 0, other, mine)], axis=2
    )
    object_new = shrink_object(core_word, centre, inner, above, below, near_top, near_bottom, far_mid, far_above, far_below)
    return object_new, probe_new


def solution(mesh):
    fine = jax.sharding.Mesh(mesh.devices.reshape(mesh.devices.shape[0], -1, 2), AXES)
    col = AXES[1:]
    in_specs = (
        P(None, "row", col),
        P(None, "row", col),
        P(),
        P("row", col, None, None, None),
        P("row", col, None),
        P("row", col, None),
        P("row", col),
    )
    out_specs = (P(None, "row", col), P())
    return jax.shard_map(
        on_device, mesh=fine, in_specs=in_specs, out_specs=out_specs, check_vma=False
    )
```

time: 847 us -> 115 us (0.14); the launches traced: 833 us -> 114 us
  local copies, waits for them, and re-layouts: 481 us -> 1.69 us
  waiting for transfers between devices: 205 us -> 27.2 us
  matrix products: 55.7 us -> 0 us
  starting transfers between devices: 33 us -> 65.8 us
  other arithmetic: 27.4 us -> 8.15 us
  loops' own time: 15.6 us -> 0 us
  between operations: 15.6 us -> 1.61 us
  Pallas kernels: 0 us -> 9.27 us
    psum x1 -> x0, waiting for transfers between devices: 145 us -> none  [on_device(): probe_total = lax.psum(probe_sum, ('row', 'col'))]
    reshape x5 -> x0, local copies, waits for them, and re-layouts: 133 us -> none  [the longest x1 68.5 us: haar_shrink(): blocks = field.reshape(2, height, 2, breadth, 2)]
    slice x7 -> x3, local copies, waits for them, and re-layouts: 120 us -> 0.11 us  [the longest x1 0.07 us: on_device(): bottom = permuted(centre[:, :margin], up_by(-1))]
    unnamed x53 -> x22, local copies, waits for them, and re-layouts: 110 us -> 0.83 us
    dot_general x16 -> x0, matrix products: 55.7 us -> none  [the longest x8 32.9 us: left_product(): jnp.einsum('jk,bkl->bjl', table, values, precision=lax.Precision.HIGHEST)]
    another operation x5 -> x1, local copies, waits for them, and re-layouts: 44.6 us -> 0.01 us  [the longest x4 44.6 us: haar_shrink(): jnp.stack([upper_pair, lower_pair], axis=2)]
    ppermute x8 -> x16, waiting for transfers between devices: 60.1 us -> 22.2 us  [permuted(): return lax.ppermute(value, AXES, pairs)]
    dynamic_update_slice x4 -> x0, local copies, waits for them, and re-layouts: 25.9 us -> none  [add_patch(): lax.dynamic_update_slice(running, current + terms[slot_index], corner)]
  transfers between devices with their start and end apart: 9 -> 18, of which waited for: 7 -> 7; matrix products, arithmetic and copies ran while one was open for 0% -> 5% of each run, Pallas kernels for 0% -> 1%
where the time goes in v1:
time: 115 us; the launch traced here: 114 us
  starting transfers between devices  65.8 us (57%)
  waiting for transfers between devices  27.2 us (24%)
  Pallas kernels  9.27 us (8%)
  other arithmetic  8.15 us (7%)
  local copies, waits for them, and re-layouts  1.69 us (1%)
  between operations  1.61 us (1%)
    ppermute x16, starting transfers between devices, permuted(): return lax.ppermute(value, AXES, pairs)  40.6 us
    ppermute x16, waiting for transfers between devices, permuted(): return lax.ppermute(value, AXES, pairs)  22.2 us
    all_to_all x1, starting transfers between devices, on_device(): shares = lax.all_to_all(shares, CHIPS, 0, 0, tiled=True)  13.2 us
    all_to_all x1, starting transfers between devices, handed_out(): return lax.all_to_all(tiles, CHIPS, 0, 0, tiled=True)  12 us
    all_to_all x1, waiting for transfers between devices, handed_out(): return lax.all_to_all(tiles, CHIPS, 0, 0, tiled=True)  4.97 us
    pallas_call x1, Pallas kernels, patches(): pl.pallas_call(patch_kernel, out_shape=tuple((pltpu.VMEM((2,) + shape, jn...  4.7 us
    pallas_call x1, Pallas kernels, shrink_object(): pl.pallas_call(haar_kernel, out_shape=jax.ShapeDtypeStruct(shape, jnp.flo...  3.88 us
  transfers between devices with their start and end apart: 18, of which 7 were waited for; matrix products, arithmetic and copies ran while one was open for 5% of the time, Pallas kernels for 1%

profile of v1, /device:TPU:1, one launch (start us, length us, event | category | flops | bytes accessed | tf_op | source)
XLA Modules:
  0.0 113.7 jit_solution(6293783492273454442)
XLA Ops:
  0.6 1.8 %multiply_add_fusion.centre = f32[2,256,512]{2,1,0:T(8,128)S(1)} fusion(f32[2,256,512]{2,1,0:T(8,128)} %param.12, f32[2,256,512]{2,1,0:T(8,128)} %param.13), kind=kLoop, calls=%fused_computation | loop fusion | flops 786432 | bytes 3145728 | tf_op jit(solution)/shard_map/add | solution.py:562
  2.4 0.1 fusion.1
  2.5 1.3 %collective-permute-start.1 = (f32[2,128,512]{2,1,0:T(8,128)S(1)}, f32[2,128,512]{2,1,0:T(8,128)S(1)}, u32[]{:S(2)}, u32[]{:S(2)}) collective-permute-start(f32[2,128,512]{2,1,0:T(8,128)S(1)} %get-tuple-element.60), channel_id=1, source_target_pairs={{16,0},{17,1},{18,2},{19,3},{20,4},{21,5},{22,6},{23,7},{24,8},{25... | collective-permute-start | bytes 1572872 | tf_op jit(solution)/shard_map/ppermute | solution.py:537
  3.8 6.1 %collective-permute-start = (f32[2,128,512]{2,1,0:T(8,128)S(1)}, f32[2,128,512]{2,1,0:T(8,128)S(1)}, u32[]{:S(2)}, u32[]{:S(2)}) collective-permute-start(f32[2,128,512]{2,1,0:T(8,128)S(1)} %get-tuple-element.61), channel_id=1, source_target_pairs={{0,16},{1,17},{2,18},{3,19},{4,20},{5,21},{6,22},{7,23},{8,24},{9,... | collective-permute-start | bytes 1572872 | tf_op jit(solution)/shard_map/ppermute | solution.py:537
  10.0 0.0 copy-start.3
  10.0 4.6 %collective-permute-start.5 = (f32[2,256,128]{2,1,0:T(8,128)S(1)}, f32[2,256,128]{2,1,0:T(8,128)S(1)}, u32[]{:S(2)}, u32[]{:S(2)}) collective-permute-start(f32[2,256,128]{2,1,0:T(8,128)S(1)} %get-tuple-element.58), channel_id=1, source_target_pairs={{1,2},{2,1},{3,4},{4,3},{5,6},{6,5},{7,8},{8,7},{9,10},{10,9},{11,... | collective-permute-start | bytes 786440 | tf_op jit(solution)/shard_map/ppermute | solution.py:537
  14.7 4.1 %collective-permute-start.3 = (f32[2,128,128]{2,1,0:T(8,128)S(1)}, f32[2,128,128]{2,1,0:T(8,128)S(1)}, u32[]{:S(2)}, u32[]{:S(2)}) collective-permute-start(f32[2,128,128]{2,1,0:T(8,128)S(1)} %get-tuple-element.71), channel_id=1, source_target_pairs={{1,18},{2,17},{3,20},{4,19},{5,22},{6,21},{7,24},{8,23},{9,26},{10... | collective-permute-start | bytes 393224 | tf_op jit(solution)/shard_map/ppermute | solution.py:537
  18.7 1.3 %collective-permute-start.4 = (f32[2,128,128]{2,1,0:T(8,128)S(1)}, f32[2,128,128]{2,1,0:T(8,128)S(1)}, u32[]{:S(2)}, u32[]{:S(2)}) collective-permute-start(f32[2,128,128]{2,1,0:T(8,128)S(1)} %get-tuple-element.70), channel_id=1, source_target_pairs={{17,2},{18,1},{19,4},{20,3},{21,6},{22,5},{23,8},{24,7},{25,10},{2... | collective-permute-start | bytes 393224 | tf_op jit(solution)/shard_map/ppermute | solution.py:537
  20.0 0.0 collective-permute-done.1.bottom
  20.0 2.1 %collective-permute-start.2 = (f32[2,256,128]{2,1,0:T(8,128)S(1)}, f32[2,256,128]{2,1,0:T(8,128)S(1)}, u32[]{:S(2)}, u32[]{:S(2)}) collective-permute-start(f32[2,256,128]{2,1,0:T(8,128)S(1)} %get-tuple-element.59), channel_id=1, source_target_pairs={{0,1},{1,0},{2,3},{3,2},{4,5},{5,4},{6,7},{7,6},{8,9},{9,8},{10,11... | collective-permute-start | bytes 786440 | tf_op jit(solution)/shard_map/ppermute | solution.py:537
  22.2 0.0 copy-start.4
  22.2 0.0 collective-permute-done.top
  22.3 1.7 %collective-permute-done.3.far_top = f32[2,128,128]{2,1,0:T(8,128)S(1)} collective-permute-done((f32[2,128,128]{2,1,0:T(8,128)S(1)}, f32[2,128,128]{2,1,0:T(8,128)S(1)}, u32[]{:S(2)}, u32[]{:S(2)}) %collective-permute-start.3) | collective-permute-done | bytes 131104 | tf_op jit(solution)/shard_map/ppermute | solution.py:537
  24.0 13.1 %collective-permute-done.4.far_bottom = f32[2,128,128]{2,1,0:T(8,128)S(1)} collective-permute-done((f32[2,128,128]{2,1,0:T(8,128)S(1)}, f32[2,128,128]{2,1,0:T(8,128)S(1)}, u32[]{:S(2)}, u32[]{:S(2)}) %collective-permute-start.4) | collective-permute-done | bytes 131104 | tf_op jit(solution)/shard_map/ppermute | solution.py:537
  37.0 0.0 collective-permute-done.5.far_mid
  37.0 0.0 collective-permute-start.6
  37.7 0.0 copy-start
  37.7 0.0 copy-start.5
  37.7 0.0 copy-start.6
  37.8 0.0 copy-start.7
  37.8 0.0 copy-start.8
  37.8 0.7 ordered_amplitude.1.amplitude
  38.5 0.0 collective-permute-done.2.near_mid
  38.5 0.1 collective-permute-done.6.near_corner
  38.6 0.2 copy-done
  38.8 0.1 copy-done.5
  38.9 0.1 copy-done.6
  39.0 0.0 copy-done.7
  39.0 0.0 copy-done.8
  39.1 0.3 copy-done.9
  39.4 0.0 copy-done.10
  39.4 4.7 %patches.1 = (f32[2,256,512]{2,1,0:T(8,128)S(1)}, f32[2,128,512]{2,1,0:T(8,128)S(1)}, f32[2,128,512]{2,1,0:T(8,128)S(1)}, f32[2,256,128]{2,1,0:T(8,128)S(1)}, f3...) custom-call(s32[1]{0:T(128)} %bitcast.17.counts, ...), custom_call_target="tpu_custom_call" | custom-call | tf_op jit(solution)/shard_map/patches/pallas_call | solution.py:369
  44.1 0.0 copy-start.1
  44.1 2.7 %collective-permute-start.7 = (f32[2,512,128]{2,1,0:T(8,128)S(1)}, f32[2,512,128]{2,1,0:T(8,128)S(1)}, u32[]{:S(2)}, u32[]{:S(2)}) collective-permute-start(f32[2,512,128]{2,1,0:T(8,128)S(1)} %get-tuple-element.36), channel_id=1, source_target_pairs={{0,1},{1,0},{2,3},{3,2},{4,5},{5,4},{6,7},{7,6},{8,9},{9,8},{10,11... | collective-permute-start | bytes 1572872 | tf_op jit(solution)/shard_map/ppermute | solution.py:537
  46.8 1.5 %collective-permute-done.7 = f32[2,512,128]{2,1,0:T(8,128)S(1)} collective-permute-done((f32[2,512,128]{2,1,0:T(8,128)S(1)}, f32[2,512,128]{2,1,0:T(8,128)S(1)}, u32[]{:S(2)}, u32[]{:S(2)}) %collective-permute-start.7) | collective-permute-done | bytes 524320 | tf_op jit(solution)/shard_map/ppermute | solution.py:537
  48.4 1.1 maximum_add_fusion.1
  49.5 0.7 slice_add_fusion
  50.3 13.2 %all-to-all-start = ((f32[64,8,128]{2,1,0:T(8,128)}), f32[64,8,128]{2,1,0:T(8,128)}, u32[]{:S(2)}, u32[]{:S(2)}) async-start(f32[64,8,128]{2,1,0:T(8,128)} %bitcast.5), calls=%async_computation | async-start | bytes 524288 | tf_op jit(solution)/shard_map/all_to_all | solution.py:625
  63.5 4.4 %collective-permute-start.8 = (f32[2,128,512]{2,1,0:T(8,128)}, f32[2,128,512]{2,1,0:T(8,128)S(1)}, u32[]{:S(2)}, u32[]{:S(2)}) collective-permute-start(f32[2,128,512]{2,1,0:T(8,128)} %get-tuple-element.44), channel_id=1, source_target_pairs={{0,16},{1,17},{2,18},{3,19},{4,20},{5,21},{6,22},{7,23},{8,24},{9,... | collective-permute-start | bytes 1572872 | tf_op jit(solution)/shard_map/ppermute | solution.py:537
  67.9 1.3 %collective-permute-start.9 = (f32[2,128,512]{2,1,0:T(8,128)}, f32[2,128,512]{2,1,0:T(8,128)S(1)}, u32[]{:S(2)}, u32[]{:S(2)}) collective-permute-start(f32[2,128,512]{2,1,0:T(8,128)} %get-tuple-element.45), channel_id=1, source_target_pairs={{16,0},{17,1},{18,2},{19,3},{20,4},{21,5},{22,6},{23,7},{24,8},{25... | collective-permute-start | bytes 1572872 | tf_op jit(solution)/shard_map/ppermute | solution.py:537
  69.2 0.7 slice_select_fusion
  69.9 3.3 %collective-permute-start.12 = (f32[2,256,128]{2,1,0:T(8,128)S(1)}, f32[2,256,128]{2,1,0:T(8,128)S(1)}, u32[]{:S(2)}, u32[]{:S(2)}) collective-permute-start(f32[2,256,128]{2,1,0:T(8,128)S(1)} %get-tuple-element.48), channel_id=1, source_target_pairs={{1,2},{2,1},{3,4},{4,3},{5,6},{6,5},{7,8},{8,7},{9,10},{10,9},{11,... | collective-permute-start | bytes 786440 | tf_op jit(solution)/shard_map/ppermute | solution.py:537
  73.2 0.0 all-to-all-done
  73.2 1.0 reduce_sum.9
  74.2 0.7 fusion
  74.9 0.7 broadcast_in_dim.9
  75.6 12.0 %all-to-all-start.1 = ((f32[64,8,128]{2,1,0:T(8,128)}), f32[64,8,128]{2,1,0:T(8,128)}, u32[]{:S(2)}, u32[]{:S(2)}) async-start(f32[64,8,128]{2,1,0:T(8,128)} %broadcast_in_dim.9), calls=%async_computation.1 | async-start | bytes 524288 | tf_op jit(solution)/shard_map/all_to_all | solution.py:558
  87.6 1.3 %collective-permute-start.10 = (f32[2,128,128]{2,1,0:T(8,128)S(1)}, f32[2,128,128]{2,1,0:T(8,128)S(1)}, u32[]{:S(2)}, u32[]{:S(2)}) collective-permute-start(f32[2,128,128]{2,1,0:T(8,128)S(1)} %get-tuple-element.46), channel_id=1, source_target_pairs={{17,2},{18,1},{19,4},{20,3},{21,6},{22,5},{23,8},{24,7},{25,10},{2... | collective-permute-start | bytes 393224 | tf_op jit(solution)/shard_map/ppermute | solution.py:537
  88.9 5.5 %collective-permute-start.11 = (f32[2,128,128]{2,1,0:T(8,128)S(1)}, f32[2,128,128]{2,1,0:T(8,128)S(1)}, u32[]{:S(2)}, u32[]{:S(2)}) collective-permute-start(f32[2,128,128]{2,1,0:T(8,128)S(1)} %get-tuple-element.47), channel_id=1, source_target_pairs={{1,18},{2,17},{3,20},{4,19},{5,22},{6,21},{7,24},{8,23},{9,26},{10... | collective-permute-start | bytes 393224 | tf_op jit(solution)/shard_map/ppermute | solution.py:537
  94.4 4.5 %collective-permute-done.10.far_bottom = f32[2,128,128]{2,1,0:T(8,128)S(1)} collective-permute-done((f32[2,128,128]{2,1,0:T(8,128)S(1)}, f32[2,128,128]{2,1,0:T(8,128)S(1)}, u32[]{:S(2)}, u32[]{:S(2)}) %collective-permute-start.10) | collective-permute-done | bytes 131104 | tf_op jit(solution)/shard_map/ppermute | solution.py:537
  98.9 5.0 %all-to-all-done.1 = f32[64,8,128]{2,1,0:T(8,128)} async-done(((f32[64,8,128]{2,1,0:T(8,128)}), f32[64,8,128]{2,1,0:T(8,128)}, u32[]{:S(2)}, u32[]{:S(2)}) %all-to-all-start.1) | async-done | bytes 262176 | tf_op jit(solution)/shard_map/all_to_all | solution.py:558
  103.9 2.3 %collective-permute-start.15 = (f32[2,256,128]{2,1,0:T(8,128)}, f32[2,256,128]{2,1,0:T(8,128)S(1)}, u32[]{:S(2)}, u32[]{:S(2)}) collective-permute-start(f32[2,256,128]{2,1,0:T(8,128)} %bitcast.9), channel_id=1, source_target_pairs={{0,1},{1,0},{2,3},{3,2},{4,5},{5,4},{6,7},{7,6},{8,9},{9,8},{10,11... | collective-permute-start | bytes 786440 | tf_op jit(solution)/shard_map/ppermute | solution.py:537
  106.2 0.0 collective-permute-done.11.far_top
  106.2 0.0 collective-permute-done.12.far_mid
  106.2 0.0 collective-permute-done.8.above
  106.2 0.0 collective-permute-done.9.below
  106.2 0.1 collective-permute-start.13
  106.3 1.3 %collective-permute-done.13.near_top = f32[2,128,128]{2,1,0:T(8,128)S(1)} collective-permute-done((f32[2,128,128]{2,1,0:T(8,128)S(1)}, f32[2,128,128]{2,1,0:T(8,128)S(1)}, u32[]{:S(2)}, u32[]{:S(2)}) %collective-permute-start.13) | collective-permute-done | bytes 131104 | tf_op jit(solution)/shard_map/ppermute | solution.py:537
  107.7 0.2 collective-permute-start.14
  107.9 0.0 collective-permute-done.15
  107.9 1.1 broadcast_select_fusion.1
  109.0 0.8 pad_maximum_fusion
  109.8 0.0 collective-permute-done.14.near_bottom
  109.8 3.9 %haar.1 = f32[2,256,512]{2,1,0:T(8,128)} custom-call(s32[1]{0:T(128)} %bitcast.core, f32[2,256,512]{2,1,0:T(8,128)S(1)} %multiply_add_fusion.centre, f32[2,256,512]{2,1,0:T(8,128)S(1)} %copy-done.2, f32[2,128,512]{2,1,0:T(8,128)S(1)} %collective-permute-done.8.above, f32[2,128,512]{2,1,0:T(8,128)S(1)} %collective-permute-done.9.below, ...), custom_call_target="tpu_custom_call" | custom-call | tf_op jit(solution)/shard_map/haar/pallas_call | solution.py:519
  (16 shorter events, 0.2 us)
Async XLA Ops:
  2.5 17.5 %collective-permute-start.1 = (f32[2,128,512]{2,1,0:T(8,128)S(1)}, f32[2,128,512]{2,1,0:T(8,128)S(1)}, u32[]{:S(2)}, u32[]{:S(2)}) collective-permute-start(f32[2,128,512]{2,1,0:T(8,128)S(1)} %get-tuple-element.60), channel_id=1, source_target_pairs={{16,0},{17,1},{18,2},{19,3},{20,4},{21,5},{22,6},{23,7},{24,8},{25... | collective-permute-start | bytes 1572872 | tf_op jit(solution)/shard_map/ppermute | solution.py:537
  3.8 18.4 %collective-permute-start = (f32[2,128,512]{2,1,0:T(8,128)S(1)}, f32[2,128,512]{2,1,0:T(8,128)S(1)}, u32[]{:S(2)}, u32[]{:S(2)}) collective-permute-start(f32[2,128,512]{2,1,0:T(8,128)S(1)} %get-tuple-element.61), channel_id=1, source_target_pairs={{0,16},{1,17},{2,18},{3,19},{4,20},{5,21},{6,22},{7,23},{8,24},{9,... | collective-permute-start | bytes 1572872 | tf_op jit(solution)/shard_map/ppermute | solution.py:537
  10.0 27.7 %copy-start.3 = (f32[1,1,4,256,256]{4,3,2,1,0:T(8,128)S(1)}, f32[1,1,4,256,256]{4,3,2,1,0:T(8,128)}, u32[]{:S(2)}) copy-start(f32[1,1,4,256,256]{4,3,2,1,0:T(8,128)} %param.15) | copy-start | bytes 3145732
  10.0 27.0 %collective-permute-start.5 = (f32[2,256,128]{2,1,0:T(8,128)S(1)}, f32[2,256,128]{2,1,0:T(8,128)S(1)}, u32[]{:S(2)}, u32[]{:S(2)}) collective-permute-start(f32[2,256,128]{2,1,0:T(8,128)S(1)} %get-tuple-element.58), channel_id=1, source_target_pairs={{1,2},{2,1},{3,4},{4,3},{5,6},{6,5},{7,8},{8,7},{9,10},{10,9},{11,... | collective-permute-start | bytes 786440 | tf_op jit(solution)/shard_map/ppermute | solution.py:537
  14.7 9.3 %collective-permute-start.3 = (f32[2,128,128]{2,1,0:T(8,128)S(1)}, f32[2,128,128]{2,1,0:T(8,128)S(1)}, u32[]{:S(2)}, u32[]{:S(2)}) collective-permute-start(f32[2,128,128]{2,1,0:T(8,128)S(1)} %get-tuple-element.71), channel_id=1, source_target_pairs={{1,18},{2,17},{3,20},{4,19},{5,22},{6,21},{7,24},{8,23},{9,26},{10... | collective-permute-start | bytes 393224 | tf_op jit(solution)/shard_map/ppermute | solution.py:537
  18.7 18.3 %collective-permute-start.4 = (f32[2,128,128]{2,1,0:T(8,128)S(1)}, f32[2,128,128]{2,1,0:T(8,128)S(1)}, u32[]{:S(2)}, u32[]{:S(2)}) collective-permute-start(f32[2,128,128]{2,1,0:T(8,128)S(1)} %get-tuple-element.70), channel_id=1, source_target_pairs={{17,2},{18,1},{19,4},{20,3},{21,6},{22,5},{23,8},{24,7},{25,10},{2... | collective-permute-start | bytes 393224 | tf_op jit(solution)/shard_map/ppermute | solution.py:537
  20.0 18.5 %collective-permute-start.2 = (f32[2,256,128]{2,1,0:T(8,128)S(1)}, f32[2,256,128]{2,1,0:T(8,128)S(1)}, u32[]{:S(2)}, u32[]{:S(2)}) collective-permute-start(f32[2,256,128]{2,1,0:T(8,128)S(1)} %get-tuple-element.59), channel_id=1, source_target_pairs={{0,1},{1,0},{2,3},{3,2},{4,5},{5,4},{6,7},{7,6},{8,9},{9,8},{10,11... | collective-permute-start | bytes 786440 | tf_op jit(solution)/shard_map/ppermute | solution.py:537
  22.2 15.5 %copy-start.4 = (bf16[768,256]{1,0:T(8,128)(2,1)S(1)}, bf16[768,256]{1,0:T(8,128)(2,1)}, u32[]{:S(2)}) copy-start(bf16[768,256]{1,0:T(8,128)(2,1)} %constant.39.clone.table) | copy-start | bytes 1179652
  37.0 1.5 %collective-permute-start.6 = (f32[2,256,128]{2,1,0:T(8,128)S(1)}, f32[2,256,128]{2,1,0:T(8,128)S(1)}, u32[]{:S(2)}, u32[]{:S(2)}) collective-permute-start(f32[2,256,128]{2,1,0:T(8,128)S(1)} %pad_maximum_fusion.1), channel_id=1, source_target_pairs={{0,1},{1,0},{2,3},{3,2},{4,5},{5,4},{6,7},{7,6},{8,9},{9,8},{10,11... | collective-permute-start | bytes 786440 | tf_op jit(solution)/shard_map/ppermute | solution.py:537
  37.7 1.0 copy-start
  37.7 1.1 %copy-start.5 = (bf16[256,768]{1,0:T(8,128)(2,1)S(1)}, bf16[256,768]{1,0:T(8,128)(2,1)}, u32[]{:S(2)}) copy-start(bf16[256,768]{1,0:T(8,128)(2,1)} %constant.40.clone.left_table) | copy-start | bytes 1179652
  37.7 1.3 %copy-start.6 = (bf16[768,256]{1,0:T(8,128)(2,1)S(1)}, bf16[768,256]{1,0:T(8,128)(2,1)}, u32[]{:S(2)}) copy-start(bf16[768,256]{1,0:T(8,128)(2,1)} %constant.41.clone.right_table) | copy-start | bytes 1179652
  37.8 1.3 %copy-start.7 = (f32[2,128,128]{2,1,0:T(8,128)S(1)}, f32[2,128,128]{2,1,0:T(8,128)}, u32[]{:S(2)}) copy-start(f32[2,128,128]{2,1,0:T(8,128)} %constant.42.clone.row_table) | copy-start | bytes 393220
  37.8 1.3 %copy-start.8 = (f32[2,128,128]{2,1,0:T(8,128)S(1)}, f32[2,128,128]{2,1,0:T(8,128)}, u32[]{:S(2)}) copy-start(f32[2,128,128]{2,1,0:T(8,128)} %constant.43.clone.lane_table) | copy-start | bytes 393220
  38.6 0.8 copy-start.9
  38.6 0.8 copy-start.10
  44.1 5.5 %copy-start.1 = (f32[2,256,512]{2,1,0:T(8,128)}, f32[2,256,512]{2,1,0:T(8,128)S(1)}, u32[]{:S(2)}) copy-start(f32[2,256,512]{2,1,0:T(8,128)S(1)} %get-tuple-element.34.inner) | copy-start | bytes 3145732
  44.1 4.3 %collective-permute-start.7 = (f32[2,512,128]{2,1,0:T(8,128)S(1)}, f32[2,512,128]{2,1,0:T(8,128)S(1)}, u32[]{:S(2)}, u32[]{:S(2)}) collective-permute-start(f32[2,512,128]{2,1,0:T(8,128)S(1)} %get-tuple-element.36), channel_id=1, source_target_pairs={{0,1},{1,0},{2,3},{3,2},{4,5},{5,4},{6,7},{7,6},{8,9},{9,8},{10,11... | collective-permute-start | bytes 1572872 | tf_op jit(solution)/shard_map/ppermute | solution.py:537
  50.3 22.9 %all-to-all-start = ((f32[64,8,128]{2,1,0:T(8,128)}), f32[64,8,128]{2,1,0:T(8,128)}, u32[]{:S(2)}, u32[]{:S(2)}) async-start(f32[64,8,128]{2,1,0:T(8,128)} %bitcast.5), calls=%async_computation | async-start | bytes 524288 | tf_op jit(solution)/shard_map/all_to_all | solution.py:625
  63.5 42.7 %collective-permute-start.8 = (f32[2,128,512]{2,1,0:T(8,128)}, f32[2,128,512]{2,1,0:T(8,128)S(1)}, u32[]{:S(2)}, u32[]{:S(2)}) collective-permute-start(f32[2,128,512]{2,1,0:T(8,128)} %get-tuple-element.44), channel_id=1, source_target_pairs={{0,16},{1,17},{2,18},{3,19},{4,20},{5,21},{6,22},{7,23},{8,24},{9,... | collective-permute-start | bytes 1572872 | tf_op jit(solution)/shard_map/ppermute | solution.py:537
  67.9 38.3 %collective-permute-start.9 = (f32[2,128,512]{2,1,0:T(8,128)}, f32[2,128,512]{2,1,0:T(8,128)S(1)}, u32[]{:S(2)}, u32[]{:S(2)}) collective-permute-start(f32[2,128,512]{2,1,0:T(8,128)} %get-tuple-element.45), channel_id=1, source_target_pairs={{16,0},{17,1},{18,2},{19,3},{20,4},{21,5},{22,6},{23,7},{24,8},{25... | collective-permute-start | bytes 1572872 | tf_op jit(solution)/shard_map/ppermute | solution.py:537
  69.9 36.3 %collective-permute-start.12 = (f32[2,256,128]{2,1,0:T(8,128)S(1)}, f32[2,256,128]{2,1,0:T(8,128)S(1)}, u32[]{:S(2)}, u32[]{:S(2)}) collective-permute-start(f32[2,256,128]{2,1,0:T(8,128)S(1)} %get-tuple-element.48), channel_id=1, source_target_pairs={{1,2},{2,1},{3,4},{4,3},{5,6},{6,5},{7,8},{8,7},{9,10},{10,9},{11,... | collective-permute-start | bytes 786440 | tf_op jit(solution)/shard_map/ppermute | solution.py:537
  75.6 28.3 %all-to-all-start.1 = ((f32[64,8,128]{2,1,0:T(8,128)}), f32[64,8,128]{2,1,0:T(8,128)}, u32[]{:S(2)}, u32[]{:S(2)}) async-start(f32[64,8,128]{2,1,0:T(8,128)} %broadcast_in_dim.9), calls=%async_computation.1 | async-start | bytes 524288 | tf_op jit(solution)/shard_map/all_to_all | solution.py:558
  87.6 11.3 %collective-permute-start.10 = (f32[2,128,128]{2,1,0:T(8,128)S(1)}, f32[2,128,128]{2,1,0:T(8,128)S(1)}, u32[]{:S(2)}, u32[]{:S(2)}) collective-permute-start(f32[2,128,128]{2,1,0:T(8,128)S(1)} %get-tuple-element.46), channel_id=1, source_target_pairs={{17,2},{18,1},{19,4},{20,3},{21,6},{22,5},{23,8},{24,7},{25,10},{2... | collective-permute-start | bytes 393224 | tf_op jit(solution)/shard_map/ppermute | solution.py:537
  88.9 17.3 %collective-permute-start.11 = (f32[2,128,128]{2,1,0:T(8,128)S(1)}, f32[2,128,128]{2,1,0:T(8,128)S(1)}, u32[]{:S(2)}, u32[]{:S(2)}) collective-permute-start(f32[2,128,128]{2,1,0:T(8,128)S(1)} %get-tuple-element.47), channel_id=1, source_target_pairs={{1,18},{2,17},{3,20},{4,19},{5,22},{6,21},{7,24},{8,23},{9,26},{10... | collective-permute-start | bytes 393224 | tf_op jit(solution)/shard_map/ppermute | solution.py:537
  103.9 4.0 %collective-permute-start.15 = (f32[2,256,128]{2,1,0:T(8,128)}, f32[2,256,128]{2,1,0:T(8,128)S(1)}, u32[]{:S(2)}, u32[]{:S(2)}) collective-permute-start(f32[2,256,128]{2,1,0:T(8,128)} %bitcast.9), channel_id=1, source_target_pairs={{0,1},{1,0},{2,3},{3,2},{4,5},{5,4},{6,7},{7,6},{8,9},{9,8},{10,11... | collective-permute-start | bytes 786440 | tf_op jit(solution)/shard_map/ppermute | solution.py:537
  106.2 1.4 %collective-permute-start.13 = (f32[2,128,128]{2,1,0:T(8,128)S(1)}, f32[2,128,128]{2,1,0:T(8,128)S(1)}, u32[]{:S(2)}, u32[]{:S(2)}) collective-permute-start(f32[2,128,128]{2,1,0:T(8,128)S(1)} %get-tuple-element.69), channel_id=1, source_target_pairs={{0,1},{1,0},{2,3},{3,2},{4,5},{5,4},{6,7},{7,6},{8,9},{9,8},{10,11... | collective-permute-start | bytes 393224 | tf_op jit(solution)/shard_map/ppermute | solution.py:537
  107.7 2.2 %collective-permute-start.14 = (f32[2,128,128]{2,1,0:T(8,128)S(1)}, f32[2,128,128]{2,1,0:T(8,128)S(1)}, u32[]{:S(2)}, u32[]{:S(2)}) collective-permute-start(f32[2,128,128]{2,1,0:T(8,128)S(1)} %get-tuple-element.53), channel_id=1, source_target_pairs={{0,1},{1,0},{2,3},{3,2},{4,5},{5,4},{6,7},{7,6},{8,9},{9,8},{10,11... | collective-permute-start | bytes 393224 | tf_op jit(solution)/shard_map/ppermute | solution.py:537
  107.9 1.9 %copy-start.2 = (f32[2,256,512]{2,1,0:T(8,128)S(1)}, f32[2,256,512]{2,1,0:T(8,128)}, u32[]{:S(2)}) copy-start(f32[2,256,512]{2,1,0:T(8,128)} %copy-done.1) | copy-start | bytes 3145732

commit v2 on v1

--- a/solution.py
+++ b/solution.py
@@ -19,6 +19,7 @@
 AXES = ("row", "pair", "core")
 CHIPS = ("row", "pair")
 LANES = 128
+PATCHES = 4
 TILE = 8
 VMEM_LIMIT = 28 * 1024 * 1024
 
@@ -173,7 +174,7 @@
     counts,
     rows,
     cols,
-    core,
+    place_of,
     centre,
     top,
     bottom,
@@ -189,8 +190,8 @@
     row_table,
     lane_table,
     inner_out,
-    up_out,
-    down_out,
+    first_out,
+    second_out,
     near_mid_out,
     far_mid_out,
     given_out,
@@ -206,8 +207,11 @@
     margin = size // 2
     height, width = centre.shape[1:]
     inner = pl.ds(margin, width)
-    near = pl.ds(pl.multiple_of((1 - core[0]) * (margin + width), LANES), margin)
-    far = pl.ds(pl.multiple_of(core[0] * (margin + width), LANES), margin)
+    core, odd = place_of[0], place_of[1]
+    near = pl.ds(pl.multiple_of((1 - core) * (margin + width), LANES), margin)
+    far = pl.ds(pl.multiple_of(core * (margin + width), LANES), margin)
+    first = pl.ds(pl.multiple_of((1 - odd) * (margin + height), margin), margin)
+    second = pl.ds(pl.multiple_of(odd * (margin + height), margin), margin)
     head, middle, tail = pl.ds(0, margin), pl.ds(margin, height), pl.ds(margin + height, margin)
     moves = [
         (centre, extended.at[:, middle, inner]),
@@ -333,21 +337,21 @@
     def _():
         some_patches([count - 1])
 
-    given_out[:, :margin] = gradient[:, head, near]
-    given_out[:, margin : 2 * margin] = gradient[:, tail, near]
+    given_out[:, :margin] = gradient[:, first, near]
+    given_out[:, margin : 2 * margin] = gradient[:, second, near]
     for part in range(2):
-        given_out[part, 2 * margin :] = probe_sum[part, 1 - core[0]]
-        probe_out[part] = probe_sum[part, core[0]]
+        given_out[part, 2 * margin :] = probe_sum[part, 1 - core]
+        probe_out[part] = probe_sum[part, core]
     inner_out[...] = gradient[:, middle, inner]
-    up_out[...] = gradient[:, head, inner]
-    down_out[...] = gradient[:, tail, inner]
+    first_out[...] = gradient[:, first, inner]
+    second_out[...] = gradient[:, second, inner]
     near_mid_out[...] = gradient[:, middle, near]
     far_mid_out[...] = gradient[:, middle, far]
     far_top_out[...] = gradient[:, head, far]
     far_bottom_out[...] = gradient[:, tail, far]
 
 
-def patches(counts, rows, cols, core, pieces, probe, amplitude):
+def patches(counts, rows, cols, place_of, pieces, probe, amplitude):
     size = probe.shape[1]
     margin = size // 2
     height, width = pieces[0].shape[1:]
@@ -383,7 +387,7 @@
         counts,
         rows,
         cols,
-        core,
+        place_of,
         *pieces,
         probe,
         amplitude,
@@ -392,13 +396,12 @@
 
 
 def haar_kernel(
-    core,
+    place_of,
     centre,
     inner,
-    above,
-    below,
-    near_top,
-    near_bottom,
+    first,
+    second,
+    near_mid,
     far_mid,
     far_top,
     far_bottom,
@@ -406,20 +409,23 @@
     *scratch,
 ):
     height, width = centre.shape[1:]
-    margin = above.shape[1]
+    margin = first.shape[1]
+    core, odd = place_of[0], place_of[1]
     levels = [scratch[level] for level in range(LEVELS)]
     details = [scratch[LEVELS + level] for level in range(LEVELS - 1)]
     columns = width // LANES
     work = levels[0]
-    near = (1 - core[0]) * (columns - 1)
-    far = core[0] * (columns - 1)
+    near = (1 - core) * (columns - 1)
+    far = core * (columns - 1)
+    first_rows = pl.ds(pl.multiple_of((1 - odd) * (height - margin), margin), margin)
+    second_rows = pl.ds(pl.multiple_of(odd * (height - margin), margin), margin)
     for part in range(2):
         for column in range(columns):
             piece = part, slice(None), pl.ds(column * LANES, LANES)
-            gathered = jnp.concatenate([above[piece], below[piece]], axis=0) + inner[piece]
-            work[part, column] = centre[piece] - STEP_OBJECT * gathered
-        sides = jnp.concatenate([near_top[part], near_bottom[part]], axis=0)
-        work[part, near] -= STEP_OBJECT * sides
+            work[part, column] = centre[piece] - STEP_OBJECT * inner[piece]
+            work[part, column, first_rows] -= STEP_OBJECT * first[piece]
+            work[part, column, second_rows] -= STEP_OBJECT * second[piece]
+        work[part, near] -= STEP_OBJECT * near_mid[part]
         corners = jnp.concatenate([far_top[part], far_bottom[part]], axis=0)
         work[part, far] -= STEP_OBJECT * (far_mid[part] + corners)
 
@@ -511,7 +517,7 @@
             out[part, :, pl.ds(column * LANES, LANES)] = work[part, column]
 
 
-def shrink_object(core, *pieces):
+def shrink_object(place_of, *pieces):
     smem = pl.BlockSpec(memory_space=pltpu.SMEM)
     vmem = pl.BlockSpec(memory_space=pltpu.VMEM)
     shape = pieces[0].shape
@@ -524,7 +530,74 @@
         scratch_shapes=[pltpu.VMEM(size, jnp.float32) for size in sizes + sizes[1:]],
         compiler_params=pltpu.CompilerParams(vmem_limit_bytes=VMEM_LIMIT),
         name="haar",
-    )(core, *pieces)
+    )(place_of, *pieces)
+
+
+def join_kernel(place_of, first, second, given, kept, first_out, second_out, shares):
+    margin = first.shape[1]
+    width = first.shape[2]
+    near = pl.ds(pl.multiple_of((1 - place_of[0]) * (width - LANES), LANES), LANES)
+    first_out[...] = first[...]
+    second_out[...] = second[...]
+    first_out[:, :, near] += given[:, :margin]
+    second_out[:, :, near] += given[:, margin : 2 * margin]
+    shares[...] = (kept[...] + given[:, 2 * margin :]).reshape(shares.shape)
+
+
+def joined(place_of, first, second, given, kept):
+    smem = pl.BlockSpec(memory_space=pltpu.SMEM)
+    vmem = pl.BlockSpec(memory_space=pltpu.VMEM)
+    shapes = [first.shape, second.shape, (kept.size // (TILE * LANES), TILE, LANES)]
+    return pl.pallas_call(
+        join_kernel,
+        out_shape=tuple(jax.ShapeDtypeStruct(shape, jnp.float32) for shape in shapes),
+        in_specs=[smem] + [vmem] * 4,
+        out_specs=[vmem] * 3,
+        compiler_params=pltpu.CompilerParams(vmem_limit_bytes=VMEM_LIMIT),
+        name="joined",
+    )(place_of, first, second, given, kept)
+
+
+def total_kernel(shares, tile, out):
+    total = shares[0]
+    for index in range(1, shares.shape[0]):
+        total = total + shares[index]
+    total = tile[...] - total * (PROBE_STEP / (PATCHES * out.shape[0]))
+    for index in range(out.shape[0]):
+        out[index] = total
+
+
+def new_tiles(shares, tile, devices):
+    vmem = pl.BlockSpec(memory_space=pltpu.VMEM)
+    return pl.pallas_call(
+        total_kernel,
+        out_shape=jax.ShapeDtypeStruct((devices,) + tile.shape, jnp.float32),
+        in_specs=[vmem] * 2,
+        out_specs=vmem,
+        compiler_params=pltpu.CompilerParams(vmem_limit_bytes=VMEM_LIMIT),
+        name="new_tiles",
+    )(shares, tile)
+
+
+def probe_kernel(tiles, out):
+    size = out.shape[1]
+    chips = size // TILE
+    for part in range(2):
+        for half in range(2):
+            value = tiles[pl.ds(part * chips, chips), half]
+            out[part, :, pl.ds(half * LANES, LANES)] = value.reshape(size, LANES)
+
+
+def laid_out(tiles, shape):
+    vmem = pl.BlockSpec(memory_space=pltpu.VMEM)
+    return pl.pallas_call(
+        probe_kernel,
+        out_shape=jax.ShapeDtypeStruct(shape, jnp.float32),
+        in_specs=[vmem],
+        out_specs=vmem,
+        compiler_params=pltpu.CompilerParams(vmem_limit_bytes=VMEM_LIMIT),
+        name="laid_out",
+    )(tiles)
 
 
 def permuted(value, move):
@@ -553,9 +626,8 @@
     return half.reshape(lax.axis_size(CHIPS), -1, LANES)
 
 
-def handed_out(tile):
-    tiles = jnp.broadcast_to(tile[None], (lax.axis_size(CHIPS),) + tile.shape)
-    return lax.all_to_all(tiles, CHIPS, 0, 0, tiled=True)
+def pair_to(first):
+    return lambda row, col: (row + (1 if (row % 2 == 0) == first else -1), col)
 
 
 def on_device(object_now, object_prev, probe, amplitudes, pos_row, pos_col, counts):
@@ -564,8 +636,8 @@
     height, width = centre.shape[1:]
     slots = amplitudes.shape[2]
     core = lax.axis_index("core")
-    core_word = core.reshape(1)
-    devices = lax.axis_size(AXES)
+    odd = lax.axis_index("row") % 2
+    place_of = jnp.stack([core, odd])
 
     def sides(value):
         first, last = value[:, :, :margin], value[:, :, width - margin :]
@@ -589,8 +661,8 @@
     near_corner = permuted(near_corner, near_to)
     (
         inner,
-        up,
-        down,
+        first,
+        second,
         near_mid,
         far_mid,
         given,
@@ -601,50 +673,37 @@
         counts.reshape(1),
         pos_row.reshape(slots),
         pos_col.reshape(slots),
-        core_word,
+        place_of,
         (centre, top, bottom, near_mid, far_mid, near_corner, far_top, far_bottom),
         probe,
         ordered_amplitude(amplitudes[0, 0]),
     )
     given = permuted(given, near_to)
-    corner = given[:, : 2 * margin]
-    shares = chip_tiles(probe_kept + given[:, 2 * margin :])
-
-    def with_corner(strip, piece):
-        none = jnp.zeros_like(piece)
-        first = jnp.where(core == 0, none, piece)
-        last = jnp.where(core == 0, piece, none)
-        gap = jnp.zeros(piece.shape[:2] + (width - 2 * margin,), piece.dtype)
-        return strip + jnp.concatenate([first, gap, last], axis=2)
-
-    up = with_corner(up, corner[:, :margin])
-    down = with_corner(down, corner[:, margin:])
-    up, down, far_top, far_bottom, far_mid, near_mid, shares = lax.optimization_barrier(
-        (up, down, far_top, far_bottom, far_mid, near_mid, shares)
-    )
-    shares = lax.all_to_all(shares, CHIPS, 0, 0, tiled=True)
-    below = permuted(up, up_by(-1))
-    above = permuted(down, up_by(1))
+    first, second, shares = joined(place_of, first, second, given, probe_kept)
+    first, second, far_top, far_bottom, far_mid, near_mid, shares = lax.optimization_barrier(
+        (first, second, far_top, far_bottom, far_mid, near_mid, shares)
+    )
+    first = permuted(first, pair_to(True))
+    first, second = lax.optimization_barrier((first, second))
+    second = permuted(second, pair_to(False))
     far_below = permuted(far_top, far_to(-1))
     far_above = permuted(far_bottom, far_to(1))
     far_mid = permuted(far_mid, far_to(0))
-    near_mid, above, below, far_below, far_above, far_mid = lax.optimization_barrier(
-        (near_mid, above, below, far_below, far_above, far_mid)
-    )
-    near_top = permuted(near_mid[:, :margin], near_to)
-    near_top, near_bottom = lax.optimization_barrier((near_top, near_mid[:, margin:]))
-    near_bottom = permuted(near_bottom, near_to)
+    near_mid, first, second, far_below, far_above, far_mid = lax.optimization_barrier(
+        (near_mid, first, second, far_below, far_above, far_mid)
+    )
+    near_mid = permuted(near_mid, near_to)
+    shares = lax.all_to_all(shares, CHIPS, 0, 0, tiled=True)
     columns = [probe[:, :, LANES * index : LANES * (index + 1)] for index in range(2)]
     tile = lax.dynamic_index_in_dim(
         chip_tiles(jnp.where(core == 0, *columns)), lax.axis_index(CHIPS), keepdims=False
     )
-    tile = tile - PROBE_STEP / (slots * devices) * jnp.sum(shares, axis=0)
-    mine = handed_out(tile).reshape(columns[0].shape)
-    other = permuted(mine, near_to)
-    probe_new = jnp.concatenate(
-        [jnp.where(core == 0, mine, other), jnp.where(core == 0, other, mine)], axis=2
-    )
-    object_new = shrink_object(core_word, centre, inner, above, below, near_top, near_bottom, far_mid, far_above, far_below)
+    tiles = new_tiles(shares, tile, lax.axis_size(AXES))
+    tiles = lax.all_to_all(tiles, AXES, 0, 0, tiled=True)
+    probe_new = laid_out(tiles.reshape(-1, 2, TILE, LANES), probe.shape)
+    object_new = shrink_object(
+        place_of, centre, inner, first, second, near_mid, far_mid, far_above, far_below
+    )
     return object_new, probe_new
 
 

time: 115 us -> 112 us (0.974)
  starting transfers between devices: 65.8 us -> 52.2 us
  Pallas kernels: 9.27 us -> 18.5 us
  other arithmetic: 8.15 us -> 3.41 us
  local copies, waits for them, and re-layouts: 1.69 us -> 5.97 us
  waiting for transfers between devices: 27.2 us -> 30.1 us
    ppermute x16 -> x14, starting transfers between devices: 40.6 us -> 32.5 us  [permuted(): return lax.ppermute(value, AXES, pairs)]
    all_to_all x1, waiting for transfers between devices: 0.01 us -> 5.46 us  [on_device(): shares = lax.all_to_all(shares, CHIPS, 0, 0, tiled=True)]
    pallas_call x1, Pallas kernels: 4.7 us -> 9.44 us  [patches(): pl.pallas_call(patch_kernel, out_shape=tuple((pltpu.VMEM((2,) + shape, jn...]
    unnamed x22 -> x40, local copies, waits for them, and re-layouts: 0.83 us -> 5.07 us
    pallas_call x0 -> x3, Pallas kernels: none -> 3.33 us  [the longest x1 1.56 us: joined(): pl.pallas_call(join_kernel, out_shape=tuple((jax.ShapeDtypeStruct(shape,...]
    all_to_all x1, starting transfers between devices: 13.2 us -> 10.3 us  [on_device(): shares = lax.all_to_all(shares, CHIPS, 0, 0, tiled=True)]
    all_to_all x1, starting transfers between devices: 12 us -> 9.46 us  [on_device(): tiles = lax.all_to_all(tiles, AXES, 0, 0, tiled=True)]
    all_to_all x1, waiting for transfers between devices: 4.97 us -> 2.88 us  [on_device(): tiles = lax.all_to_all(tiles, AXES, 0, 0, tiled=True)]
  transfers between devices with their start and end apart: 18 -> 16, of which waited for: 7 -> 7; matrix products, arithmetic and copies ran while one was open for 5% -> 1% of each run, Pallas kernels for 1% -> 2%
where the time goes in v2:
time: 112 us
  starting transfers between devices  52.2 us (47%)
  waiting for transfers between devices  30.1 us (27%)
  Pallas kernels  18.5 us (17%)
  local copies, waits for them, and re-layouts  5.97 us (5%)
  other arithmetic  3.41 us (3%)
  between operations  1.55 us (1%)
    ppermute x14, starting transfers between devices, permuted(): return lax.ppermute(value, AXES, pairs)  32.5 us
    ppermute x14, waiting for transfers between devices, permuted(): return lax.ppermute(value, AXES, pairs)  21.8 us
    all_to_all x1, starting transfers between devices, on_device(): shares = lax.all_to_all(shares, CHIPS, 0, 0, tiled=True)  10.3 us
    all_to_all x1, starting transfers between devices, on_device(): tiles = lax.all_to_all(tiles, AXES, 0, 0, tiled=True)  9.46 us
    pallas_call x1, Pallas kernels, patches(): pl.pallas_call(patch_kernel, out_shape=tuple((pltpu.VMEM((2,) + shape, jn...  9.44 us
    all_to_all x1, waiting for transfers between devices, on_device(): shares = lax.all_to_all(shares, CHIPS, 0, 0, tiled=True)  5.46 us
    unnamed x40, local copies, waits for them, and re-layouts  5.07 us
    pallas_call x1, Pallas kernels, shrink_object(): pl.pallas_call(haar_kernel, out_shape=jax.ShapeDtypeStruct(shape, jnp.flo...  5.07 us
  transfers between devices with their start and end apart: 16, of which 7 were waited for; matrix products, arithmetic and copies ran while one was open for 1% of the time, Pallas kernels for 2%

profile of v2, /device:TPU:1, one launch (start us, length us, event | category | flops | bytes accessed | tf_op | source)
XLA Modules:
  0.0 111.8 jit_solution(8161399359437459167)
XLA Ops:
  0.6 1.8 %multiply_add_fusion.centre = f32[2,256,512]{2,1,0:T(8,128)S(1)} fusion(f32[2,256,512]{2,1,0:T(8,128)} %param.12, f32[2,256,512]{2,1,0:T(8,128)} %param.13), kind=kLoop, calls=%fused_computation | loop fusion | flops 786432 | bytes 3145728 | tf_op jit(solution)/shard_map/add | solution.py:634
  2.4 0.9 fusion
  3.3 1.3 %collective-permute-start.1 = (f32[2,128,512]{2,1,0:T(8,128)S(1)}, f32[2,128,512]{2,1,0:T(8,128)S(1)}, u32[]{:S(2)}, u32[]{:S(2)}) collective-permute-start(f32[2,128,512]{2,1,0:T(8,128)S(1)} %get-tuple-element.66), channel_id=1, source_target_pairs={{16,0},{17,1},{18,2},{19,3},{20,4},{21,5},{22,6},{23,7},{24,8},{25... | collective-permute-start | bytes 1572872 | tf_op jit(solution)/shard_map/ppermute | solution.py:610
  4.6 6.1 %collective-permute-start = (f32[2,128,512]{2,1,0:T(8,128)}, f32[2,128,512]{2,1,0:T(8,128)S(1)}, u32[]{:S(2)}, u32[]{:S(2)}) collective-permute-start(f32[2,128,512]{2,1,0:T(8,128)} %get-tuple-element.67), channel_id=1, source_target_pairs={{0,16},{1,17},{2,18},{3,19},{4,20},{5,21},{6,22},{7,23},{8,24},{9,... | collective-permute-start | bytes 1572872 | tf_op jit(solution)/shard_map/ppermute | solution.py:610
  10.7 0.7 slice_select_fusion.1
  11.5 4.4 %collective-permute-start.5 = (f32[2,256,128]{2,1,0:T(8,128)S(1)}, f32[2,256,128]{2,1,0:T(8,128)S(1)}, u32[]{:S(2)}, u32[]{:S(2)}) collective-permute-start(f32[2,256,128]{2,1,0:T(8,128)S(1)} %get-tuple-element.64), channel_id=1, source_target_pairs={{1,2},{2,1},{3,4},{4,3},{5,6},{6,5},{7,8},{8,7},{9,10},{10,9},{11,... | collective-permute-start | bytes 786440 | tf_op jit(solution)/shard_map/ppermute | solution.py:610
  16.0 4.1 %collective-permute-start.3 = (f32[2,128,128]{2,1,0:T(8,128)S(1)}, f32[2,128,128]{2,1,0:T(8,128)S(1)}, u32[]{:S(2)}, u32[]{:S(2)}) collective-permute-start(f32[2,128,128]{2,1,0:T(8,128)S(1)} %get-tuple-element.69), channel_id=1, source_target_pairs={{1,18},{2,17},{3,20},{4,19},{5,22},{6,21},{7,24},{8,23},{9,26},{10... | collective-permute-start | bytes 393224 | tf_op jit(solution)/shard_map/ppermute | solution.py:610
  20.0 1.3 %collective-permute-start.4 = (f32[2,128,128]{2,1,0:T(8,128)S(1)}, f32[2,128,128]{2,1,0:T(8,128)S(1)}, u32[]{:S(2)}, u32[]{:S(2)}) collective-permute-start(f32[2,128,128]{2,1,0:T(8,128)S(1)} %get-tuple-element.68), channel_id=1, source_target_pairs={{17,2},{18,1},{19,4},{20,3},{21,6},{22,5},{23,8},{24,7},{25,10},{2... | collective-permute-start | bytes 393224 | tf_op jit(solution)/shard_map/ppermute | solution.py:610
  21.3 0.0 collective-permute-done.1.bottom
  21.3 1.6 %collective-permute-start.2 = (f32[2,256,128]{2,1,0:T(8,128)}, f32[2,256,128]{2,1,0:T(8,128)S(1)}, u32[]{:S(2)}, u32[]{:S(2)}) collective-permute-start(f32[2,256,128]{2,1,0:T(8,128)} %get-tuple-element.65), channel_id=1, source_target_pairs={{0,1},{1,0},{2,3},{3,2},{4,5},{5,4},{6,7},{7,6},{8,9},{9,8},{10,11... | collective-permute-start | bytes 786440 | tf_op jit(solution)/shard_map/ppermute | solution.py:610
  23.0 0.0 copy-start.4
  23.0 0.0 collective-permute-done.top
  23.0 0.7 pad_maximum_fusion
  23.7 1.2 %collective-permute-done.3.far_top = f32[2,128,128]{2,1,0:T(8,128)S(1)} collective-permute-done((f32[2,128,128]{2,1,0:T(8,128)S(1)}, f32[2,128,128]{2,1,0:T(8,128)S(1)}, u32[]{:S(2)}, u32[]{:S(2)}) %collective-permute-start.3) | collective-permute-done | bytes 131104 | tf_op jit(solution)/shard_map/ppermute | solution.py:610
  25.0 0.7 copy-done.11
  25.6 12.2 %collective-permute-done.4.far_bottom = f32[2,128,128]{2,1,0:T(8,128)S(1)} collective-permute-done((f32[2,128,128]{2,1,0:T(8,128)S(1)}, f32[2,128,128]{2,1,0:T(8,128)S(1)}, u32[]{:S(2)}, u32[]{:S(2)}) %collective-permute-start.4) | collective-permute-done | bytes 131104 | tf_op jit(solution)/shard_map/ppermute | solution.py:610
  37.8 0.6 copy-done.13
  38.5 0.0 collective-permute-done.5.far_mid
  38.5 0.0 collective-permute-start.6
  39.1 0.0 copy-start.3
  39.1 1.2 %copy-done.3 = f32[1,1,4,256,256]{4,3,2,1,0:T(8,128)S(1)} copy-done((f32[1,1,4,256,256]{4,3,2,1,0:T(8,128)S(1)}, f32[1,1,4,256,256]{4,3,2,1,0:T(8,128)}, u32[]{:S(2)}) %copy-start.3) | copy-done | bytes 1048600
  40.4 0.0 copy-start.10
  40.4 0.7 ordered_amplitude.1.amplitude
  41.1 0.1 pad_add_fusion.place_of
  41.2 0.0 collective-permute-done.2.near_mid
  41.2 0.0 collective-permute-done.6.near_corner
  41.2 0.0 copy-start.16
  41.2 0.2 copy-done
  41.4 0.1 copy-done.5
  41.5 0.1 copy-done.6
  41.6 0.0 copy-done.9
  41.7 0.0 copy-done.10
  41.7 0.0 copy-done.12
  41.7 0.0 copy-done.14
  41.8 0.2 copy-done.15
  42.0 0.0 copy-done.16
  42.0 9.4 %patches.1 = (f32[2,256,512]{2,1,0:T(8,128)S(1)}, f32[2,128,512]{2,1,0:T(8,128)S(1)}, f32[2,128,512]{2,1,0:T(8,128)S(1)}, f32[2,256,128]{2,1,0:T(8,128)S(1)}, f3...) custom-call(s32[1]{0:T(128)} %bitcast.10.counts, ...), custom_call_target="tpu_custom_call" | custom-call | tf_op jit(solution)/shard_map/patches/pallas_call | solution.py:373
  51.5 0.0 copy-start.1
  51.5 1.0 copy-done.1
  52.4 0.0 collective-permute-start.7
  52.4 1.9 %collective-permute-done.7.given = f32[2,512,128]{2,1,0:T(8,128)S(1)} collective-permute-done((f32[2,512,128]{2,1,0:T(8,128)S(1)}, f32[2,512,128]{2,1,0:T(8,128)S(1)}, u32[]{:S(2)}, u32[]{:S(2)}) %collective-permute-start.7) | collective-permute-done | bytes 524320 | tf_op jit(solution)/shard_map/ppermute | solution.py:610
  54.3 1.6 %joined.1 = (f32[2,128,512]{2,1,0:T(8,128)S(1)}, f32[2,128,512]{2,1,0:T(8,128)}, f32[64,8,128]{2,1,0:T(8,128)}) custom-call(s32[2]{0:T(128)S(1)} %pad_add_fusion.place_of, f32[2,128,512]{2,1,0:T(8,128)S(1)} %get-tuple-element.38.first, f32[2,128,512]{2,1,0:T(8,128)S(1)} %get-tuple-element.39.second, f32[2,512,128]{2,1,0:T(8,128)S(1)} %collective-permute-done.7.given, ...), custom_call_target="tpu_custom_call" | custom-call | tf_op jit(solution)/shard_map/joined/pallas_call | solution.py:551
  55.9 0.0 copy-done.17
  55.9 3.0 %collective-permute-start.8 = (f32[2,128,512]{2,1,0:T(8,128)S(1)}, f32[2,128,512]{2,1,0:T(8,128)S(1)}, u32[]{:S(2)}, u32[]{:S(2)}) collective-permute-start(f32[2,128,512]{2,1,0:T(8,128)S(1)} %get-tuple-element.50), channel_id=1, source_target_pairs={{0,16},{1,17},{2,18},{3,19},{4,20},{5,21},{6,22},{7,23},{8,24},{9,... | collective-permute-start | bytes 1572872 | tf_op jit(solution)/shard_map/ppermute | solution.py:610
  59.0 10.3 %all-to-all-start = ((f32[64,8,128]{2,1,0:T(8,128)}), f32[64,8,128]{2,1,0:T(8,128)S(1)}, u32[]{:S(2)}, u32[]{:S(2)}) async-start(f32[64,8,128]{2,1,0:T(8,128)} %get-tuple-element.63), calls=%async_computation | async-start | bytes 524288 | tf_op jit(solution)/shard_map/all_to_all | solution.py:696
  69.2 1.7 %collective-permute-done.8.first = f32[2,128,512]{2,1,0:T(8,128)S(1)} collective-permute-done((f32[2,128,512]{2,1,0:T(8,128)S(1)}, f32[2,128,512]{2,1,0:T(8,128)S(1)}, u32[]{:S(2)}, u32[]{:S(2)}) %collective-permute-start.8) | collective-permute-done | bytes 524320 | tf_op jit(solution)/shard_map/ppermute | solution.py:610
  70.9 1.4 %collective-permute-start.9 = (f32[2,128,512]{2,1,0:T(8,128)}, f32[2,128,512]{2,1,0:T(8,128)}, u32[]{:S(2)}, u32[]{:S(2)}) collective-permute-start(f32[2,128,512]{2,1,0:T(8,128)} %get-tuple-element.53), channel_id=1, source_target_pairs={{16,32},{17,33},{18,34},{19,35},{20,36},{21,37},{22,38},{23,39},{2... | collective-permute-start | bytes 1572872 | tf_op jit(solution)/shard_map/ppermute | solution.py:610
  72.4 2.4 %collective-permute-start.12 = (f32[2,256,128]{2,1,0:T(8,128)}, f32[2,256,128]{2,1,0:T(8,128)S(1)}, u32[]{:S(2)}, u32[]{:S(2)}) collective-permute-start(f32[2,256,128]{2,1,0:T(8,128)} %get-tuple-element.56), channel_id=1, source_target_pairs={{1,2},{2,1},{3,4},{4,3},{5,6},{6,5},{7,8},{8,7},{9,10},{10,9},{11,... | collective-permute-start | bytes 786440 | tf_op jit(solution)/shard_map/ppermute | solution.py:610
  74.8 5.5 %all-to-all-done.shares = f32[64,8,128]{2,1,0:T(8,128)S(1)} async-done(((f32[64,8,128]{2,1,0:T(8,128)}), f32[64,8,128]{2,1,0:T(8,128)S(1)}, u32[]{:S(2)}, u32[]{:S(2)}) %all-to-all-start) | async-done | bytes 262176 | tf_op jit(solution)/shard_map/all_to_all | solution.py:696
  80.2 0.9 new_tiles.1
  81.2 9.5 %all-to-all-start.1 = ((f32[128,8,128]{2,1,0:T(8,128)}), f32[128,8,128]{2,1,0:T(8,128)S(1)}, u32[]{:S(2)}, u32[]{:S(2)}) async-start(f32[128,8,128]{2,1,0:T(8,128)} %new_tiles.1), calls=%async_computation.1 | async-start | bytes 1048576 | tf_op jit(solution)/shard_map/all_to_all | solution.py:702
  90.6 1.3 %collective-permute-start.10 = (f32[2,128,128]{2,1,0:T(8,128)}, f32[2,128,128]{2,1,0:T(8,128)S(1)}, u32[]{:S(2)}, u32[]{:S(2)}) collective-permute-start(f32[2,128,128]{2,1,0:T(8,128)} %copy-done.19), channel_id=1, source_target_pairs={{17,2},{18,1},{19,4},{20,3},{21,6},{22,5},{23,8},{24,7},{25,10},{2... | collective-permute-start | bytes 393224 | tf_op jit(solution)/shard_map/ppermute | solution.py:610
  91.9 5.5 %collective-permute-start.11 = (f32[2,128,128]{2,1,0:T(8,128)}, f32[2,128,128]{2,1,0:T(8,128)S(1)}, u32[]{:S(2)}, u32[]{:S(2)}) collective-permute-start(f32[2,128,128]{2,1,0:T(8,128)} %copy-done.18), channel_id=1, source_target_pairs={{1,18},{2,17},{3,20},{4,19},{5,22},{6,21},{7,24},{8,23},{9,26},{10... | collective-permute-start | bytes 393224 | tf_op jit(solution)/shard_map/ppermute | solution.py:610
  97.4 4.8 %collective-permute-done.10.far_bottom = f32[2,128,128]{2,1,0:T(8,128)S(1)} collective-permute-done((f32[2,128,128]{2,1,0:T(8,128)}, f32[2,128,128]{2,1,0:T(8,128)S(1)}, u32[]{:S(2)}, u32[]{:S(2)}) %collective-permute-start.10) | collective-permute-done | bytes 131104 | tf_op jit(solution)/shard_map/ppermute | solution.py:610
  102.2 0.0 collective-permute-done.11.far_top
  102.2 0.7 copy-done.7
  102.9 0.0 collective-permute-done.12.far_mid
  102.9 0.0 collective-permute-done.9.second
  102.9 0.0 collective-permute-start.13
  102.9 2.9 %all-to-all-done.1 = f32[128,8,128]{2,1,0:T(8,128)S(1)} async-done(((f32[128,8,128]{2,1,0:T(8,128)}), f32[128,8,128]{2,1,0:T(8,128)S(1)}, u32[]{:S(2)}, u32[]{:S(2)}) %all-to-all-start.1) | async-done | bytes 524320 | tf_op jit(solution)/shard_map/all_to_all | solution.py:702
  105.8 0.8 laid_out.1
  106.6 0.0 collective-permute-done.13.near_mid
  106.6 0.1 copy-done.8
  106.7 5.1 %haar.1 = f32[2,256,512]{2,1,0:T(8,128)} custom-call(s32[2]{0:T(128)S(1)} %pad_add_fusion.place_of, f32[2,256,512]{2,1,0:T(8,128)S(1)} %multiply_add_fusion.centre, f32[2,256,512]{2,1,0:T(8,128)S(1)} %copy-done.2, f32[2,128,512]{2,1,0:T(8,128)S(1)} %collective-permute-done.8.first, f32[2,128,512]{2,1,0:T(8,128)} %collective-permute-done.9.second, ...), custom_call_target="tpu_custom_call" | custom-call | tf_op jit(solution)/shard_map/haar/pallas_call | solution.py:525
  (24 shorter events, 0.1 us)
Async XLA Ops:
  3.3 18.0 %collective-permute-start.1 = (f32[2,128,512]{2,1,0:T(8,128)S(1)}, f32[2,128,512]{2,1,0:T(8,128)S(1)}, u32[]{:S(2)}, u32[]{:S(2)}) collective-permute-start(f32[2,128,512]{2,1,0:T(8,128)S(1)} %get-tuple-element.66), channel_id=1, source_target_pairs={{16,0},{17,1},{18,2},{19,3},{20,4},{21,5},{22,6},{23,7},{24,8},{25... | collective-permute-start | bytes 1572872 | tf_op jit(solution)/shard_map/ppermute | solution.py:610
  4.6 18.4 %collective-permute-start = (f32[2,128,512]{2,1,0:T(8,128)}, f32[2,128,512]{2,1,0:T(8,128)S(1)}, u32[]{:S(2)}, u32[]{:S(2)}) collective-permute-start(f32[2,128,512]{2,1,0:T(8,128)} %get-tuple-element.67), channel_id=1, source_target_pairs={{0,16},{1,17},{2,18},{3,19},{4,20},{5,21},{6,22},{7,23},{8,24},{9,... | collective-permute-start | bytes 1572872 | tf_op jit(solution)/shard_map/ppermute | solution.py:610
  11.5 27.0 %collective-permute-start.5 = (f32[2,256,128]{2,1,0:T(8,128)S(1)}, f32[2,256,128]{2,1,0:T(8,128)S(1)}, u32[]{:S(2)}, u32[]{:S(2)}) collective-permute-start(f32[2,256,128]{2,1,0:T(8,128)S(1)} %get-tuple-element.64), channel_id=1, source_target_pairs={{1,2},{2,1},{3,4},{4,3},{5,6},{6,5},{7,8},{8,7},{9,10},{10,9},{11,... | collective-permute-start | bytes 786440 | tf_op jit(solution)/shard_map/ppermute | solution.py:610
  16.0 9.0 %collective-permute-start.3 = (f32[2,128,128]{2,1,0:T(8,128)S(1)}, f32[2,128,128]{2,1,0:T(8,128)S(1)}, u32[]{:S(2)}, u32[]{:S(2)}) collective-permute-start(f32[2,128,128]{2,1,0:T(8,128)S(1)} %get-tuple-element.69), channel_id=1, source_target_pairs={{1,18},{2,17},{3,20},{4,19},{5,22},{6,21},{7,24},{8,23},{9,26},{10... | collective-permute-start | bytes 393224 | tf_op jit(solution)/shard_map/ppermute | solution.py:610
  20.0 17.8 %collective-permute-start.4 = (f32[2,128,128]{2,1,0:T(8,128)S(1)}, f32[2,128,128]{2,1,0:T(8,128)S(1)}, u32[]{:S(2)}, u32[]{:S(2)}) collective-permute-start(f32[2,128,128]{2,1,0:T(8,128)S(1)} %get-tuple-element.68), channel_id=1, source_target_pairs={{17,2},{18,1},{19,4},{20,3},{21,6},{22,5},{23,8},{24,7},{25,10},{2... | collective-permute-start | bytes 393224 | tf_op jit(solution)/shard_map/ppermute | solution.py:610
  21.3 19.8 %collective-permute-start.2 = (f32[2,256,128]{2,1,0:T(8,128)}, f32[2,256,128]{2,1,0:T(8,128)S(1)}, u32[]{:S(2)}, u32[]{:S(2)}) collective-permute-start(f32[2,256,128]{2,1,0:T(8,128)} %get-tuple-element.65), channel_id=1, source_target_pairs={{0,1},{1,0},{2,3},{3,2},{4,5},{5,4},{6,7},{7,6},{8,9},{9,8},{10,11... | collective-permute-start | bytes 786440 | tf_op jit(solution)/shard_map/ppermute | solution.py:610
  23.0 16.2 %copy-start.4 = (bf16[768,256]{1,0:T(8,128)(2,1)S(1)}, bf16[768,256]{1,0:T(8,128)(2,1)}, u32[]{:S(2)}) copy-start(bf16[768,256]{1,0:T(8,128)(2,1)} %constant.45.clone.table) | copy-start | bytes 1179652
  24.9 0.7 copy-start.11
  37.8 0.7 copy-start.13
  38.5 2.7 %collective-permute-start.6 = (f32[2,256,128]{2,1,0:T(8,128)}, f32[2,256,128]{2,1,0:T(8,128)}, u32[]{:S(2)}, u32[]{:S(2)}) collective-permute-start(f32[2,256,128]{2,1,0:T(8,128)} %pad_maximum_fusion), channel_id=1, source_target_pairs={{0,1},{1,0},{2,3},{3,2},{4,5},{5,4},{6,7},{7,6},{8,9},{9,8},{10,11... | collective-permute-start | bytes 786440 | tf_op jit(solution)/shard_map/ppermute | solution.py:610
  39.1 1.2 %copy-start.3 = (f32[1,1,4,256,256]{4,3,2,1,0:T(8,128)S(1)}, f32[1,1,4,256,256]{4,3,2,1,0:T(8,128)}, u32[]{:S(2)}) copy-start(f32[1,1,4,256,256]{4,3,2,1,0:T(8,128)} %param.15) | copy-start | bytes 3145732
  40.4 1.0 copy-start
  40.4 1.2 %copy-start.5 = (bf16[256,768]{1,0:T(8,128)(2,1)S(1)}, bf16[256,768]{1,0:T(8,128)(2,1)}, u32[]{:S(2)}) copy-start(bf16[256,768]{1,0:T(8,128)(2,1)} %constant.46.clone.left_table) | copy-start | bytes 1179652
  40.4 1.3 %copy-start.6 = (bf16[768,256]{1,0:T(8,128)(2,1)S(1)}, bf16[768,256]{1,0:T(8,128)(2,1)}, u32[]{:S(2)}) copy-start(bf16[768,256]{1,0:T(8,128)(2,1)} %constant.47.clone.right_table) | copy-start | bytes 1179652
  40.4 1.3 %copy-start.9 = (f32[2,128,128]{2,1,0:T(8,128)S(1)}, f32[2,128,128]{2,1,0:T(8,128)}, u32[]{:S(2)}) copy-start(f32[2,128,128]{2,1,0:T(8,128)} %constant.48.clone.row_table) | copy-start | bytes 393220
  40.4 1.3 %copy-start.10 = (f32[2,128,128]{2,1,0:T(8,128)S(1)}, f32[2,128,128]{2,1,0:T(8,128)}, u32[]{:S(2)}) copy-start(f32[2,128,128]{2,1,0:T(8,128)} %constant.49.clone.lane_table) | copy-start | bytes 393220
  40.4 1.4 %copy-start.12 = (f32[2,128,128]{2,1,0:T(8,128)S(1)}, f32[2,128,128]{2,1,0:T(8,128)}, u32[]{:S(2)}) copy-start(f32[2,128,128]{2,1,0:T(8,128)} %copy-done.11) | copy-start | bytes 393220
  40.4 1.4 %copy-start.14 = (f32[2,128,128]{2,1,0:T(8,128)S(1)}, f32[2,128,128]{2,1,0:T(8,128)}, u32[]{:S(2)}) copy-start(f32[2,128,128]{2,1,0:T(8,128)} %copy-done.13) | copy-start | bytes 393220
  41.2 0.8 copy-start.15
  41.2 0.8 copy-start.16
  51.5 1.0 copy-start.1
  52.4 3.5 %copy-start.17 = (f32[2,256,128]{2,1,0:T(8,128)}, f32[2,256,128]{2,1,0:T(8,128)S(1)}, u32[]{:S(2)}) copy-start(f32[2,256,128]{2,1,0:T(8,128)S(1)} %get-tuple-element.59) | copy-start | bytes 786436
  52.4 3.5 %copy-start.18 = (f32[2,128,128]{2,1,0:T(8,128)}, f32[2,128,128]{2,1,0:T(8,128)S(1)}, u32[]{:S(2)}) copy-start(f32[2,128,128]{2,1,0:T(8,128)S(1)} %get-tuple-element.55) | copy-start | bytes 393220
  52.4 3.5 %copy-start.19 = (f32[2,128,128]{2,1,0:T(8,128)}, f32[2,128,128]{2,1,0:T(8,128)S(1)}, u32[]{:S(2)}) copy-start(f32[2,128,128]{2,1,0:T(8,128)S(1)} %get-tuple-element.54) | copy-start | bytes 393220
  52.4 1.9 %collective-permute-start.7 = (f32[2,512,128]{2,1,0:T(8,128)S(1)}, f32[2,512,128]{2,1,0:T(8,128)S(1)}, u32[]{:S(2)}, u32[]{:S(2)}) collective-permute-start(f32[2,512,128]{2,1,0:T(8,128)S(1)} %get-tuple-element.40), channel_id=1, source_target_pairs={{0,1},{1,0},{2,3},{3,2},{4,5},{5,4},{6,7},{7,6},{8,9},{9,8},{10,11... | collective-permute-start | bytes 1572872 | tf_op jit(solution)/shard_map/ppermute | solution.py:610
  55.9 15.0 %collective-permute-start.8 = (f32[2,128,512]{2,1,0:T(8,128)S(1)}, f32[2,128,512]{2,1,0:T(8,128)S(1)}, u32[]{:S(2)}, u32[]{:S(2)}) collective-permute-start(f32[2,128,512]{2,1,0:T(8,128)S(1)} %get-tuple-element.50), channel_id=1, source_target_pairs={{0,16},{1,17},{2,18},{3,19},{4,20},{5,21},{6,22},{7,23},{8,24},{9,... | collective-permute-start | bytes 1572872 | tf_op jit(solution)/shard_map/ppermute | solution.py:610
  59.0 21.3 %all-to-all-start = ((f32[64,8,128]{2,1,0:T(8,128)}), f32[64,8,128]{2,1,0:T(8,128)S(1)}, u32[]{:S(2)}, u32[]{:S(2)}) async-start(f32[64,8,128]{2,1,0:T(8,128)} %get-tuple-element.63), calls=%async_computation | async-start | bytes 524288 | tf_op jit(solution)/shard_map/all_to_all | solution.py:696
  70.9 32.0 %collective-permute-start.9 = (f32[2,128,512]{2,1,0:T(8,128)}, f32[2,128,512]{2,1,0:T(8,128)}, u32[]{:S(2)}, u32[]{:S(2)}) collective-permute-start(f32[2,128,512]{2,1,0:T(8,128)} %get-tuple-element.53), channel_id=1, source_target_pairs={{16,32},{17,33},{18,34},{19,35},{20,36},{21,37},{22,38},{23,39},{2... | collective-permute-start | bytes 1572872 | tf_op jit(solution)/shard_map/ppermute | solution.py:610
  72.4 30.5 %collective-permute-start.12 = (f32[2,256,128]{2,1,0:T(8,128)}, f32[2,256,128]{2,1,0:T(8,128)S(1)}, u32[]{:S(2)}, u32[]{:S(2)}) collective-permute-start(f32[2,256,128]{2,1,0:T(8,128)} %get-tuple-element.56), channel_id=1, source_target_pairs={{1,2},{2,1},{3,4},{4,3},{5,6},{6,5},{7,8},{8,7},{9,10},{10,9},{11,... | collective-permute-start | bytes 786440 | tf_op jit(solution)/shard_map/ppermute | solution.py:610
  81.2 25.5 %copy-start.2 = (f32[2,256,512]{2,1,0:T(8,128)S(1)}, f32[2,256,512]{2,1,0:T(8,128)}, u32[]{:S(2)}) copy-start(f32[2,256,512]{2,1,0:T(8,128)} %copy-done.1) | copy-start | bytes 3145732
  81.2 24.6 %all-to-all-start.1 = ((f32[128,8,128]{2,1,0:T(8,128)}), f32[128,8,128]{2,1,0:T(8,128)S(1)}, u32[]{:S(2)}, u32[]{:S(2)}) async-start(f32[128,8,128]{2,1,0:T(8,128)} %new_tiles.1), calls=%async_computation.1 | async-start | bytes 1048576 | tf_op jit(solution)/shard_map/all_to_all | solution.py:702
  90.6 11.6 %collective-permute-start.10 = (f32[2,128,128]{2,1,0:T(8,128)}, f32[2,128,128]{2,1,0:T(8,128)S(1)}, u32[]{:S(2)}, u32[]{:S(2)}) collective-permute-start(f32[2,128,128]{2,1,0:T(8,128)} %copy-done.19), channel_id=1, source_target_pairs={{17,2},{18,1},{19,4},{20,3},{21,6},{22,5},{23,8},{24,7},{25,10},{2... | collective-permute-start | bytes 393224 | tf_op jit(solution)/shard_map/ppermute | solution.py:610
  91.9 10.3 %collective-permute-start.11 = (f32[2,128,128]{2,1,0:T(8,128)}, f32[2,128,128]{2,1,0:T(8,128)S(1)}, u32[]{:S(2)}, u32[]{:S(2)}) collective-permute-start(f32[2,128,128]{2,1,0:T(8,128)} %copy-done.18), channel_id=1, source_target_pairs={{1,18},{2,17},{3,20},{4,19},{5,22},{6,21},{7,24},{8,23},{9,26},{10... | collective-permute-start | bytes 393224 | tf_op jit(solution)/shard_map/ppermute | solution.py:610
  102.2 0.7 copy-start.7
  102.9 3.7 %collective-permute-start.13 = (f32[2,256,128]{2,1,0:T(8,128)}, f32[2,256,128]{2,1,0:T(8,128)}, u32[]{:S(2)}, u32[]{:S(2)}) collective-permute-start(f32[2,256,128]{2,1,0:T(8,128)} %copy-done.17), channel_id=1, source_target_pairs={{0,1},{1,0},{2,3},{3,2},{4,5},{5,4},{6,7},{7,6},{8,9},{9,8},{10,11... | collective-permute-start | bytes 786440 | tf_op jit(solution)/shard_map/ppermute | solution.py:610
  105.8 0.9 copy-start.8

commit v3 on v2

--- a/solution.py
+++ b/solution.py
@@ -16,12 +16,15 @@
 THRESHOLD = 0.3
 FLOOR = 0.5
 
-AXES = ("row", "pair", "core")
-CHIPS = ("row", "pair")
+ROW = ("z", "xh")
+COL = ("y", "xl", "core")
+AXES = ROW + COL
+CHIPS = ROW + COL[:2]
 LANES = 128
 PATCHES = 4
+DEVICES = 128
 TILE = 8
-VMEM_LIMIT = 28 * 1024 * 1024
+MIB = 1024 * 1024
 
 
 def split_table(table):
@@ -43,8 +46,9 @@
     return (
         np.concatenate([left_high, left_high, left_low], axis=1),
         np.concatenate([right_high, right_high, right_low], axis=0),
-        np.repeat(twiddle[:, :, None], LANES, axis=2),
-        np.repeat(twiddle[:, None, :], half, axis=1),
+        np.concatenate(
+            [np.repeat(twiddle[:, :, None], LANES, axis=2), np.repeat(twiddle[:, None, :], half, axis=1)]
+        ),
     )
 
 
@@ -158,11 +162,11 @@
     vmem = pl.BlockSpec(memory_space=pltpu.VMEM)
     return pl.pallas_call(
         amplitude_kernel,
-        out_shape=pltpu.VMEM((slots, 4, half, half), jnp.float32),
+        out_shape=jax.ShapeDtypeStruct((slots, 4, half, half), jnp.float32),
         in_specs=[vmem, vmem],
         out_specs=vmem,
         scratch_shapes=[pltpu.VMEM((slots, 2, size, half), jnp.float32)],
-        compiler_params=pltpu.CompilerParams(vmem_limit_bytes=VMEM_LIMIT),
+        compiler_params=pltpu.CompilerParams(vmem_limit_bytes=8 * MIB),
         cost_estimate=pl.CostEstimate(
             flops=2 * slots * size**3 * 3, bytes_accessed=8 * slots * size**2, transcendentals=0
         ),
@@ -174,7 +178,8 @@
     counts,
     rows,
     cols,
-    place_of,
+    core_of,
+    odd_of,
     centre,
     top,
     bottom,
@@ -187,8 +192,7 @@
     amplitude,
     left_table,
     right_table,
-    row_table,
-    lane_table,
+    twiddle_table,
     inner_out,
     first_out,
     second_out,
@@ -207,7 +211,7 @@
     margin = size // 2
     height, width = centre.shape[1:]
     inner = pl.ds(margin, width)
-    core, odd = place_of[0], place_of[1]
+    core, odd = core_of[0], odd_of[0]
     near = pl.ds(pl.multiple_of((1 - core) * (margin + width), LANES), margin)
     far = pl.ds(pl.multiple_of(core * (margin + width), LANES), margin)
     first = pl.ds(pl.multiple_of((1 - odd) * (margin + height), margin), margin)
@@ -243,8 +247,8 @@
     tables = (
         left_table,
         right_table,
-        (row_table[0], row_table[1]),
-        (lane_table[0], lane_table[1]),
+        (twiddle_table[0], twiddle_table[1]),
+        (twiddle_table[2], twiddle_table[3]),
     )
 
     def place(slot):
@@ -337,18 +341,23 @@
     def _():
         some_patches([count - 1])
 
+    gradient[:, middle, inner] = (
+        extended[:, middle, inner] - STEP_OBJECT * gradient[:, middle, inner]
+    )
+    inner_copy = pltpu.make_async_copy(gradient.at[:, middle, inner], inner_out, sems.at[0])
+    inner_copy.start()
     given_out[:, :margin] = gradient[:, first, near]
     given_out[:, margin : 2 * margin] = gradient[:, second, near]
     for part in range(2):
         given_out[part, 2 * margin :] = probe_sum[part, 1 - core]
         probe_out[part] = probe_sum[part, core]
-    inner_out[...] = gradient[:, middle, inner]
     first_out[...] = gradient[:, first, inner]
     second_out[...] = gradient[:, second, inner]
     near_mid_out[...] = gradient[:, middle, near]
     far_mid_out[...] = gradient[:, middle, far]
     far_top_out[...] = gradient[:, head, far]
     far_bottom_out[...] = gradient[:, tail, far]
+    inner_copy.wait()
 
 
 def patches(counts, rows, cols, place_of, pieces, probe, amplitude):
@@ -372,22 +381,22 @@
     ]
     return pl.pallas_call(
         patch_kernel,
-        out_shape=tuple(pltpu.VMEM((2,) + shape, jnp.float32) for shape in shapes),
-        in_specs=[smem] * 4 + [anywhere] * 8 + [vmem] * 6,
-        out_specs=[vmem] * 9,
+        out_shape=tuple(jax.ShapeDtypeStruct((2,) + shape, jnp.float32) for shape in shapes),
+        in_specs=[smem] * 5 + [anywhere] * 8 + [vmem] * 5,
+        out_specs=[anywhere] + [vmem] * 8,
         scratch_shapes=[
             pltpu.VMEM((2, tall, wide), jnp.float32),
             pltpu.VMEM((2, tall, wide), jnp.float32),
             pltpu.VMEM((2, size // LANES, size, LANES), jnp.float32),
             pltpu.SemaphoreType.DMA((9,)),
         ],
-        compiler_params=pltpu.CompilerParams(vmem_limit_bytes=VMEM_LIMIT),
+        compiler_params=pltpu.CompilerParams(vmem_limit_bytes=28 * MIB),
         name="patches",
     )(
         counts,
         rows,
         cols,
-        place_of,
+        *place_of,
         *pieces,
         probe,
         amplitude,
@@ -396,8 +405,8 @@
 
 
 def haar_kernel(
-    place_of,
-    centre,
+    core_of,
+    odd_of,
     inner,
     first,
     second,
@@ -408,9 +417,9 @@
     out,
     *scratch,
 ):
-    height, width = centre.shape[1:]
+    height, width = inner.shape[1:]
     margin = first.shape[1]
-    core, odd = place_of[0], place_of[1]
+    core, odd = core_of[0], odd_of[0]
     levels = [scratch[level] for level in range(LEVELS)]
     details = [scratch[LEVELS + level] for level in range(LEVELS - 1)]
     columns = width // LANES
@@ -422,7 +431,7 @@
     for part in range(2):
         for column in range(columns):
             piece = part, slice(None), pl.ds(column * LANES, LANES)
-            work[part, column] = centre[piece] - STEP_OBJECT * inner[piece]
+            work[part, column] = inner[piece]
             work[part, column, first_rows] -= STEP_OBJECT * first[piece]
             work[part, column, second_rows] -= STEP_OBJECT * second[piece]
         work[part, near] -= STEP_OBJECT * near_mid[part]
@@ -525,18 +534,18 @@
     return pl.pallas_call(
         haar_kernel,
         out_shape=jax.ShapeDtypeStruct(shape, jnp.float32),
-        in_specs=[smem] + [vmem] * len(pieces),
+        in_specs=[smem] * 2 + [vmem] * len(pieces),
         out_specs=vmem,
         scratch_shapes=[pltpu.VMEM(size, jnp.float32) for size in sizes + sizes[1:]],
-        compiler_params=pltpu.CompilerParams(vmem_limit_bytes=VMEM_LIMIT),
+        compiler_params=pltpu.CompilerParams(vmem_limit_bytes=16 * MIB),
         name="haar",
-    )(place_of, *pieces)
-
-
-def join_kernel(place_of, first, second, given, kept, first_out, second_out, shares):
+    )(*place_of, *pieces)
+
+
+def join_kernel(core_of, first, second, given, kept, first_out, second_out, shares):
     margin = first.shape[1]
     width = first.shape[2]
-    near = pl.ds(pl.multiple_of((1 - place_of[0]) * (width - LANES), LANES), LANES)
+    near = pl.ds(pl.multiple_of((1 - core_of[0]) * (width - LANES), LANES), LANES)
     first_out[...] = first[...]
     second_out[...] = second[...]
     first_out[:, :, near] += given[:, :margin]
@@ -544,48 +553,51 @@
     shares[...] = (kept[...] + given[:, 2 * margin :]).reshape(shares.shape)
 
 
-def joined(place_of, first, second, given, kept):
+def joined(core_of, first, second, given, kept, parts):
     smem = pl.BlockSpec(memory_space=pltpu.SMEM)
     vmem = pl.BlockSpec(memory_space=pltpu.VMEM)
-    shapes = [first.shape, second.shape, (kept.size // (TILE * LANES), TILE, LANES)]
+    shapes = [first.shape, second.shape, (parts, kept.size // (parts * LANES), LANES)]
     return pl.pallas_call(
         join_kernel,
         out_shape=tuple(jax.ShapeDtypeStruct(shape, jnp.float32) for shape in shapes),
         in_specs=[smem] + [vmem] * 4,
         out_specs=[vmem] * 3,
-        compiler_params=pltpu.CompilerParams(vmem_limit_bytes=VMEM_LIMIT),
+        compiler_params=pltpu.CompilerParams(vmem_limit_bytes=8 * MIB),
         name="joined",
-    )(place_of, first, second, given, kept)
-
-
-def total_kernel(shares, tile, out):
-    total = shares[0]
-    for index in range(1, shares.shape[0]):
-        total = total + shares[index]
-    total = tile[...] - total * (PROBE_STEP / (PATCHES * out.shape[0]))
-    for index in range(out.shape[0]):
-        out[index] = total
-
-
-def new_tiles(shares, tile, devices):
+    )(core_of, first, second, given, kept)
+
+
+def added(parts):
+    total = parts[0]
+    for index in range(1, parts.shape[0]):
+        total = total + parts[index]
+    return total
+
+
+def tile_kernel(parts, tile, out):
+    scale = PROBE_STEP / (PATCHES * DEVICES)
+    out[...] = jnp.broadcast_to((tile[...] - scale * added(parts))[None], out.shape)
+
+
+def summed(parts, copies, tile):
     vmem = pl.BlockSpec(memory_space=pltpu.VMEM)
     return pl.pallas_call(
-        total_kernel,
-        out_shape=jax.ShapeDtypeStruct((devices,) + tile.shape, jnp.float32),
+        tile_kernel,
+        out_shape=jax.ShapeDtypeStruct((copies,) + parts.shape[1:], jnp.float32),
         in_specs=[vmem] * 2,
         out_specs=vmem,
-        compiler_params=pltpu.CompilerParams(vmem_limit_bytes=VMEM_LIMIT),
-        name="new_tiles",
-    )(shares, tile)
+        compiler_params=pltpu.CompilerParams(vmem_limit_bytes=4 * MIB),
+        name="summed",
+    )(parts, tile)
 
 
 def probe_kernel(tiles, out):
-    size = out.shape[1]
-    chips = size // TILE
+    rows = tiles.shape[2]
+    chunks = out.shape[1] // rows
     for part in range(2):
         for half in range(2):
-            value = tiles[pl.ds(part * chips, chips), half]
-            out[part, :, pl.ds(half * LANES, LANES)] = value.reshape(size, LANES)
+            value = tiles[pl.ds(part * chunks, chunks), half]
+            out[part, :, pl.ds(half * LANES, LANES)] = value.reshape(out.shape[1], LANES)
 
 
 def laid_out(tiles, shape):
@@ -595,13 +607,13 @@
         out_shape=jax.ShapeDtypeStruct(shape, jnp.float32),
         in_specs=[vmem],
         out_specs=vmem,
-        compiler_params=pltpu.CompilerParams(vmem_limit_bytes=VMEM_LIMIT),
+        compiler_params=pltpu.CompilerParams(vmem_limit_bytes=4 * MIB),
         name="laid_out",
     )(tiles)
 
 
 def permuted(value, move):
-    rows, cols = lax.axis_size("row"), lax.axis_size(AXES[1:])
+    rows, cols = lax.axis_size(ROW), lax.axis_size(COL)
     pairs = []
     for source in range(rows * cols):
         row, col = move(source // cols, source % cols)
@@ -622,10 +634,6 @@
     return lambda row, col: (row + step, col - 1 if col % 2 == 0 else col + 1)
 
 
-def chip_tiles(half):
-    return half.reshape(lax.axis_size(CHIPS), -1, LANES)
-
-
 def pair_to(first):
     return lambda row, col: (row + (1 if (row % 2 == 0) == first else -1), col)
 
@@ -636,8 +644,7 @@
     height, width = centre.shape[1:]
     slots = amplitudes.shape[2]
     core = lax.axis_index("core")
-    odd = lax.axis_index("row") % 2
-    place_of = jnp.stack([core, odd])
+    place_of = core.reshape(1), lax.axis_index("xh").reshape(1)
 
     def sides(value):
         first, last = value[:, :, :margin], value[:, :, width - margin :]
@@ -679,7 +686,9 @@
         ordered_amplitude(amplitudes[0, 0]),
     )
     given = permuted(given, near_to)
-    first, second, shares = joined(place_of, first, second, given, probe_kept)
+    first, second, shares = joined(
+        place_of[0], first, second, given, probe_kept, lax.axis_size(CHIPS)
+    )
     first, second, far_top, far_bottom, far_mid, near_mid, shares = lax.optimization_barrier(
         (first, second, far_top, far_bottom, far_mid, near_mid, shares)
     )
@@ -688,38 +697,38 @@
     second = permuted(second, pair_to(False))
     far_below = permuted(far_top, far_to(-1))
     far_above = permuted(far_bottom, far_to(1))
+    far_mid, far_below, far_above = lax.optimization_barrier((far_mid, far_below, far_above))
     far_mid = permuted(far_mid, far_to(0))
-    near_mid, first, second, far_below, far_above, far_mid = lax.optimization_barrier(
-        (near_mid, first, second, far_below, far_above, far_mid)
+    near_mid, first, second, far_mid = lax.optimization_barrier(
+        (near_mid, first, second, far_mid)
     )
     near_mid = permuted(near_mid, near_to)
     shares = lax.all_to_all(shares, CHIPS, 0, 0, tiled=True)
     columns = [probe[:, :, LANES * index : LANES * (index + 1)] for index in range(2)]
-    tile = lax.dynamic_index_in_dim(
-        chip_tiles(jnp.where(core == 0, *columns)), lax.axis_index(CHIPS), keepdims=False
-    )
-    tiles = new_tiles(shares, tile, lax.axis_size(AXES))
+    tile = jnp.where(core == 0, *columns).reshape(shares.shape)
+    tile = lax.dynamic_index_in_dim(tile, lax.axis_index(CHIPS), keepdims=False)
+    tiles = summed(shares, lax.axis_size(AXES), tile)
     tiles = lax.all_to_all(tiles, AXES, 0, 0, tiled=True)
-    probe_new = laid_out(tiles.reshape(-1, 2, TILE, LANES), probe.shape)
     object_new = shrink_object(
-        place_of, centre, inner, first, second, near_mid, far_mid, far_above, far_below
-    )
+        place_of, inner, first, second, near_mid, far_mid, far_above, far_below
+    )
+    object_new, tiles = lax.optimization_barrier((object_new, tiles))
+    probe_new = laid_out(tiles.reshape((-1, 2) + tile.shape), probe.shape)
     return object_new, probe_new
 
 
 def solution(mesh):
-    fine = jax.sharding.Mesh(mesh.devices.reshape(mesh.devices.shape[0], -1, 2), AXES)
-    col = AXES[1:]
+    fine = jax.sharding.Mesh(mesh.devices.reshape(4, 2, 4, 2, 2), AXES)
     in_specs = (
-        P(None, "row", col),
-        P(None, "row", col),
+        P(None, ROW, COL),
+        P(None, ROW, COL),
         P(),
-        P("row", col, None, None, None),
-        P("row", col, None),
-        P("row", col, None),
-        P("row", col),
-    )
-    out_specs = (P(None, "row", col), P())
+        P(ROW, COL, None, None, None),
+        P(ROW, COL, None),
+        P(ROW, COL, None),
+        P(ROW, COL),
+    )
+    out_specs = (P(None, ROW, COL), P())
     return jax.shard_map(
         on_device, mesh=fine, in_specs=in_specs, out_specs=out_specs, check_vma=False
     )

time: 112 us -> 111 us (level)
  Pallas kernels: 18.5 us -> 12.5 us
  starting transfers between devices: 52.2 us -> 56.4 us
  waiting for transfers between devices: 30.1 us -> 31.4 us
    all_to_all x1, waiting for transfers between devices: 2.88 us -> 9.23 us  [on_device(): tiles = lax.all_to_all(tiles, AXES, 0, 0, tiled=True)]
    ppermute x14, waiting for transfers between devices: 21.8 us -> 16.1 us  [permuted(): return lax.ppermute(value, AXES, pairs)]
    ppermute x14, starting transfers between devices: 32.5 us -> 38.1 us  [permuted(): return lax.ppermute(value, AXES, pairs)]
    pallas_call x3, Pallas kernels: 11.1 us -> 6.85 us  [the longest x1 5.26 us: patches(): pl.pallas_call(patch_kernel, out_shape=tuple((jax.ShapeDtypeStruct((2,) +...]
    all_to_all x1, starting transfers between devices: 9.46 us -> 6.97 us  [on_device(): tiles = lax.all_to_all(tiles, AXES, 0, 0, tiled=True)]
    pallas_call x1, Pallas kernels: 5.07 us -> 3.8 us  [shrink_object(): pl.pallas_call(haar_kernel, out_shape=jax.ShapeDtypeStruct(shape, jnp.flo...]
    unnamed x40 -> x36, local copies, waits for them, and re-layouts: 5.07 us -> 4.33 us
  transfers between devices with their start and end apart: 16 -> 16, of which waited for: 7 -> 6; matrix products, arithmetic and copies ran while one was open for 1% -> 1% of each run, Pallas kernels for 2% -> 5%
where the time goes in v3:
time: 111 us
  starting transfers between devices  56.4 us (51%)
  waiting for transfers between devices  31.4 us (28%)
  Pallas kernels  12.5 us (11%)
  local copies, waits for them, and re-layouts  5.39 us (5%)
  other arithmetic  3.31 us (3%)
  between operations  1.61 us (1%)
    ppermute x14, starting transfers between devices, permuted(): return lax.ppermute(value, AXES, pairs)  38.1 us
    ppermute x14, waiting for transfers between devices, permuted(): return lax.ppermute(value, AXES, pairs)  16.1 us
    all_to_all x1, starting transfers between devices, on_device(): shares = lax.all_to_all(shares, CHIPS, 0, 0, tiled=True)  11.4 us
    all_to_all x1, waiting for transfers between devices, on_device(): tiles = lax.all_to_all(tiles, AXES, 0, 0, tiled=True)  9.23 us
    all_to_all x1, starting transfers between devices, on_device(): tiles = lax.all_to_all(tiles, AXES, 0, 0, tiled=True)  6.97 us
    all_to_all x1, waiting for transfers between devices, on_device(): shares = lax.all_to_all(shares, CHIPS, 0, 0, tiled=True)  6.07 us
    pallas_call x1, Pallas kernels, patches(): pl.pallas_call(patch_kernel, out_shape=tuple((jax.ShapeDtypeStruct((2,) +...  5.26 us
    unnamed x36, local copies, waits for them, and re-layouts  4.33 us
  transfers between devices with their start and end apart: 16, of which 6 were waited for; matrix products, arithmetic and copies ran while one was open for 1% of the time, Pallas kernels for 5%

profile of v3, /device:TPU:1, one launch (start us, length us, event | category | flops | bytes accessed | tf_op | source)
XLA Modules:
  0.0 110.7 jit_solution(14795074661409103174)
XLA Ops:
  0.6 1.8 %multiply_add_fusion.centre = f32[2,256,512]{2,1,0:T(8,128)S(1)} fusion(f32[2,256,512]{2,1,0:T(8,128)} %param.11, f32[2,256,512]{2,1,0:T(8,128)} %param.12), kind=kLoop, calls=%fused_computation | loop fusion | flops 786432 | bytes 3145728 | tf_op jit(solution)/shard_map/add | solution.py:642
  2.4 1.0 fusion
  3.4 1.3 %collective-permute-start.1 = (f32[2,128,512]{2,1,0:T(8,128)}, f32[2,128,512]{2,1,0:T(8,128)S(1)}, u32[]{:S(2)}, u32[]{:S(2)}) collective-permute-start(f32[2,128,512]{2,1,0:T(8,128)} %get-tuple-element.72), channel_id=1, source_target_pairs={{16,0},{17,1},{18,2},{19,3},{20,4},{21,5},{22,6},{23,7},{24,8},{25... | collective-permute-start | bytes 1572872 | tf_op jit(solution)/shard_map/ppermute | solution.py:622
  4.7 6.1 %collective-permute-start = (f32[2,128,512]{2,1,0:T(8,128)}, f32[2,128,512]{2,1,0:T(8,128)S(1)}, u32[]{:S(2)}, u32[]{:S(2)}) collective-permute-start(f32[2,128,512]{2,1,0:T(8,128)} %get-tuple-element.73), channel_id=1, source_target_pairs={{0,16},{1,17},{2,18},{3,19},{4,20},{5,21},{6,22},{7,23},{8,24},{9,... | collective-permute-start | bytes 1572872 | tf_op jit(solution)/shard_map/ppermute | solution.py:622
  10.9 0.7 slice_select_fusion.1
  11.6 4.4 %collective-permute-start.5 = (f32[2,256,128]{2,1,0:T(8,128)S(1)}, f32[2,256,128]{2,1,0:T(8,128)S(1)}, u32[]{:S(2)}, u32[]{:S(2)}) collective-permute-start(f32[2,256,128]{2,1,0:T(8,128)S(1)} %get-tuple-element.70), channel_id=1, source_target_pairs={{1,2},{2,1},{3,4},{4,3},{5,6},{6,5},{7,8},{8,7},{9,10},{10,9},{11,... | collective-permute-start | bytes 786440 | tf_op jit(solution)/shard_map/ppermute | solution.py:622
  16.1 4.1 %collective-permute-start.3 = (f32[2,128,128]{2,1,0:T(8,128)S(1)}, f32[2,128,128]{2,1,0:T(8,128)S(1)}, u32[]{:S(2)}, u32[]{:S(2)}) collective-permute-start(f32[2,128,128]{2,1,0:T(8,128)S(1)} %get-tuple-element.75), channel_id=1, source_target_pairs={{1,18},{2,17},{3,20},{4,19},{5,22},{6,21},{7,24},{8,23},{9,26},{10... | collective-permute-start | bytes 393224 | tf_op jit(solution)/shard_map/ppermute | solution.py:622
  20.2 1.3 %collective-permute-start.4 = (f32[2,128,128]{2,1,0:T(8,128)S(1)}, f32[2,128,128]{2,1,0:T(8,128)S(1)}, u32[]{:S(2)}, u32[]{:S(2)}) collective-permute-start(f32[2,128,128]{2,1,0:T(8,128)S(1)} %get-tuple-element.74), channel_id=1, source_target_pairs={{17,2},{18,1},{19,4},{20,3},{21,6},{22,5},{23,8},{24,7},{25,10},{2... | collective-permute-start | bytes 393224 | tf_op jit(solution)/shard_map/ppermute | solution.py:622
  21.5 0.0 collective-permute-done.1.bottom
  21.5 1.8 %collective-permute-start.2 = (f32[2,256,128]{2,1,0:T(8,128)}, f32[2,256,128]{2,1,0:T(8,128)S(1)}, u32[]{:S(2)}, u32[]{:S(2)}) collective-permute-start(f32[2,256,128]{2,1,0:T(8,128)} %get-tuple-element.71), channel_id=1, source_target_pairs={{0,1},{1,0},{2,3},{3,2},{4,5},{5,4},{6,7},{7,6},{8,9},{9,8},{10,11... | collective-permute-start | bytes 786440 | tf_op jit(solution)/shard_map/ppermute | solution.py:622
  23.3 0.0 copy-start.4
  23.3 0.0 collective-permute-done.top
  23.4 0.7 pad_maximum_fusion
  24.1 1.0 collective-permute-done.3.far_top
  25.1 0.7 copy-done.8
  25.7 12.4 %collective-permute-done.4.far_bottom = f32[2,128,128]{2,1,0:T(8,128)S(1)} collective-permute-done((f32[2,128,128]{2,1,0:T(8,128)S(1)}, f32[2,128,128]{2,1,0:T(8,128)S(1)}, u32[]{:S(2)}, u32[]{:S(2)}) %collective-permute-start.4) | collective-permute-done | bytes 131104 | tf_op jit(solution)/shard_map/ppermute | solution.py:622
  38.2 0.7 copy-done.10
  38.8 0.0 collective-permute-done.5.far_mid
  38.8 0.0 collective-permute-start.6
  39.5 0.0 copy-done.4
  39.5 0.0 copy-start.3
  39.5 1.2 %copy-done.3 = f32[1,1,4,256,256]{4,3,2,1,0:T(8,128)S(1)} copy-done((f32[1,1,4,256,256]{4,3,2,1,0:T(8,128)S(1)}, f32[1,1,4,256,256]{4,3,2,1,0:T(8,128)}, u32[]{:S(2)}) %copy-start.3) | copy-done | bytes 1048600
  40.7 0.0 copy-start.9
  40.7 0.0 copy-start.11
  40.8 0.7 ordered_amplitude.1.amplitude
  41.4 0.0 collective-permute-done.2.near_mid
  41.5 0.0 collective-permute-done.6.near_corner
  41.5 0.0 copy-start.12
  41.5 0.0 copy-start.13
  41.5 0.3 copy-done
  41.8 0.1 copy-done.5
  41.9 0.1 copy-done.6
  42.0 0.1 copy-done.7
  42.1 0.0 copy-done.9
  42.1 0.0 copy-done.11
  42.1 0.1 copy-done.12
  42.3 0.0 copy-done.13
  42.3 5.3 %patches.1 = (f32[2,256,512]{2,1,0:T(8,128)S(1)}, f32[2,128,512]{2,1,0:T(8,128)S(1)}, f32[2,128,512]{2,1,0:T(8,128)S(1)}, f32[2,256,128]{2,1,0:T(8,128)S(1)}, f3...) custom-call(s32[1]{0:T(128)} %bitcast.10.counts, ...), custom_call_target="tpu_custom_call" | custom-call | tf_op jit(solution)/shard_map/patches/pallas_call | solution.py:382
  47.5 0.0 copy-start.1
  47.6 1.0 copy-done.1
  48.5 0.5 collective-permute-start.7
  49.0 1.5 %collective-permute-done.7.given = f32[2,512,128]{2,1,0:T(8,128)S(1)} collective-permute-done((f32[2,512,128]{2,1,0:T(8,128)S(1)}, f32[2,512,128]{2,1,0:T(8,128)S(1)}, u32[]{:S(2)}, u32[]{:S(2)}) %collective-permute-start.7) | collective-permute-done | bytes 524320 | tf_op jit(solution)/shard_map/ppermute | solution.py:622
  50.6 1.0 joined.1
  51.6 4.8 %collective-permute-start.8 = (f32[2,128,512]{2,1,0:T(8,128)S(1)}, f32[2,128,512]{2,1,0:T(8,128)S(1)}, u32[]{:S(2)}, u32[]{:S(2)}) collective-permute-start(f32[2,128,512]{2,1,0:T(8,128)S(1)} %get-tuple-element.53), channel_id=1, source_target_pairs={{0,16},{1,17},{2,18},{3,19},{4,20},{5,21},{6,22},{7,23},{8,24},{9,... | collective-permute-start | bytes 1572872 | tf_op jit(solution)/shard_map/ppermute | solution.py:622
  56.4 1.3 %collective-permute-start.10 = (f32[2,128,128]{2,1,0:T(8,128)}, f32[2,128,128]{2,1,0:T(8,128)S(1)}, u32[]{:S(2)}, u32[]{:S(2)}) collective-permute-start(f32[2,128,128]{2,1,0:T(8,128)} %copy-done.17), channel_id=1, source_target_pairs={{17,2},{18,1},{19,4},{20,3},{21,6},{22,5},{23,8},{24,7},{25,10},{2... | collective-permute-start | bytes 393224 | tf_op jit(solution)/shard_map/ppermute | solution.py:622
  57.7 7.0 %collective-permute-start.11 = (f32[2,128,128]{2,1,0:T(8,128)}, f32[2,128,128]{2,1,0:T(8,128)S(1)}, u32[]{:S(2)}, u32[]{:S(2)}) collective-permute-start(f32[2,128,128]{2,1,0:T(8,128)} %copy-done.16), channel_id=1, source_target_pairs={{1,18},{2,17},{3,20},{4,19},{5,22},{6,21},{7,24},{8,23},{9,26},{10... | collective-permute-start | bytes 393224 | tf_op jit(solution)/shard_map/ppermute | solution.py:622
  64.7 11.4 %all-to-all-start = ((f32[64,8,128]{2,1,0:T(8,128)}), f32[64,8,128]{2,1,0:T(8,128)S(1)}, u32[]{:S(2)}, u32[]{:S(2)}) async-start(f32[64,8,128]{2,1,0:T(8,128)} %get-tuple-element.67), calls=%async_computation | async-start | bytes 524288 | tf_op jit(solution)/shard_map/all_to_all | solution.py:706
  76.1 0.0 collective-permute-done.8.first
  76.1 0.7 collective-permute-start.9
  76.8 0.0 copy-start.2
  76.9 0.0 collective-permute-done.10.far_bottom
  76.9 0.0 collective-permute-done.11.far_top
  76.9 3.4 %collective-permute-start.12 = (f32[2,256,128]{2,1,0:T(8,128)}, f32[2,256,128]{2,1,0:T(8,128)S(1)}, u32[]{:S(2)}, u32[]{:S(2)}) collective-permute-start(f32[2,256,128]{2,1,0:T(8,128)} %get-tuple-element.60), channel_id=1, source_target_pairs={{1,2},{2,1},{3,4},{4,3},{5,6},{6,5},{7,8},{8,7},{9,10},{10,9},{11,... | collective-permute-start | bytes 786440 | tf_op jit(solution)/shard_map/ppermute | solution.py:622
  80.3 6.1 %all-to-all-done.parts = f32[64,8,128]{2,1,0:T(8,128)S(1)} async-done(((f32[64,8,128]{2,1,0:T(8,128)}), f32[64,8,128]{2,1,0:T(8,128)S(1)}, u32[]{:S(2)}, u32[]{:S(2)}) %all-to-all-start) | async-done | bytes 262176 | tf_op jit(solution)/shard_map/all_to_all | solution.py:706
  86.4 0.9 summed.1
  87.3 7.0 %all-to-all-start.1 = ((f32[128,8,128]{2,1,0:T(8,128)}), f32[128,8,128]{2,1,0:T(8,128)S(1)}, u32[]{:S(2)}, u32[]{:S(2)}) async-start(f32[128,8,128]{2,1,0:T(8,128)} %summed.1), calls=%async_computation.1 | async-start | bytes 1048576 | tf_op jit(solution)/shard_map/all_to_all | solution.py:711
  94.3 0.0 collective-permute-done.12.far_mid
  94.3 0.0 collective-permute-done.9.second
  94.3 1.3 %collective-permute-start.13 = (f32[2,256,128]{2,1,0:T(8,128)S(1)}, f32[2,256,128]{2,1,0:T(8,128)S(1)}, u32[]{:S(2)}, u32[]{:S(2)}) collective-permute-start(f32[2,256,128]{2,1,0:T(8,128)S(1)} %copy-done.15), channel_id=1, source_target_pairs={{0,1},{1,0},{2,3},{3,2},{4,5},{5,4},{6,7},{7,6},{8,9},{9,8},{10,11... | collective-permute-start | bytes 786440 | tf_op jit(solution)/shard_map/ppermute | solution.py:622
  95.7 1.2 %collective-permute-done.13.near_mid = f32[2,256,128]{2,1,0:T(8,128)S(1)} collective-permute-done((f32[2,256,128]{2,1,0:T(8,128)S(1)}, f32[2,256,128]{2,1,0:T(8,128)S(1)}, u32[]{:S(2)}, u32[]{:S(2)}) %collective-permute-start.13) | collective-permute-done | bytes 262176 | tf_op jit(solution)/shard_map/ppermute | solution.py:622
  96.8 0.0 copy-done.2
  96.8 3.8 %haar.1 = f32[2,256,512]{2,1,0:T(8,128)} custom-call(s32[1]{0:T(128)} %bitcast.core_of, s32[1]{0:T(128)} %bitcast.1.odd_of, f32[2,256,512]{2,1,0:T(8,128)S(1)} %copy-done.2, f32[2,128,512]{2,1,0:T(8,128)S(1)} %collective-permute-done.8.first, f32[2,128,512]{2,1,0:T(8,128)S(1)} %collective-permute-done.9.second, ...), custom_call_target="tpu_custom_call" | custom-call | tf_op jit(solution)/shard_map/haar/pallas_call | solution.py:534
  100.6 9.2 %all-to-all-done.1 = f32[128,8,128]{2,1,0:T(8,128)S(1)} async-done(((f32[128,8,128]{2,1,0:T(8,128)}), f32[128,8,128]{2,1,0:T(8,128)S(1)}, u32[]{:S(2)}, u32[]{:S(2)}) %all-to-all-start.1) | async-done | bytes 524320 | tf_op jit(solution)/shard_map/all_to_all | solution.py:711
  109.9 0.8 laid_out.1
  (19 shorter events, 0.1 us)
Async XLA Ops:
  3.4 18.0 %collective-permute-start.1 = (f32[2,128,512]{2,1,0:T(8,128)}, f32[2,128,512]{2,1,0:T(8,128)S(1)}, u32[]{:S(2)}, u32[]{:S(2)}) collective-permute-start(f32[2,128,512]{2,1,0:T(8,128)} %get-tuple-element.72), channel_id=1, source_target_pairs={{16,0},{17,1},{18,2},{19,3},{20,4},{21,5},{22,6},{23,7},{24,8},{25... | collective-permute-start | bytes 1572872 | tf_op jit(solution)/shard_map/ppermute | solution.py:622
  4.7 18.6 %collective-permute-start = (f32[2,128,512]{2,1,0:T(8,128)}, f32[2,128,512]{2,1,0:T(8,128)S(1)}, u32[]{:S(2)}, u32[]{:S(2)}) collective-permute-start(f32[2,128,512]{2,1,0:T(8,128)} %get-tuple-element.73), channel_id=1, source_target_pairs={{0,16},{1,17},{2,18},{3,19},{4,20},{5,21},{6,22},{7,23},{8,24},{9,... | collective-permute-start | bytes 1572872 | tf_op jit(solution)/shard_map/ppermute | solution.py:622
  11.6 27.2 %collective-permute-start.5 = (f32[2,256,128]{2,1,0:T(8,128)S(1)}, f32[2,256,128]{2,1,0:T(8,128)S(1)}, u32[]{:S(2)}, u32[]{:S(2)}) collective-permute-start(f32[2,256,128]{2,1,0:T(8,128)S(1)} %get-tuple-element.70), channel_id=1, source_target_pairs={{1,2},{2,1},{3,4},{4,3},{5,6},{6,5},{7,8},{8,7},{9,10},{10,9},{11,... | collective-permute-start | bytes 786440 | tf_op jit(solution)/shard_map/ppermute | solution.py:622
  16.1 9.0 %collective-permute-start.3 = (f32[2,128,128]{2,1,0:T(8,128)S(1)}, f32[2,128,128]{2,1,0:T(8,128)S(1)}, u32[]{:S(2)}, u32[]{:S(2)}) collective-permute-start(f32[2,128,128]{2,1,0:T(8,128)S(1)} %get-tuple-element.75), channel_id=1, source_target_pairs={{1,18},{2,17},{3,20},{4,19},{5,22},{6,21},{7,24},{8,23},{9,26},{10... | collective-permute-start | bytes 393224 | tf_op jit(solution)/shard_map/ppermute | solution.py:622
  20.2 18.0 %collective-permute-start.4 = (f32[2,128,128]{2,1,0:T(8,128)S(1)}, f32[2,128,128]{2,1,0:T(8,128)S(1)}, u32[]{:S(2)}, u32[]{:S(2)}) collective-permute-start(f32[2,128,128]{2,1,0:T(8,128)S(1)} %get-tuple-element.74), channel_id=1, source_target_pairs={{17,2},{18,1},{19,4},{20,3},{21,6},{22,5},{23,8},{24,7},{25,10},{2... | collective-permute-start | bytes 393224 | tf_op jit(solution)/shard_map/ppermute | solution.py:622
  21.5 20.0 %collective-permute-start.2 = (f32[2,256,128]{2,1,0:T(8,128)}, f32[2,256,128]{2,1,0:T(8,128)S(1)}, u32[]{:S(2)}, u32[]{:S(2)}) collective-permute-start(f32[2,256,128]{2,1,0:T(8,128)} %get-tuple-element.71), channel_id=1, source_target_pairs={{0,1},{1,0},{2,3},{3,2},{4,5},{5,4},{6,7},{7,6},{8,9},{9,8},{10,11... | collective-permute-start | bytes 786440 | tf_op jit(solution)/shard_map/ppermute | solution.py:622
  23.3 16.2 %copy-start.4 = (bf16[768,256]{1,0:T(8,128)(2,1)S(1)}, bf16[768,256]{1,0:T(8,128)(2,1)}, u32[]{:S(2)}) copy-start(bf16[768,256]{1,0:T(8,128)(2,1)} %constant.42.clone.table) | copy-start | bytes 1179652
  25.1 0.7 copy-start.8
  38.2 0.7 copy-start.10
  38.8 2.6 %collective-permute-start.6 = (f32[2,256,128]{2,1,0:T(8,128)}, f32[2,256,128]{2,1,0:T(8,128)}, u32[]{:S(2)}, u32[]{:S(2)}) collective-permute-start(f32[2,256,128]{2,1,0:T(8,128)} %pad_maximum_fusion), channel_id=1, source_target_pairs={{0,1},{1,0},{2,3},{3,2},{4,5},{5,4},{6,7},{7,6},{8,9},{9,8},{10,11... | collective-permute-start | bytes 786440 | tf_op jit(solution)/shard_map/ppermute | solution.py:622
  39.5 1.2 %copy-start.3 = (f32[1,1,4,256,256]{4,3,2,1,0:T(8,128)S(1)}, f32[1,1,4,256,256]{4,3,2,1,0:T(8,128)}, u32[]{:S(2)}) copy-start(f32[1,1,4,256,256]{4,3,2,1,0:T(8,128)} %param.14) | copy-start | bytes 3145732
  40.7 1.0 copy-start
  40.7 1.2 %copy-start.5 = (bf16[256,768]{1,0:T(8,128)(2,1)S(1)}, bf16[256,768]{1,0:T(8,128)(2,1)}, u32[]{:S(2)}) copy-start(bf16[256,768]{1,0:T(8,128)(2,1)} %constant.43.clone.left_table) | copy-start | bytes 1179652
  40.7 1.3 %copy-start.6 = (bf16[768,256]{1,0:T(8,128)(2,1)S(1)}, bf16[768,256]{1,0:T(8,128)(2,1)}, u32[]{:S(2)}) copy-start(bf16[768,256]{1,0:T(8,128)(2,1)} %constant.44.clone.right_table) | copy-start | bytes 1179652
  40.7 1.3 %copy-start.7 = (f32[4,128,128]{2,1,0:T(8,128)S(1)}, f32[4,128,128]{2,1,0:T(8,128)}, u32[]{:S(2)}) copy-start(f32[4,128,128]{2,1,0:T(8,128)} %constant.45.clone.twiddle_table) | copy-start | bytes 786436
  40.7 1.4 %copy-start.9 = (f32[2,128,128]{2,1,0:T(8,128)S(1)}, f32[2,128,128]{2,1,0:T(8,128)}, u32[]{:S(2)}) copy-start(f32[2,128,128]{2,1,0:T(8,128)} %copy-done.8) | copy-start | bytes 393220
  40.7 1.4 %copy-start.11 = (f32[2,128,128]{2,1,0:T(8,128)S(1)}, f32[2,128,128]{2,1,0:T(8,128)}, u32[]{:S(2)}) copy-start(f32[2,128,128]{2,1,0:T(8,128)} %copy-done.10) | copy-start | bytes 393220
  41.5 0.8 copy-start.12
  41.5 0.8 copy-start.13
  47.5 1.0 copy-start.1
  48.5 3.1 %copy-start.14 = (f32[2,256,128]{2,1,0:T(8,128)}, f32[2,256,128]{2,1,0:T(8,128)S(1)}, u32[]{:S(2)}) copy-start(f32[2,256,128]{2,1,0:T(8,128)S(1)} %get-tuple-element.63) | copy-start | bytes 786436
  48.5 3.1 %copy-start.16 = (f32[2,128,128]{2,1,0:T(8,128)}, f32[2,128,128]{2,1,0:T(8,128)S(1)}, u32[]{:S(2)}) copy-start(f32[2,128,128]{2,1,0:T(8,128)S(1)} %get-tuple-element.59) | copy-start | bytes 393220
  48.5 3.1 %copy-start.17 = (f32[2,128,128]{2,1,0:T(8,128)}, f32[2,128,128]{2,1,0:T(8,128)S(1)}, u32[]{:S(2)}) copy-start(f32[2,128,128]{2,1,0:T(8,128)S(1)} %get-tuple-element.58) | copy-start | bytes 393220
  48.5 2.1 %collective-permute-start.7 = (f32[2,512,128]{2,1,0:T(8,128)S(1)}, f32[2,512,128]{2,1,0:T(8,128)S(1)}, u32[]{:S(2)}, u32[]{:S(2)}) collective-permute-start(f32[2,512,128]{2,1,0:T(8,128)S(1)} %get-tuple-element.43), channel_id=1, source_target_pairs={{0,1},{1,0},{2,3},{3,2},{4,5},{5,4},{6,7},{7,6},{8,9},{9,8},{10,11... | collective-permute-start | bytes 1572872 | tf_op jit(solution)/shard_map/ppermute | solution.py:622
  51.6 24.5 %collective-permute-start.8 = (f32[2,128,512]{2,1,0:T(8,128)S(1)}, f32[2,128,512]{2,1,0:T(8,128)S(1)}, u32[]{:S(2)}, u32[]{:S(2)}) collective-permute-start(f32[2,128,512]{2,1,0:T(8,128)S(1)} %get-tuple-element.53), channel_id=1, source_target_pairs={{0,16},{1,17},{2,18},{3,19},{4,20},{5,21},{6,22},{7,23},{8,24},{9,... | collective-permute-start | bytes 1572872 | tf_op jit(solution)/shard_map/ppermute | solution.py:622
  56.4 20.4 %collective-permute-start.10 = (f32[2,128,128]{2,1,0:T(8,128)}, f32[2,128,128]{2,1,0:T(8,128)S(1)}, u32[]{:S(2)}, u32[]{:S(2)}) collective-permute-start(f32[2,128,128]{2,1,0:T(8,128)} %copy-done.17), channel_id=1, source_target_pairs={{17,2},{18,1},{19,4},{20,3},{21,6},{22,5},{23,8},{24,7},{25,10},{2... | collective-permute-start | bytes 393224 | tf_op jit(solution)/shard_map/ppermute | solution.py:622
  57.7 19.2 %collective-permute-start.11 = (f32[2,128,128]{2,1,0:T(8,128)}, f32[2,128,128]{2,1,0:T(8,128)S(1)}, u32[]{:S(2)}, u32[]{:S(2)}) collective-permute-start(f32[2,128,128]{2,1,0:T(8,128)} %copy-done.16), channel_id=1, source_target_pairs={{1,18},{2,17},{3,20},{4,19},{5,22},{6,21},{7,24},{8,23},{9,26},{10... | collective-permute-start | bytes 393224 | tf_op jit(solution)/shard_map/ppermute | solution.py:622
  64.7 21.7 %all-to-all-start = ((f32[64,8,128]{2,1,0:T(8,128)}), f32[64,8,128]{2,1,0:T(8,128)S(1)}, u32[]{:S(2)}, u32[]{:S(2)}) async-start(f32[64,8,128]{2,1,0:T(8,128)} %get-tuple-element.67), calls=%async_computation | async-start | bytes 524288 | tf_op jit(solution)/shard_map/all_to_all | solution.py:706
  76.1 18.2 %collective-permute-start.9 = (f32[2,128,512]{2,1,0:T(8,128)}, f32[2,128,512]{2,1,0:T(8,128)S(1)}, u32[]{:S(2)}, u32[]{:S(2)}) collective-permute-start(f32[2,128,512]{2,1,0:T(8,128)} %get-tuple-element.56), channel_id=1, source_target_pairs={{16,32},{17,33},{18,34},{19,35},{20,36},{21,37},{22,38},{23,39},{2... | collective-permute-start | bytes 1572872 | tf_op jit(solution)/shard_map/ppermute | solution.py:622
  76.8 20.0 %copy-start.2 = (f32[2,256,512]{2,1,0:T(8,128)S(1)}, f32[2,256,512]{2,1,0:T(8,128)}, u32[]{:S(2)}) copy-start(f32[2,256,512]{2,1,0:T(8,128)} %copy-done.1) | copy-start | bytes 3145732
  76.9 17.4 %collective-permute-start.12 = (f32[2,256,128]{2,1,0:T(8,128)}, f32[2,256,128]{2,1,0:T(8,128)S(1)}, u32[]{:S(2)}, u32[]{:S(2)}) collective-permute-start(f32[2,256,128]{2,1,0:T(8,128)} %get-tuple-element.60), channel_id=1, source_target_pairs={{1,2},{2,1},{3,4},{4,3},{5,6},{6,5},{7,8},{8,7},{9,10},{10,9},{11,... | collective-permute-start | bytes 786440 | tf_op jit(solution)/shard_map/ppermute | solution.py:622
  87.3 7.0 %copy-start.15 = (f32[2,256,128]{2,1,0:T(8,128)S(1)}, f32[2,256,128]{2,1,0:T(8,128)}, u32[]{:S(2)}) copy-start(f32[2,256,128]{2,1,0:T(8,128)} %copy-done.14) | copy-start | bytes 786436
  87.3 22.5 %all-to-all-start.1 = ((f32[128,8,128]{2,1,0:T(8,128)}), f32[128,8,128]{2,1,0:T(8,128)S(1)}, u32[]{:S(2)}, u32[]{:S(2)}) async-start(f32[128,8,128]{2,1,0:T(8,128)} %summed.1), calls=%async_computation.1 | async-start | bytes 1048576 | tf_op jit(solution)/shard_map/all_to_all | solution.py:711
  94.3 2.5 %collective-permute-start.13 = (f32[2,256,128]{2,1,0:T(8,128)S(1)}, f32[2,256,128]{2,1,0:T(8,128)S(1)}, u32[]{:S(2)}, u32[]{:S(2)}) collective-permute-start(f32[2,256,128]{2,1,0:T(8,128)S(1)} %copy-done.15), channel_id=1, source_target_pairs={{0,1},{1,0},{2,3},{3,2},{4,5},{5,4},{6,7},{7,6},{8,9},{9,8},{10,11... | collective-permute-start | bytes 786440 | tf_op jit(solution)/shard_map/ppermute | solution.py:622

commit v4 on v3

--- a/solution.py
+++ b/solution.py
@@ -133,45 +133,31 @@
     )
 
 
-def amplitude_kernel(amplitude, table, out, sorted_lanes):
-    slots, size, _ = amplitude.shape
-    half = size // 2
-    for slot in range(slots):
-        value = amplitude[slot]
-        high = value.astype(jnp.bfloat16)
-        rest = value - high.astype(jnp.float32)
-        middle, low = split_value(rest)
-        ordered = jnp.dot(
-            jnp.concatenate([high, middle, low], axis=1),
-            table[...],
-            preferred_element_type=jnp.float32,
-        )
-        for index in range(2):
-            sorted_lanes[slot, index] = ordered[:, index * half : (index + 1) * half]
-            for parity in range(2):
-                out[slot, 2 * parity + index] = sorted_lanes[slot, index, pl.ds(parity, half, stride=2), :]
-
-
-def ordered_amplitude(amplitude):
-    slots, size, _ = amplitude.shape
+def order_table(size):
     half = size // 2
     table = np.zeros((size, size), np.float32)
     table[2 * np.arange(half), np.arange(half)] = 1
     table[2 * np.arange(half) + 1, half + np.arange(half)] = 1
-    table = np.concatenate([table] * 3, axis=0).astype(ml_dtypes.bfloat16)
-    vmem = pl.BlockSpec(memory_space=pltpu.VMEM)
-    return pl.pallas_call(
-        amplitude_kernel,
-        out_shape=jax.ShapeDtypeStruct((slots, 4, half, half), jnp.float32),
-        in_specs=[vmem, vmem],
-        out_specs=vmem,
-        scratch_shapes=[pltpu.VMEM((slots, 2, size, half), jnp.float32)],
-        compiler_params=pltpu.CompilerParams(vmem_limit_bytes=8 * MIB),
-        cost_estimate=pl.CostEstimate(
-            flops=2 * slots * size**3 * 3, bytes_accessed=8 * slots * size**2, transcendentals=0
-        ),
-        name="ordered_amplitude",
-    )(amplitude, jnp.asarray(table))
+    return np.concatenate([table] * 3, axis=0).astype(ml_dtypes.bfloat16)
+
+
+def order_amplitude(slot, amplitude, table, sorted_lanes, ordered):
+    size = amplitude.shape[1]
+    half = size // 2
+    value = amplitude[slot]
+    high = value.astype(jnp.bfloat16)
+    middle, low = split_value(value - high.astype(jnp.float32))
+    turned = jnp.dot(
+        jnp.concatenate([high, middle, low], axis=1),
+        table[...],
+        preferred_element_type=jnp.float32,
+    )
+    for index in range(2):
+        sorted_lanes[index] = turned[:, index * half : (index + 1) * half]
+        for parity in range(2):
+            ordered[slot, 2 * parity + index] = sorted_lanes[
+                index, pl.ds(parity, half, stride=2), :
+            ]
 
 
 def patch_kernel(
@@ -188,8 +174,9 @@
     near_corner,
     far_top,
     far_bottom,
+    amplitude_in,
     probe,
-    amplitude,
+    order,
     left_table,
     right_table,
     twiddle_table,
@@ -205,6 +192,9 @@
     extended,
     gradient,
     probe_sum,
+    measured,
+    sorted_lanes,
+    amplitude,
     sems,
 ):
     size = probe.shape[1]
@@ -232,10 +222,19 @@
         pltpu.make_async_copy(source, target, sems.at[index])
         for index, (source, target) in enumerate(moves)
     ]
+    measured_copy = pltpu.make_async_copy(amplitude_in, measured, sems.at[len(moves)])
+    measured_copy.start()
     for copy in copies:
         copy.start()
     gradient[...] = jnp.zeros_like(gradient)
     probe_sum[...] = jnp.zeros_like(probe_sum)
+    measured_copy.wait()
+
+    def order_slot(slot, carry):
+        order_amplitude(slot, measured, order, sorted_lanes, amplitude)
+        return carry
+
+    lax.fori_loop(0, counts[0], order_slot, 0)
     for copy in copies:
         copy.wait()
     tile = (1, TILE, LANES)
@@ -381,14 +380,18 @@
     ]
     return pl.pallas_call(
         patch_kernel,
-        out_shape=tuple(jax.ShapeDtypeStruct((2,) + shape, jnp.float32) for shape in shapes),
-        in_specs=[smem] * 5 + [anywhere] * 8 + [vmem] * 5,
+        out_shape=(pltpu.HBM((2,) + shapes[0], jnp.float32),)
+        + tuple(jax.ShapeDtypeStruct((2,) + shape, jnp.float32) for shape in shapes[1:]),
+        in_specs=[smem] * 5 + [anywhere] * 9 + [vmem] * 5,
         out_specs=[anywhere] + [vmem] * 8,
         scratch_shapes=[
             pltpu.VMEM((2, tall, wide), jnp.float32),
             pltpu.VMEM((2, tall, wide), jnp.float32),
             pltpu.VMEM((2, size // LANES, size, LANES), jnp.float32),
-            pltpu.SemaphoreType.DMA((9,)),
+            pltpu.VMEM(amplitude.shape, jnp.float32),
+            pltpu.VMEM((2, size, size // 2), jnp.float32),
+            pltpu.VMEM((amplitude.shape[0], 4, size // 2, size // 2), jnp.float32),
+            pltpu.SemaphoreType.DMA((10,)),
         ],
         compiler_params=pltpu.CompilerParams(vmem_limit_bytes=28 * MIB),
         name="patches",
@@ -398,8 +401,9 @@
         cols,
         *place_of,
         *pieces,
+        amplitude,
         probe,
-        amplitude,
+        jnp.asarray(order_table(size)),
         *(jnp.asarray(table) for table in dft_tables(size)),
     )
 
@@ -683,7 +687,7 @@
         place_of,
         (centre, top, bottom, near_mid, far_mid, near_corner, far_top, far_bottom),
         probe,
-        ordered_amplitude(amplitudes[0, 0]),
+        amplitudes[0, 0],
     )
     given = permuted(given, near_to)
     first, second, shares = joined(

time: 111 us -> 116 us (1.045)
  local copies, waits for them, and re-layouts: 5.39 us -> 7.99 us
  starting transfers between devices: 56.4 us -> 57.9 us
    unnamed x36 -> x34, local copies, waits for them, and re-layouts: 4.33 us -> 7.07 us
    ppermute x14, waiting for transfers between devices: 16.1 us -> 18.2 us  [permuted(): return lax.ppermute(value, AXES, pairs)]
    all_to_all x1, waiting for transfers between devices: 6.07 us -> 4.43 us  [on_device(): shares = lax.all_to_all(shares, CHIPS, 0, 0, tiled=True)]
    pallas_call x2 -> x1, Pallas kernels: 5.95 us -> 6 us  [patches(): pl.pallas_call(patch_kernel, out_shape=(pltpu.HBM((2,) + shapes[0], jnp.f...]
  transfers between devices with their start and end apart: 16 -> 16, of which waited for: 6 -> 7; matrix products, arithmetic and copies ran while one was open for 1% -> 1% of each run, Pallas kernels for 5% -> 4%
where the time goes in v4:
time: 116 us
  starting transfers between devices  57.9 us (50%)
  waiting for transfers between devices  32.2 us (28%)
  Pallas kernels  12.5 us (11%)
  local copies, waits for them, and re-layouts  7.99 us (7%)
  other arithmetic  3.3 us (3%)
  between operations  1.58 us (1%)
    ppermute x14, starting transfers between devices, permuted(): return lax.ppermute(value, AXES, pairs)  39 us
    ppermute x14, waiting for transfers between devices, permuted(): return lax.ppermute(value, AXES, pairs)  18.2 us
    all_to_all x1, starting transfers between devices, on_device(): shares = lax.all_to_all(shares, CHIPS, 0, 0, tiled=True)  11.4 us
    all_to_all x1, waiting for transfers between devices, on_device(): tiles = lax.all_to_all(tiles, AXES, 0, 0, tiled=True)  9.56 us
    all_to_all x1, starting transfers between devices, on_device(): tiles = lax.all_to_all(tiles, AXES, 0, 0, tiled=True)  7.57 us
    unnamed x34, local copies, waits for them, and re-layouts  7.07 us
    pallas_call x1, Pallas kernels, patches(): pl.pallas_call(patch_kernel, out_shape=(pltpu.HBM((2,) + shapes[0], jnp.f...  6 us
    all_to_all x1, waiting for transfers between devices, on_device(): shares = lax.all_to_all(shares, CHIPS, 0, 0, tiled=True)  4.43 us
  transfers between devices with their start and end apart: 16, of which 7 were waited for; matrix products, arithmetic and copies ran while one was open for 1% of the time, Pallas kernels for 4%

profile of v4, /device:TPU:1, one launch (start us, length us, event | category | flops | bytes accessed | tf_op | source)
XLA Modules:
  0.0 115.6 jit_solution(1696191769896444324)
XLA Ops:
  0.6 1.8 %multiply_add_fusion.centre = f32[2,256,512]{2,1,0:T(8,128)S(1)} fusion(f32[2,256,512]{2,1,0:T(8,128)} %param.11, f32[2,256,512]{2,1,0:T(8,128)} %param.12), kind=kLoop, calls=%fused_computation | loop fusion | flops 786432 | bytes 3145728 | tf_op jit(solution)/shard_map/add | solution.py:646
  2.4 0.9 fusion
  3.3 1.3 %collective-permute-start.1 = (f32[2,128,512]{2,1,0:T(8,128)S(1)}, f32[2,128,512]{2,1,0:T(8,128)S(1)}, u32[]{:S(2)}, u32[]{:S(2)}) collective-permute-start(f32[2,128,512]{2,1,0:T(8,128)S(1)} %get-tuple-element.72), channel_id=1, source_target_pairs={{16,0},{17,1},{18,2},{19,3},{20,4},{21,5},{22,6},{23,7},{24,8},{25... | collective-permute-start | bytes 1572872 | tf_op jit(solution)/shard_map/ppermute | solution.py:626
  4.6 6.1 %collective-permute-start = (f32[2,128,512]{2,1,0:T(8,128)}, f32[2,128,512]{2,1,0:T(8,128)S(1)}, u32[]{:S(2)}, u32[]{:S(2)}) collective-permute-start(f32[2,128,512]{2,1,0:T(8,128)} %get-tuple-element.73), channel_id=1, source_target_pairs={{0,16},{1,17},{2,18},{3,19},{4,20},{5,21},{6,22},{7,23},{8,24},{9,... | collective-permute-start | bytes 1572872 | tf_op jit(solution)/shard_map/ppermute | solution.py:626
  10.7 0.7 slice_select_fusion.1
  11.5 4.4 %collective-permute-start.5 = (f32[2,256,128]{2,1,0:T(8,128)S(1)}, f32[2,256,128]{2,1,0:T(8,128)S(1)}, u32[]{:S(2)}, u32[]{:S(2)}) collective-permute-start(f32[2,256,128]{2,1,0:T(8,128)S(1)} %get-tuple-element.70), channel_id=1, source_target_pairs={{1,2},{2,1},{3,4},{4,3},{5,6},{6,5},{7,8},{8,7},{9,10},{10,9},{11,... | collective-permute-start | bytes 786440 | tf_op jit(solution)/shard_map/ppermute | solution.py:626
  16.0 4.1 %collective-permute-start.3 = (f32[2,128,128]{2,1,0:T(8,128)S(1)}, f32[2,128,128]{2,1,0:T(8,128)S(1)}, u32[]{:S(2)}, u32[]{:S(2)}) collective-permute-start(f32[2,128,128]{2,1,0:T(8,128)S(1)} %get-tuple-element.75), channel_id=1, source_target_pairs={{1,18},{2,17},{3,20},{4,19},{5,22},{6,21},{7,24},{8,23},{9,26},{10... | collective-permute-start | bytes 393224 | tf_op jit(solution)/shard_map/ppermute | solution.py:626
  20.0 1.3 %collective-permute-start.4 = (f32[2,128,128]{2,1,0:T(8,128)S(1)}, f32[2,128,128]{2,1,0:T(8,128)S(1)}, u32[]{:S(2)}, u32[]{:S(2)}) collective-permute-start(f32[2,128,128]{2,1,0:T(8,128)S(1)} %get-tuple-element.74), channel_id=1, source_target_pairs={{17,2},{18,1},{19,4},{20,3},{21,6},{22,5},{23,8},{24,7},{25,10},{2... | collective-permute-start | bytes 393224 | tf_op jit(solution)/shard_map/ppermute | solution.py:626
  21.3 0.0 collective-permute-done.1.bottom
  21.3 1.6 %collective-permute-start.2 = (f32[2,256,128]{2,1,0:T(8,128)}, f32[2,256,128]{2,1,0:T(8,128)}, u32[]{:S(2)}, u32[]{:S(2)}) collective-permute-start(f32[2,256,128]{2,1,0:T(8,128)} %get-tuple-element.71), channel_id=1, source_target_pairs={{0,1},{1,0},{2,3},{3,2},{4,5},{5,4},{6,7},{7,6},{8,9},{9,8},{10,11... | collective-permute-start | bytes 786440 | tf_op jit(solution)/shard_map/ppermute | solution.py:626
  23.0 0.0 copy-start
  23.0 0.0 copy-start.3
  23.0 0.0 collective-permute-done.top
  23.0 0.7 pad_maximum_fusion
  23.7 1.2 %collective-permute-done.3.far_top = f32[2,128,128]{2,1,0:T(8,128)S(1)} collective-permute-done((f32[2,128,128]{2,1,0:T(8,128)S(1)}, f32[2,128,128]{2,1,0:T(8,128)S(1)}, u32[]{:S(2)}, u32[]{:S(2)}) %collective-permute-start.3) | collective-permute-done | bytes 131104 | tf_op jit(solution)/shard_map/ppermute | solution.py:626
  24.9 12.9 %collective-permute-done.4.far_bottom = f32[2,128,128]{2,1,0:T(8,128)S(1)} collective-permute-done((f32[2,128,128]{2,1,0:T(8,128)S(1)}, f32[2,128,128]{2,1,0:T(8,128)S(1)}, u32[]{:S(2)}, u32[]{:S(2)}) %collective-permute-start.4) | collective-permute-done | bytes 131104 | tf_op jit(solution)/shard_map/ppermute | solution.py:626
  37.8 0.7 copy-done.9
  38.5 0.0 collective-permute-done.5.far_mid
  38.5 0.7 copy-done.7
  39.2 0.0 collective-permute-start.6
  39.8 0.0 collective-permute-done.2.near_mid
  39.8 1.2 %collective-permute-done.6.near_corner = f32[2,256,128]{2,1,0:T(8,128)} collective-permute-done((f32[2,256,128]{2,1,0:T(8,128)}, f32[2,256,128]{2,1,0:T(8,128)}, u32[]{:S(2)}, u32[]{:S(2)}) %collective-permute-start.6) | collective-permute-done | bytes 262176 | tf_op jit(solution)/shard_map/ppermute | solution.py:626
  41.0 0.0 copy-done.4
  41.1 0.0 copy-done
  41.1 0.0 copy-done.3
  41.1 0.6 copy-done.11
  41.7 0.0 copy-done.12
  41.7 1.2 %copy-done.2 = f32[1,1,4,256,256]{4,3,2,1,0:T(8,128)S(1)} copy-done((f32[1,1,4,256,256]{4,3,2,1,0:T(8,128)S(1)}, f32[1,1,4,256,256]{4,3,2,1,0:T(8,128)}, u32[]{:S(2)}) %copy-start.2) | copy-done | bytes 1048600
  42.9 1.0 copy-done.5
  43.9 0.9 copy-done.6
  44.9 0.9 copy-done.8
  45.8 0.9 copy-done.10
  46.7 6.0 %patches.1 = (f32[2,256,512]{2,1,0:T(8,128)}, f32[2,128,512]{2,1,0:T(8,128)S(1)}, f32[2,128,512]{2,1,0:T(8,128)S(1)}, f32[2,256,128]{2,1,0:T(8,128)S(1)}, f32[2,...) custom-call(s32[1]{0:T(128)} %bitcast.10.counts, ...), custom_call_target="tpu_custom_call" | custom-call | tf_op jit(solution)/shard_map/patches/pallas_call | solution.py:381
  52.8 0.0 copy-start.13
  52.8 0.0 copy-start.15
  52.8 0.0 copy-start.16
  52.8 0.2 collective-permute-start.7
  53.0 1.8 %collective-permute-done.7.given = f32[2,512,128]{2,1,0:T(8,128)S(1)} collective-permute-done((f32[2,512,128]{2,1,0:T(8,128)S(1)}, f32[2,512,128]{2,1,0:T(8,128)S(1)}, u32[]{:S(2)}, u32[]{:S(2)}) %collective-permute-start.7) | collective-permute-done | bytes 524320 | tf_op jit(solution)/shard_map/ppermute | solution.py:626
  54.8 1.0 joined.1
  55.8 0.0 copy-done.13
  55.8 0.0 copy-done.15
  55.8 0.0 copy-done.16
  55.8 3.9 %collective-permute-start.8 = (f32[2,128,512]{2,1,0:T(8,128)S(1)}, f32[2,128,512]{2,1,0:T(8,128)S(1)}, u32[]{:S(2)}, u32[]{:S(2)}) collective-permute-start(f32[2,128,512]{2,1,0:T(8,128)S(1)} %get-tuple-element.53), channel_id=1, source_target_pairs={{0,16},{1,17},{2,18},{3,19},{4,20},{5,21},{6,22},{7,23},{8,24},{9,... | collective-permute-start | bytes 1572872 | tf_op jit(solution)/shard_map/ppermute | solution.py:626
  59.7 1.3 %collective-permute-start.10 = (f32[2,128,128]{2,1,0:T(8,128)}, f32[2,128,128]{2,1,0:T(8,128)S(1)}, u32[]{:S(2)}, u32[]{:S(2)}) collective-permute-start(f32[2,128,128]{2,1,0:T(8,128)} %copy-done.16), channel_id=1, source_target_pairs={{17,2},{18,1},{19,4},{20,3},{21,6},{22,5},{23,8},{24,7},{25,10},{2... | collective-permute-start | bytes 393224 | tf_op jit(solution)/shard_map/ppermute | solution.py:626
  61.0 8.6 %collective-permute-start.11 = (f32[2,128,128]{2,1,0:T(8,128)}, f32[2,128,128]{2,1,0:T(8,128)S(1)}, u32[]{:S(2)}, u32[]{:S(2)}) collective-permute-start(f32[2,128,128]{2,1,0:T(8,128)} %copy-done.15), channel_id=1, source_target_pairs={{1,18},{2,17},{3,20},{4,19},{5,22},{6,21},{7,24},{8,23},{9,26},{10... | collective-permute-start | bytes 393224 | tf_op jit(solution)/shard_map/ppermute | solution.py:626
  69.6 11.4 %all-to-all-start = ((f32[64,8,128]{2,1,0:T(8,128)}), f32[64,8,128]{2,1,0:T(8,128)S(1)}, u32[]{:S(2)}, u32[]{:S(2)}) async-start(f32[64,8,128]{2,1,0:T(8,128)} %get-tuple-element.67), calls=%async_computation | async-start | bytes 524288 | tf_op jit(solution)/shard_map/all_to_all | solution.py:710
  81.0 0.0 collective-permute-done.8.first
  81.0 0.7 collective-permute-start.9
  81.7 0.0 copy-start.1
  81.7 0.0 collective-permute-done.10.far_bottom
  81.8 0.0 collective-permute-done.11.far_top
  81.8 4.2 %collective-permute-start.12 = (f32[2,256,128]{2,1,0:T(8,128)}, f32[2,256,128]{2,1,0:T(8,128)S(1)}, u32[]{:S(2)}, u32[]{:S(2)}) collective-permute-start(f32[2,256,128]{2,1,0:T(8,128)} %get-tuple-element.60), channel_id=1, source_target_pairs={{1,2},{2,1},{3,4},{4,3},{5,6},{6,5},{7,8},{8,7},{9,10},{10,9},{11,... | collective-permute-start | bytes 786440 | tf_op jit(solution)/shard_map/ppermute | solution.py:626
  86.0 4.4 %all-to-all-done.parts = f32[64,8,128]{2,1,0:T(8,128)S(1)} async-done(((f32[64,8,128]{2,1,0:T(8,128)}), f32[64,8,128]{2,1,0:T(8,128)S(1)}, u32[]{:S(2)}, u32[]{:S(2)}) %all-to-all-start) | async-done | bytes 262176 | tf_op jit(solution)/shard_map/all_to_all | solution.py:710
  90.4 0.9 summed.1
  91.3 7.6 %all-to-all-start.1 = ((f32[128,8,128]{2,1,0:T(8,128)}), f32[128,8,128]{2,1,0:T(8,128)S(1)}, u32[]{:S(2)}, u32[]{:S(2)}) async-start(f32[128,8,128]{2,1,0:T(8,128)} %summed.1), calls=%async_computation.1 | async-start | bytes 1048576 | tf_op jit(solution)/shard_map/all_to_all | solution.py:715
  98.9 0.0 collective-permute-done.12.far_mid
  98.9 0.0 collective-permute-done.9.second
  98.9 0.0 copy-done.14
  98.9 1.3 %collective-permute-start.13 = (f32[2,256,128]{2,1,0:T(8,128)S(1)}, f32[2,256,128]{2,1,0:T(8,128)S(1)}, u32[]{:S(2)}, u32[]{:S(2)}) collective-permute-start(f32[2,256,128]{2,1,0:T(8,128)S(1)} %copy-done.14), channel_id=1, source_target_pairs={{0,1},{1,0},{2,3},{3,2},{4,5},{5,4},{6,7},{7,6},{8,9},{9,8},{10,11... | collective-permute-start | bytes 786440 | tf_op jit(solution)/shard_map/ppermute | solution.py:626
  100.2 1.2 %collective-permute-done.13.near_mid = f32[2,256,128]{2,1,0:T(8,128)S(1)} collective-permute-done((f32[2,256,128]{2,1,0:T(8,128)S(1)}, f32[2,256,128]{2,1,0:T(8,128)S(1)}, u32[]{:S(2)}, u32[]{:S(2)}) %collective-permute-start.13) | collective-permute-done | bytes 262176 | tf_op jit(solution)/shard_map/ppermute | solution.py:626
  101.4 0.0 copy-done.1
  101.4 3.8 %haar.1 = f32[2,256,512]{2,1,0:T(8,128)} custom-call(s32[1]{0:T(128)} %bitcast.core_of, s32[1]{0:T(128)} %bitcast.1.odd_of, f32[2,256,512]{2,1,0:T(8,128)S(1)} %copy-done.1, f32[2,128,512]{2,1,0:T(8,128)S(1)} %collective-permute-done.8.first, f32[2,128,512]{2,1,0:T(8,128)S(1)} %collective-permute-done.9.second, ...), custom_call_target="tpu_custom_call" | custom-call | tf_op jit(solution)/shard_map/haar/pallas_call | solution.py:538
  105.2 9.6 %all-to-all-done.1 = f32[128,8,128]{2,1,0:T(8,128)S(1)} async-done(((f32[128,8,128]{2,1,0:T(8,128)}), f32[128,8,128]{2,1,0:T(8,128)S(1)}, u32[]{:S(2)}, u32[]{:S(2)}) %all-to-all-start.1) | async-done | bytes 524320 | tf_op jit(solution)/shard_map/all_to_all | solution.py:715
  114.7 0.8 laid_out.1
  (16 shorter events, 0.1 us)
Async XLA Ops:
  3.3 18.0 %collective-permute-start.1 = (f32[2,128,512]{2,1,0:T(8,128)S(1)}, f32[2,128,512]{2,1,0:T(8,128)S(1)}, u32[]{:S(2)}, u32[]{:S(2)}) collective-permute-start(f32[2,128,512]{2,1,0:T(8,128)S(1)} %get-tuple-element.72), channel_id=1, source_target_pairs={{16,0},{17,1},{18,2},{19,3},{20,4},{21,5},{22,6},{23,7},{24,8},{25... | collective-permute-start | bytes 1572872 | tf_op jit(solution)/shard_map/ppermute | solution.py:626
  4.6 18.4 %collective-permute-start = (f32[2,128,512]{2,1,0:T(8,128)}, f32[2,128,512]{2,1,0:T(8,128)S(1)}, u32[]{:S(2)}, u32[]{:S(2)}) collective-permute-start(f32[2,128,512]{2,1,0:T(8,128)} %get-tuple-element.73), channel_id=1, source_target_pairs={{0,16},{1,17},{2,18},{3,19},{4,20},{5,21},{6,22},{7,23},{8,24},{9,... | collective-permute-start | bytes 1572872 | tf_op jit(solution)/shard_map/ppermute | solution.py:626
  11.5 27.0 %collective-permute-start.5 = (f32[2,256,128]{2,1,0:T(8,128)S(1)}, f32[2,256,128]{2,1,0:T(8,128)S(1)}, u32[]{:S(2)}, u32[]{:S(2)}) collective-permute-start(f32[2,256,128]{2,1,0:T(8,128)S(1)} %get-tuple-element.70), channel_id=1, source_target_pairs={{1,2},{2,1},{3,4},{4,3},{5,6},{6,5},{7,8},{8,7},{9,10},{10,9},{11,... | collective-permute-start | bytes 786440 | tf_op jit(solution)/shard_map/ppermute | solution.py:626
  16.0 9.0 %collective-permute-start.3 = (f32[2,128,128]{2,1,0:T(8,128)S(1)}, f32[2,128,128]{2,1,0:T(8,128)S(1)}, u32[]{:S(2)}, u32[]{:S(2)}) collective-permute-start(f32[2,128,128]{2,1,0:T(8,128)S(1)} %get-tuple-element.75), channel_id=1, source_target_pairs={{1,18},{2,17},{3,20},{4,19},{5,22},{6,21},{7,24},{8,23},{9,26},{10... | collective-permute-start | bytes 393224 | tf_op jit(solution)/shard_map/ppermute | solution.py:626
  20.0 17.8 %collective-permute-start.4 = (f32[2,128,128]{2,1,0:T(8,128)S(1)}, f32[2,128,128]{2,1,0:T(8,128)S(1)}, u32[]{:S(2)}, u32[]{:S(2)}) collective-permute-start(f32[2,128,128]{2,1,0:T(8,128)S(1)} %get-tuple-element.74), channel_id=1, source_target_pairs={{17,2},{18,1},{19,4},{20,3},{21,6},{22,5},{23,8},{24,7},{25,10},{2... | collective-permute-start | bytes 393224 | tf_op jit(solution)/shard_map/ppermute | solution.py:626
  21.3 18.5 %collective-permute-start.2 = (f32[2,256,128]{2,1,0:T(8,128)}, f32[2,256,128]{2,1,0:T(8,128)}, u32[]{:S(2)}, u32[]{:S(2)}) collective-permute-start(f32[2,256,128]{2,1,0:T(8,128)} %get-tuple-element.71), channel_id=1, source_target_pairs={{0,1},{1,0},{2,3},{3,2},{4,5},{5,4},{6,7},{7,6},{8,9},{9,8},{10,11... | collective-permute-start | bytes 786440 | tf_op jit(solution)/shard_map/ppermute | solution.py:626
  22.9 18.1 %copy-start.4 = (bf16[256,768]{1,0:T(8,128)(2,1)S(1)}, bf16[256,768]{1,0:T(8,128)(2,1)}, u32[]{:S(2)}) copy-start(bf16[256,768]{1,0:T(8,128)(2,1)} %constant.43.clone.left_table) | copy-start | bytes 1179652
  23.0 18.1 %copy-start = (f32[2,256,256]{2,1,0:T(8,128)S(1)}, f32[2,256,256]{2,1,0:T(8,128)}, u32[]{:S(2)}) copy-start(f32[2,256,256]{2,1,0:T(8,128)} %probe.1) | copy-start | bytes 1572868
  23.0 18.1 %copy-start.3 = (bf16[768,256]{1,0:T(8,128)(2,1)S(1)}, bf16[768,256]{1,0:T(8,128)(2,1)}, u32[]{:S(2)}) copy-start(bf16[768,256]{1,0:T(8,128)(2,1)} %constant.42.clone.order) | copy-start | bytes 1179652
  37.8 0.7 copy-start.9
  38.5 0.7 copy-start.7
  39.2 1.9 %collective-permute-start.6 = (f32[2,256,128]{2,1,0:T(8,128)}, f32[2,256,128]{2,1,0:T(8,128)}, u32[]{:S(2)}, u32[]{:S(2)}) collective-permute-start(f32[2,256,128]{2,1,0:T(8,128)} %pad_maximum_fusion), channel_id=1, source_target_pairs={{0,1},{1,0},{2,3},{3,2},{4,5},{5,4},{6,7},{7,6},{8,9},{9,8},{10,11... | collective-permute-start | bytes 786440 | tf_op jit(solution)/shard_map/ppermute | solution.py:626
  41.0 0.7 copy-start.11
  41.0 0.7 copy-start.12
  41.7 1.2 %copy-start.2 = (f32[1,1,4,256,256]{4,3,2,1,0:T(8,128)S(1)}, f32[1,1,4,256,256]{4,3,2,1,0:T(8,128)}, u32[]{:S(2)}) copy-start(f32[1,1,4,256,256]{4,3,2,1,0:T(8,128)} %param.14) | copy-start | bytes 3145732
  42.9 1.0 copy-start.5
  43.9 0.9 copy-start.6
  44.9 0.9 copy-start.8
  45.8 0.9 copy-start.10
  52.8 3.0 %copy-start.13 = (f32[2,256,128]{2,1,0:T(8,128)}, f32[2,256,128]{2,1,0:T(8,128)S(1)}, u32[]{:S(2)}) copy-start(f32[2,256,128]{2,1,0:T(8,128)S(1)} %get-tuple-element.63) | copy-start | bytes 786436
  52.8 3.0 %copy-start.15 = (f32[2,128,128]{2,1,0:T(8,128)}, f32[2,128,128]{2,1,0:T(8,128)S(1)}, u32[]{:S(2)}) copy-start(f32[2,128,128]{2,1,0:T(8,128)S(1)} %get-tuple-element.59) | copy-start | bytes 393220
  52.8 3.0 %copy-start.16 = (f32[2,128,128]{2,1,0:T(8,128)}, f32[2,128,128]{2,1,0:T(8,128)S(1)}, u32[]{:S(2)}) copy-start(f32[2,128,128]{2,1,0:T(8,128)S(1)} %get-tuple-element.58) | copy-start | bytes 393220
  52.8 2.0 %collective-permute-start.7 = (f32[2,512,128]{2,1,0:T(8,128)S(1)}, f32[2,512,128]{2,1,0:T(8,128)S(1)}, u32[]{:S(2)}, u32[]{:S(2)}) collective-permute-start(f32[2,512,128]{2,1,0:T(8,128)S(1)} %get-tuple-element.43), channel_id=1, source_target_pairs={{0,1},{1,0},{2,3},{3,2},{4,5},{5,4},{6,7},{7,6},{8,9},{9,8},{10,11... | collective-permute-start | bytes 1572872 | tf_op jit(solution)/shard_map/ppermute | solution.py:626
  55.8 25.2 %collective-permute-start.8 = (f32[2,128,512]{2,1,0:T(8,128)S(1)}, f32[2,128,512]{2,1,0:T(8,128)S(1)}, u32[]{:S(2)}, u32[]{:S(2)}) collective-permute-start(f32[2,128,512]{2,1,0:T(8,128)S(1)} %get-tuple-element.53), channel_id=1, source_target_pairs={{0,16},{1,17},{2,18},{3,19},{4,20},{5,21},{6,22},{7,23},{8,24},{9,... | collective-permute-start | bytes 1572872 | tf_op jit(solution)/shard_map/ppermute | solution.py:626
  59.7 22.0 %collective-permute-start.10 = (f32[2,128,128]{2,1,0:T(8,128)}, f32[2,128,128]{2,1,0:T(8,128)S(1)}, u32[]{:S(2)}, u32[]{:S(2)}) collective-permute-start(f32[2,128,128]{2,1,0:T(8,128)} %copy-done.16), channel_id=1, source_target_pairs={{17,2},{18,1},{19,4},{20,3},{21,6},{22,5},{23,8},{24,7},{25,10},{2... | collective-permute-start | bytes 393224 | tf_op jit(solution)/shard_map/ppermute | solution.py:626
  61.0 20.7 %collective-permute-start.11 = (f32[2,128,128]{2,1,0:T(8,128)}, f32[2,128,128]{2,1,0:T(8,128)S(1)}, u32[]{:S(2)}, u32[]{:S(2)}) collective-permute-start(f32[2,128,128]{2,1,0:T(8,128)} %copy-done.15), channel_id=1, source_target_pairs={{1,18},{2,17},{3,20},{4,19},{5,22},{6,21},{7,24},{8,23},{9,26},{10... | collective-permute-start | bytes 393224 | tf_op jit(solution)/shard_map/ppermute | solution.py:626
  69.6 20.8 %all-to-all-start = ((f32[64,8,128]{2,1,0:T(8,128)}), f32[64,8,128]{2,1,0:T(8,128)S(1)}, u32[]{:S(2)}, u32[]{:S(2)}) async-start(f32[64,8,128]{2,1,0:T(8,128)} %get-tuple-element.67), calls=%async_computation | async-start | bytes 524288 | tf_op jit(solution)/shard_map/all_to_all | solution.py:710
  81.0 17.9 %collective-permute-start.9 = (f32[2,128,512]{2,1,0:T(8,128)}, f32[2,128,512]{2,1,0:T(8,128)S(1)}, u32[]{:S(2)}, u32[]{:S(2)}) collective-permute-start(f32[2,128,512]{2,1,0:T(8,128)} %get-tuple-element.56), channel_id=1, source_target_pairs={{16,32},{17,33},{18,34},{19,35},{20,36},{21,37},{22,38},{23,39},{2... | collective-permute-start | bytes 1572872 | tf_op jit(solution)/shard_map/ppermute | solution.py:626
  81.7 19.6 %copy-start.1 = (f32[2,256,512]{2,1,0:T(8,128)S(1)}, f32[2,256,512]{2,1,0:T(8,128)}, u32[]{:S(2)}) copy-start(f32[2,256,512]{2,1,0:T(8,128)} %get-tuple-element.40.inner) | copy-start | bytes 3145732
  81.8 17.1 %collective-permute-start.12 = (f32[2,256,128]{2,1,0:T(8,128)}, f32[2,256,128]{2,1,0:T(8,128)S(1)}, u32[]{:S(2)}, u32[]{:S(2)}) collective-permute-start(f32[2,256,128]{2,1,0:T(8,128)} %get-tuple-element.60), channel_id=1, source_target_pairs={{1,2},{2,1},{3,4},{4,3},{5,6},{6,5},{7,8},{8,7},{9,10},{10,9},{11,... | collective-permute-start | bytes 786440 | tf_op jit(solution)/shard_map/ppermute | solution.py:626
  91.3 7.6 %copy-start.14 = (f32[2,256,128]{2,1,0:T(8,128)S(1)}, f32[2,256,128]{2,1,0:T(8,128)}, u32[]{:S(2)}) copy-start(f32[2,256,128]{2,1,0:T(8,128)} %copy-done.13) | copy-start | bytes 786436
  91.3 23.5 %all-to-all-start.1 = ((f32[128,8,128]{2,1,0:T(8,128)}), f32[128,8,128]{2,1,0:T(8,128)S(1)}, u32[]{:S(2)}, u32[]{:S(2)}) async-start(f32[128,8,128]{2,1,0:T(8,128)} %summed.1), calls=%async_computation.1 | async-start | bytes 1048576 | tf_op jit(solution)/shard_map/all_to_all | solution.py:715
  98.9 2.5 %collective-permute-start.13 = (f32[2,256,128]{2,1,0:T(8,128)S(1)}, f32[2,256,128]{2,1,0:T(8,128)S(1)}, u32[]{:S(2)}, u32[]{:S(2)}) collective-permute-start(f32[2,256,128]{2,1,0:T(8,128)S(1)} %copy-done.14), channel_id=1, source_target_pairs={{0,1},{1,0},{2,3},{3,2},{4,5},{5,4},{6,7},{7,6},{8,9},{9,8},{10,11... | collective-permute-start | bytes 786440 | tf_op jit(solution)/shard_map/ppermute | solution.py:626

commit v5 on v4

--- a/solution.py
+++ b/solution.py
@@ -175,11 +175,11 @@
     far_top,
     far_bottom,
     amplitude_in,
-    probe,
-    order,
-    left_table,
-    right_table,
-    twiddle_table,
+    order_in,
+    probe_in,
+    left_in,
+    right_in,
+    twiddle_in,
     inner_out,
     first_out,
     second_out,
@@ -195,6 +195,11 @@
     measured,
     sorted_lanes,
     amplitude,
+    probe,
+    order,
+    left_table,
+    right_table,
+    twiddle_table,
     sems,
 ):
     size = probe.shape[1]
@@ -222,13 +227,24 @@
         pltpu.make_async_copy(source, target, sems.at[index])
         for index, (source, target) in enumerate(moves)
     ]
-    measured_copy = pltpu.make_async_copy(amplitude_in, measured, sems.at[len(moves)])
-    measured_copy.start()
-    for copy in copies:
+    constants = [
+        (amplitude_in, measured),
+        (order_in, order),
+        (probe_in, probe),
+        (left_in, left_table),
+        (right_in, right_table),
+        (twiddle_in, twiddle_table),
+    ]
+    constant_copies = [
+        pltpu.make_async_copy(source, target, sems.at[len(moves) + index])
+        for index, (source, target) in enumerate(constants)
+    ]
+    for copy in constant_copies + copies:
         copy.start()
     gradient[...] = jnp.zeros_like(gradient)
     probe_sum[...] = jnp.zeros_like(probe_sum)
-    measured_copy.wait()
+    for copy in constant_copies:
+        copy.wait()
 
     def order_slot(slot, carry):
         order_amplitude(slot, measured, order, sorted_lanes, amplitude)
@@ -364,9 +380,13 @@
     margin = size // 2
     height, width = pieces[0].shape[1:]
     tall, wide = height + size, width + size
+    tables = (order_table(size),) + dft_tables(size)
+    order, *tables = (jnp.asarray(table) for table in tables)
+    constants = (amplitude, order, probe, *tables)
     smem = pl.BlockSpec(memory_space=pltpu.SMEM)
     vmem = pl.BlockSpec(memory_space=pltpu.VMEM)
     anywhere = pl.BlockSpec(memory_space=pl.ANY)
+    hbm = pl.BlockSpec(memory_space=pltpu.HBM)
     shapes = [
         (height, width),
         (margin, width),
@@ -382,7 +402,7 @@
         patch_kernel,
         out_shape=(pltpu.HBM((2,) + shapes[0], jnp.float32),)
         + tuple(jax.ShapeDtypeStruct((2,) + shape, jnp.float32) for shape in shapes[1:]),
-        in_specs=[smem] * 5 + [anywhere] * 9 + [vmem] * 5,
+        in_specs=[smem] * 5 + [anywhere] * 8 + [hbm] * 6,
         out_specs=[anywhere] + [vmem] * 8,
         scratch_shapes=[
             pltpu.VMEM((2, tall, wide), jnp.float32),
@@ -391,7 +411,9 @@
             pltpu.VMEM(amplitude.shape, jnp.float32),
             pltpu.VMEM((2, size, size // 2), jnp.float32),
             pltpu.VMEM((amplitude.shape[0], 4, size // 2, size // 2), jnp.float32),
-            pltpu.SemaphoreType.DMA((10,)),
+            pltpu.VMEM(probe.shape, jnp.float32),
+            *(pltpu.VMEM(value.shape, value.dtype) for value in (order, *tables)),
+            pltpu.SemaphoreType.DMA((15,)),
         ],
         compiler_params=pltpu.CompilerParams(vmem_limit_bytes=28 * MIB),
         name="patches",
@@ -401,10 +423,7 @@
         cols,
         *place_of,
         *pieces,
-        amplitude,
-        probe,
-        jnp.asarray(order_table(size)),
-        *(jnp.asarray(table) for table in dft_tables(size)),
+        *(pltpu.with_memory_space_constraint(value, pltpu.HBM) for value in constants),
     )
 
 

time: 116 us -> 111 us (0.957); the launches traced: 116 us -> 112 us
  local copies, waits for them, and re-layouts: 7.99 us -> 1.75 us
  waiting for transfers between devices: 32.2 us -> 36 us
  starting transfers between devices: 57.9 us -> 56.6 us
    unnamed x34 -> x10, local copies, waits for them, and re-layouts: 7.07 us -> 0.68 us
    all_to_all x1, waiting for transfers between devices: 4.43 us -> 6.94 us  [on_device(): shares = lax.all_to_all(shares, CHIPS, 0, 0, tiled=True)]
    all_to_all x1, starting transfers between devices: 7.57 us -> 5.09 us  [on_device(): tiles = lax.all_to_all(tiles, AXES, 0, 0, tiled=True)]
    all_to_all x1, starting transfers between devices: 11.4 us -> 13.2 us  [on_device(): shares = lax.all_to_all(shares, CHIPS, 0, 0, tiled=True)]
where the time goes in v5:
time: 111 us; the launch traced here: 112 us
  starting transfers between devices  56.6 us (51%)
  waiting for transfers between devices  36 us (32%)
  Pallas kernels  13.4 us (12%)
  other arithmetic  2.6 us (2%)
  local copies, waits for them, and re-layouts  1.75 us (2%)
  between operations  1.53 us (1%)
    ppermute x14, starting transfers between devices, permuted(): return lax.ppermute(value, AXES, pairs)  38.3 us
    ppermute x14, waiting for transfers between devices, permuted(): return lax.ppermute(value, AXES, pairs)  18.4 us
    all_to_all x1, starting transfers between devices, on_device(): shares = lax.all_to_all(shares, CHIPS, 0, 0, tiled=True)  13.2 us
    all_to_all x1, waiting for transfers between devices, on_device(): tiles = lax.all_to_all(tiles, AXES, 0, 0, tiled=True)  10.7 us
    all_to_all x1, waiting for transfers between devices, on_device(): shares = lax.all_to_all(shares, CHIPS, 0, 0, tiled=True)  6.94 us
    pallas_call x1, Pallas kernels, patches(): pl.pallas_call(patch_kernel, out_shape=(pltpu.HBM((2,) + shapes[0], jnp.f...  6.81 us
    all_to_all x1, starting transfers between devices, on_device(): tiles = lax.all_to_all(tiles, AXES, 0, 0, tiled=True)  5.09 us
    pallas_call x1, Pallas kernels, shrink_object(): pl.pallas_call(haar_kernel, out_shape=jax.ShapeDtypeStruct(shape, jnp.flo...  3.8 us
  transfers between devices with their start and end apart: 16, of which 7 were waited for; matrix products, arithmetic and copies ran while one was open for 1% of the time, Pallas kernels for 4%

profile of v5, /device:TPU:1, one launch (start us, length us, event | category | flops | bytes accessed | tf_op | source)
XLA Modules:
  0.0 111.8 jit_solution(17200839514447808126)
XLA Ops:
  0.6 1.8 %multiply_add_fusion.centre = f32[2,256,512]{2,1,0:T(8,128)S(1)} fusion(f32[2,256,512]{2,1,0:T(8,128)} %param.11, f32[2,256,512]{2,1,0:T(8,128)} %param.12), kind=kLoop, calls=%fused_computation | loop fusion | flops 786432 | bytes 3145728 | tf_op jit(solution)/shard_map/add | solution.py:665
  2.4 1.0 fusion
  3.4 1.3 %collective-permute-start.1 = (f32[2,128,512]{2,1,0:T(8,128)}, f32[2,128,512]{2,1,0:T(8,128)S(1)}, u32[]{:S(2)}, u32[]{:S(2)}) collective-permute-start(f32[2,128,512]{2,1,0:T(8,128)} %get-tuple-element.72), channel_id=1, source_target_pairs={{16,0},{17,1},{18,2},{19,3},{20,4},{21,5},{22,6},{23,7},{24,8},{25... | collective-permute-start | bytes 1572872 | tf_op jit(solution)/shard_map/ppermute | solution.py:645
  4.7 6.1 %collective-permute-start = (f32[2,128,512]{2,1,0:T(8,128)}, f32[2,128,512]{2,1,0:T(8,128)S(1)}, u32[]{:S(2)}, u32[]{:S(2)}) collective-permute-start(f32[2,128,512]{2,1,0:T(8,128)} %get-tuple-element.73), channel_id=1, source_target_pairs={{0,16},{1,17},{2,18},{3,19},{4,20},{5,21},{6,22},{7,23},{8,24},{9,... | collective-permute-start | bytes 1572872 | tf_op jit(solution)/shard_map/ppermute | solution.py:645
  10.9 0.7 slice_select_fusion.1
  11.6 4.4 %collective-permute-start.5 = (f32[2,256,128]{2,1,0:T(8,128)S(1)}, f32[2,256,128]{2,1,0:T(8,128)S(1)}, u32[]{:S(2)}, u32[]{:S(2)}) collective-permute-start(f32[2,256,128]{2,1,0:T(8,128)S(1)} %get-tuple-element.70), channel_id=1, source_target_pairs={{1,2},{2,1},{3,4},{4,3},{5,6},{6,5},{7,8},{8,7},{9,10},{10,9},{11,... | collective-permute-start | bytes 786440 | tf_op jit(solution)/shard_map/ppermute | solution.py:645
  16.1 4.1 %collective-permute-start.3 = (f32[2,128,128]{2,1,0:T(8,128)S(1)}, f32[2,128,128]{2,1,0:T(8,128)S(1)}, u32[]{:S(2)}, u32[]{:S(2)}) collective-permute-start(f32[2,128,128]{2,1,0:T(8,128)S(1)} %get-tuple-element.75), channel_id=1, source_target_pairs={{1,18},{2,17},{3,20},{4,19},{5,22},{6,21},{7,24},{8,23},{9,26},{10... | collective-permute-start | bytes 393224 | tf_op jit(solution)/shard_map/ppermute | solution.py:645
  20.2 1.3 %collective-permute-start.4 = (f32[2,128,128]{2,1,0:T(8,128)S(1)}, f32[2,128,128]{2,1,0:T(8,128)S(1)}, u32[]{:S(2)}, u32[]{:S(2)}) collective-permute-start(f32[2,128,128]{2,1,0:T(8,128)S(1)} %get-tuple-element.74), channel_id=1, source_target_pairs={{17,2},{18,1},{19,4},{20,3},{21,6},{22,5},{23,8},{24,7},{25,10},{2... | collective-permute-start | bytes 393224 | tf_op jit(solution)/shard_map/ppermute | solution.py:645
  21.5 0.0 collective-permute-done.1.bottom
  21.5 1.8 %collective-permute-start.2 = (f32[2,256,128]{2,1,0:T(8,128)}, f32[2,256,128]{2,1,0:T(8,128)S(1)}, u32[]{:S(2)}, u32[]{:S(2)}) collective-permute-start(f32[2,256,128]{2,1,0:T(8,128)} %get-tuple-element.71), channel_id=1, source_target_pairs={{0,1},{1,0},{2,3},{3,2},{4,5},{5,4},{6,7},{7,6},{8,9},{9,8},{10,11... | collective-permute-start | bytes 786440 | tf_op jit(solution)/shard_map/ppermute | solution.py:645
  23.3 0.0 collective-permute-done.top
  23.4 1.7 %collective-permute-done.3.far_top = f32[2,128,128]{2,1,0:T(8,128)S(1)} collective-permute-done((f32[2,128,128]{2,1,0:T(8,128)S(1)}, f32[2,128,128]{2,1,0:T(8,128)S(1)}, u32[]{:S(2)}, u32[]{:S(2)}) %collective-permute-start.3) | collective-permute-done | bytes 131104 | tf_op jit(solution)/shard_map/ppermute | solution.py:645
  25.1 13.1 %collective-permute-done.4.far_bottom = f32[2,128,128]{2,1,0:T(8,128)S(1)} collective-permute-done((f32[2,128,128]{2,1,0:T(8,128)S(1)}, f32[2,128,128]{2,1,0:T(8,128)S(1)}, u32[]{:S(2)}, u32[]{:S(2)}) %collective-permute-start.4) | collective-permute-done | bytes 131104 | tf_op jit(solution)/shard_map/ppermute | solution.py:645
  38.2 0.0 collective-permute-done.5.far_mid
  38.2 0.0 collective-permute-start.6
  38.8 0.0 collective-permute-done.2.near_mid
  38.8 0.9 collective-permute-done.6.near_corner
  39.7 0.0 copy-start.1
  39.7 0.0 copy-start.2
  39.7 0.7 copy-done.1
  40.4 0.0 copy-done.2
  40.4 6.8 %patches.1 = (f32[2,256,512]{2,1,0:T(8,128)}, f32[2,128,512]{2,1,0:T(8,128)S(1)}, f32[2,128,512]{2,1,0:T(8,128)S(1)}, f32[2,256,128]{2,1,0:T(8,128)S(1)}, f32[2,...) custom-call(s32[1]{0:T(128)} %bitcast.10.counts, ...), custom_call_target="tpu_custom_call" | custom-call | tf_op jit(solution)/shard_map/patches/pallas_call | solution.py:401
  47.2 0.0 copy-start.3
  47.2 1.5 %collective-permute-start.7 = (f32[2,512,128]{2,1,0:T(8,128)S(1)}, f32[2,512,128]{2,1,0:T(8,128)S(1)}, u32[]{:S(2)}, u32[]{:S(2)}) collective-permute-start(f32[2,512,128]{2,1,0:T(8,128)S(1)} %get-tuple-element.43), channel_id=1, source_target_pairs={{0,1},{1,0},{2,3},{3,2},{4,5},{5,4},{6,7},{7,6},{8,9},{9,8},{10,11... | collective-permute-start | bytes 1572872 | tf_op jit(solution)/shard_map/ppermute | solution.py:645
  48.7 1.5 %collective-permute-done.7.given = f32[2,512,128]{2,1,0:T(8,128)S(1)} collective-permute-done((f32[2,512,128]{2,1,0:T(8,128)S(1)}, f32[2,512,128]{2,1,0:T(8,128)S(1)}, u32[]{:S(2)}, u32[]{:S(2)}) %collective-permute-start.7) | collective-permute-done | bytes 524320 | tf_op jit(solution)/shard_map/ppermute | solution.py:645
  50.3 1.0 joined.1
  51.3 0.0 copy-done.3
  51.3 0.0 copy-start.4
  51.3 2.8 %collective-permute-start.8 = (f32[2,128,512]{2,1,0:T(8,128)S(1)}, f32[2,128,512]{2,1,0:T(8,128)S(1)}, u32[]{:S(2)}, u32[]{:S(2)}) collective-permute-start(f32[2,128,512]{2,1,0:T(8,128)S(1)} %get-tuple-element.53), channel_id=1, source_target_pairs={{0,16},{1,17},{2,18},{3,19},{4,20},{5,21},{6,22},{7,23},{8,24},{9,... | collective-permute-start | bytes 1572872 | tf_op jit(solution)/shard_map/ppermute | solution.py:645
  54.1 1.3 %collective-permute-start.10 = (f32[2,128,128]{2,1,0:T(8,128)}, f32[2,128,128]{2,1,0:T(8,128)S(1)}, u32[]{:S(2)}, u32[]{:S(2)}) collective-permute-start(f32[2,128,128]{2,1,0:T(8,128)} %copy-done.3), channel_id=1, source_target_pairs={{17,2},{18,1},{19,4},{20,3},{21,6},{22,5},{23,8},{24,7},{25,10},{2... | collective-permute-start | bytes 393224 | tf_op jit(solution)/shard_map/ppermute | solution.py:645
  55.4 8.7 %collective-permute-start.11 = (f32[2,128,128]{2,1,0:T(8,128)S(1)}, f32[2,128,128]{2,1,0:T(8,128)S(1)}, u32[]{:S(2)}, u32[]{:S(2)}) collective-permute-start(f32[2,128,128]{2,1,0:T(8,128)S(1)} %get-tuple-element.59), channel_id=1, source_target_pairs={{1,18},{2,17},{3,20},{4,19},{5,22},{6,21},{7,24},{8,23},{9,26},{10... | collective-permute-start | bytes 393224 | tf_op jit(solution)/shard_map/ppermute | solution.py:645
  64.0 13.2 %all-to-all-start = ((f32[64,8,128]{2,1,0:T(8,128)}), f32[64,8,128]{2,1,0:T(8,128)S(1)}, u32[]{:S(2)}, u32[]{:S(2)}) async-start(f32[64,8,128]{2,1,0:T(8,128)} %get-tuple-element.67), calls=%async_computation | async-start | bytes 524288 | tf_op jit(solution)/shard_map/all_to_all | solution.py:729
  77.2 0.0 collective-permute-done.8.first
  77.2 0.7 collective-permute-start.9
  77.9 0.0 copy-done.4
  78.0 0.0 copy-start
  78.0 0.0 collective-permute-done.10.far_bottom
  78.0 0.0 collective-permute-done.11.far_top
  78.0 3.0 %collective-permute-start.12 = (f32[2,256,128]{2,1,0:T(8,128)}, f32[2,256,128]{2,1,0:T(8,128)S(1)}, u32[]{:S(2)}, u32[]{:S(2)}) collective-permute-start(f32[2,256,128]{2,1,0:T(8,128)} %get-tuple-element.60), channel_id=1, source_target_pairs={{1,2},{2,1},{3,4},{4,3},{5,6},{6,5},{7,8},{8,7},{9,10},{10,9},{11,... | collective-permute-start | bytes 786440 | tf_op jit(solution)/shard_map/ppermute | solution.py:645
  81.0 6.9 %all-to-all-done.parts = f32[64,8,128]{2,1,0:T(8,128)S(1)} async-done(((f32[64,8,128]{2,1,0:T(8,128)}), f32[64,8,128]{2,1,0:T(8,128)S(1)}, u32[]{:S(2)}, u32[]{:S(2)}) %all-to-all-start) | async-done | bytes 262176 | tf_op jit(solution)/shard_map/all_to_all | solution.py:729
  88.0 0.9 summed.1
  88.9 5.1 %all-to-all-start.1 = ((f32[128,8,128]{2,1,0:T(8,128)}), f32[128,8,128]{2,1,0:T(8,128)S(1)}, u32[]{:S(2)}, u32[]{:S(2)}) async-start(f32[128,8,128]{2,1,0:T(8,128)} %summed.1), calls=%async_computation.1 | async-start | bytes 1048576 | tf_op jit(solution)/shard_map/all_to_all | solution.py:734
  94.0 0.0 collective-permute-done.12.far_mid
  94.0 0.0 collective-permute-done.9.second
  94.0 1.3 %collective-permute-start.13 = (f32[2,256,128]{2,1,0:T(8,128)S(1)}, f32[2,256,128]{2,1,0:T(8,128)S(1)}, u32[]{:S(2)}, u32[]{:S(2)}) collective-permute-start(f32[2,256,128]{2,1,0:T(8,128)S(1)} %get-tuple-element.63), channel_id=1, source_target_pairs={{0,1},{1,0},{2,3},{3,2},{4,5},{5,4},{6,7},{7,6},{8,9},{9,8},{10,11... | collective-permute-start | bytes 786440 | tf_op jit(solution)/shard_map/ppermute | solution.py:645
  95.3 1.2 %collective-permute-done.13.near_mid = f32[2,256,128]{2,1,0:T(8,128)S(1)} collective-permute-done((f32[2,256,128]{2,1,0:T(8,128)S(1)}, f32[2,256,128]{2,1,0:T(8,128)S(1)}, u32[]{:S(2)}, u32[]{:S(2)}) %collective-permute-start.13) | collective-permute-done | bytes 262176 | tf_op jit(solution)/shard_map/ppermute | solution.py:645
  96.5 0.0 copy-done
  96.5 3.8 %haar.1 = f32[2,256,512]{2,1,0:T(8,128)} custom-call(s32[1]{0:T(128)} %bitcast.core_of, s32[1]{0:T(128)} %bitcast.1.odd_of, f32[2,256,512]{2,1,0:T(8,128)S(1)} %copy-done, f32[2,128,512]{2,1,0:T(8,128)S(1)} %collective-permute-done.8.first, f32[2,128,512]{2,1,0:T(8,128)S(1)} %collective-permute-done.9.second, ...), custom_call_target="tpu_custom_call" | custom-call | tf_op jit(solution)/shard_map/haar/pallas_call | solution.py:557
  100.3 10.7 %all-to-all-done.1 = f32[128,8,128]{2,1,0:T(8,128)S(1)} async-done(((f32[128,8,128]{2,1,0:T(8,128)}), f32[128,8,128]{2,1,0:T(8,128)S(1)}, u32[]{:S(2)}, u32[]{:S(2)}) %all-to-all-start.1) | async-done | bytes 524320 | tf_op jit(solution)/shard_map/all_to_all | solution.py:734
  111.0 0.8 laid_out.1
  (6 shorter events, 0.1 us)
Async XLA Ops:
  3.4 18.0 %collective-permute-start.1 = (f32[2,128,512]{2,1,0:T(8,128)}, f32[2,128,512]{2,1,0:T(8,128)S(1)}, u32[]{:S(2)}, u32[]{:S(2)}) collective-permute-start(f32[2,128,512]{2,1,0:T(8,128)} %get-tuple-element.72), channel_id=1, source_target_pairs={{16,0},{17,1},{18,2},{19,3},{20,4},{21,5},{22,6},{23,7},{24,8},{25... | collective-permute-start | bytes 1572872 | tf_op jit(solution)/shard_map/ppermute | solution.py:645
  4.7 18.6 %collective-permute-start = (f32[2,128,512]{2,1,0:T(8,128)}, f32[2,128,512]{2,1,0:T(8,128)S(1)}, u32[]{:S(2)}, u32[]{:S(2)}) collective-permute-start(f32[2,128,512]{2,1,0:T(8,128)} %get-tuple-element.73), channel_id=1, source_target_pairs={{0,16},{1,17},{2,18},{3,19},{4,20},{5,21},{6,22},{7,23},{8,24},{9,... | collective-permute-start | bytes 1572872 | tf_op jit(solution)/shard_map/ppermute | solution.py:645
  11.6 26.5 %collective-permute-start.5 = (f32[2,256,128]{2,1,0:T(8,128)S(1)}, f32[2,256,128]{2,1,0:T(8,128)S(1)}, u32[]{:S(2)}, u32[]{:S(2)}) collective-permute-start(f32[2,256,128]{2,1,0:T(8,128)S(1)} %get-tuple-element.70), channel_id=1, source_target_pairs={{1,2},{2,1},{3,4},{4,3},{5,6},{6,5},{7,8},{8,7},{9,10},{10,9},{11,... | collective-permute-start | bytes 786440 | tf_op jit(solution)/shard_map/ppermute | solution.py:645
  16.1 9.0 %collective-permute-start.3 = (f32[2,128,128]{2,1,0:T(8,128)S(1)}, f32[2,128,128]{2,1,0:T(8,128)S(1)}, u32[]{:S(2)}, u32[]{:S(2)}) collective-permute-start(f32[2,128,128]{2,1,0:T(8,128)S(1)} %get-tuple-element.75), channel_id=1, source_target_pairs={{1,18},{2,17},{3,20},{4,19},{5,22},{6,21},{7,24},{8,23},{9,26},{10... | collective-permute-start | bytes 393224 | tf_op jit(solution)/shard_map/ppermute | solution.py:645
  20.2 18.0 %collective-permute-start.4 = (f32[2,128,128]{2,1,0:T(8,128)S(1)}, f32[2,128,128]{2,1,0:T(8,128)S(1)}, u32[]{:S(2)}, u32[]{:S(2)}) collective-permute-start(f32[2,128,128]{2,1,0:T(8,128)S(1)} %get-tuple-element.74), channel_id=1, source_target_pairs={{17,2},{18,1},{19,4},{20,3},{21,6},{22,5},{23,8},{24,7},{25,10},{2... | collective-permute-start | bytes 393224 | tf_op jit(solution)/shard_map/ppermute | solution.py:645
  21.5 17.3 %collective-permute-start.2 = (f32[2,256,128]{2,1,0:T(8,128)}, f32[2,256,128]{2,1,0:T(8,128)S(1)}, u32[]{:S(2)}, u32[]{:S(2)}) collective-permute-start(f32[2,256,128]{2,1,0:T(8,128)} %get-tuple-element.71), channel_id=1, source_target_pairs={{0,1},{1,0},{2,3},{3,2},{4,5},{5,4},{6,7},{7,6},{8,9},{9,8},{10,11... | collective-permute-start | bytes 786440 | tf_op jit(solution)/shard_map/ppermute | solution.py:645
  38.2 1.5 %collective-permute-start.6 = (f32[2,256,128]{2,1,0:T(8,128)S(1)}, f32[2,256,128]{2,1,0:T(8,128)S(1)}, u32[]{:S(2)}, u32[]{:S(2)}) collective-permute-start(f32[2,256,128]{2,1,0:T(8,128)S(1)} %pad_maximum_fusion), channel_id=1, source_target_pairs={{0,1},{1,0},{2,3},{3,2},{4,5},{5,4},{6,7},{7,6},{8,9},{9,8},{10,11... | collective-permute-start | bytes 786440 | tf_op jit(solution)/shard_map/ppermute | solution.py:645
  39.7 0.7 copy-start.1
  39.7 0.7 copy-start.2
  47.2 4.1 %copy-start.3 = (f32[2,128,128]{2,1,0:T(8,128)}, f32[2,128,128]{2,1,0:T(8,128)S(1)}, u32[]{:S(2)}) copy-start(f32[2,128,128]{2,1,0:T(8,128)S(1)} %get-tuple-element.58) | copy-start | bytes 393220
  47.2 3.1 %collective-permute-start.7 = (f32[2,512,128]{2,1,0:T(8,128)S(1)}, f32[2,512,128]{2,1,0:T(8,128)S(1)}, u32[]{:S(2)}, u32[]{:S(2)}) collective-permute-start(f32[2,512,128]{2,1,0:T(8,128)S(1)} %get-tuple-element.43), channel_id=1, source_target_pairs={{0,1},{1,0},{2,3},{3,2},{4,5},{5,4},{6,7},{7,6},{8,9},{9,8},{10,11... | collective-permute-start | bytes 1572872 | tf_op jit(solution)/shard_map/ppermute | solution.py:645
  51.3 26.6 %copy-start.4 = (f32[2,256,256]{2,1,0:T(8,128)S(1)}, f32[2,256,256]{2,1,0:T(8,128)}, u32[]{:S(2)}) copy-start(f32[2,256,256]{2,1,0:T(8,128)} %probe_in.1) | copy-start | bytes 1572868
  51.3 25.9 %collective-permute-start.8 = (f32[2,128,512]{2,1,0:T(8,128)S(1)}, f32[2,128,512]{2,1,0:T(8,128)S(1)}, u32[]{:S(2)}, u32[]{:S(2)}) collective-permute-start(f32[2,128,512]{2,1,0:T(8,128)S(1)} %get-tuple-element.53), channel_id=1, source_target_pairs={{0,16},{1,17},{2,18},{3,19},{4,20},{5,21},{6,22},{7,23},{8,24},{9,... | collective-permute-start | bytes 1572872 | tf_op jit(solution)/shard_map/ppermute | solution.py:645
  54.1 23.9 %collective-permute-start.10 = (f32[2,128,128]{2,1,0:T(8,128)}, f32[2,128,128]{2,1,0:T(8,128)S(1)}, u32[]{:S(2)}, u32[]{:S(2)}) collective-permute-start(f32[2,128,128]{2,1,0:T(8,128)} %copy-done.3), channel_id=1, source_target_pairs={{17,2},{18,1},{19,4},{20,3},{21,6},{22,5},{23,8},{24,7},{25,10},{2... | collective-permute-start | bytes 393224 | tf_op jit(solution)/shard_map/ppermute | solution.py:645
  55.4 22.6 %collective-permute-start.11 = (f32[2,128,128]{2,1,0:T(8,128)S(1)}, f32[2,128,128]{2,1,0:T(8,128)S(1)}, u32[]{:S(2)}, u32[]{:S(2)}) collective-permute-start(f32[2,128,128]{2,1,0:T(8,128)S(1)} %get-tuple-element.59), channel_id=1, source_target_pairs={{1,18},{2,17},{3,20},{4,19},{5,22},{6,21},{7,24},{8,23},{9,26},{10... | collective-permute-start | bytes 393224 | tf_op jit(solution)/shard_map/ppermute | solution.py:645
  64.0 23.9 %all-to-all-start = ((f32[64,8,128]{2,1,0:T(8,128)}), f32[64,8,128]{2,1,0:T(8,128)S(1)}, u32[]{:S(2)}, u32[]{:S(2)}) async-start(f32[64,8,128]{2,1,0:T(8,128)} %get-tuple-element.67), calls=%async_computation | async-start | bytes 524288 | tf_op jit(solution)/shard_map/all_to_all | solution.py:729
  77.2 16.8 %collective-permute-start.9 = (f32[2,128,512]{2,1,0:T(8,128)}, f32[2,128,512]{2,1,0:T(8,128)S(1)}, u32[]{:S(2)}, u32[]{:S(2)}) collective-permute-start(f32[2,128,512]{2,1,0:T(8,128)} %get-tuple-element.56), channel_id=1, source_target_pairs={{16,32},{17,33},{18,34},{19,35},{20,36},{21,37},{22,38},{23,39},{2... | collective-permute-start | bytes 1572872 | tf_op jit(solution)/shard_map/ppermute | solution.py:645
  78.0 18.6 %copy-start = (f32[2,256,512]{2,1,0:T(8,128)S(1)}, f32[2,256,512]{2,1,0:T(8,128)}, u32[]{:S(2)}) copy-start(f32[2,256,512]{2,1,0:T(8,128)} %get-tuple-element.40.inner) | copy-start | bytes 3145732
  78.0 16.0 %collective-permute-start.12 = (f32[2,256,128]{2,1,0:T(8,128)}, f32[2,256,128]{2,1,0:T(8,128)S(1)}, u32[]{:S(2)}, u32[]{:S(2)}) collective-permute-start(f32[2,256,128]{2,1,0:T(8,128)} %get-tuple-element.60), channel_id=1, source_target_pairs={{1,2},{2,1},{3,4},{4,3},{5,6},{6,5},{7,8},{8,7},{9,10},{10,9},{11,... | collective-permute-start | bytes 786440 | tf_op jit(solution)/shard_map/ppermute | solution.py:645
  88.9 22.1 %all-to-all-start.1 = ((f32[128,8,128]{2,1,0:T(8,128)}), f32[128,8,128]{2,1,0:T(8,128)S(1)}, u32[]{:S(2)}, u32[]{:S(2)}) async-start(f32[128,8,128]{2,1,0:T(8,128)} %summed.1), calls=%async_computation.1 | async-start | bytes 1048576 | tf_op jit(solution)/shard_map/all_to_all | solution.py:734
  94.0 2.5 %collective-permute-start.13 = (f32[2,256,128]{2,1,0:T(8,128)S(1)}, f32[2,256,128]{2,1,0:T(8,128)S(1)}, u32[]{:S(2)}, u32[]{:S(2)}) collective-permute-start(f32[2,256,128]{2,1,0:T(8,128)S(1)} %get-tuple-element.63), channel_id=1, source_target_pairs={{0,1},{1,0},{2,3},{3,2},{4,5},{5,4},{6,7},{7,6},{8,9},{9,8},{10,11... | collective-permute-start | bytes 786440 | tf_op jit(solution)/shard_map/ppermute | solution.py:645

commit v6 on v3

--- a/solution.py
+++ b/solution.py
@@ -381,7 +381,8 @@
     ]
     return pl.pallas_call(
         patch_kernel,
-        out_shape=tuple(jax.ShapeDtypeStruct((2,) + shape, jnp.float32) for shape in shapes),
+        out_shape=(pltpu.HBM((2,) + shapes[0], jnp.float32),)
+        + tuple(jax.ShapeDtypeStruct((2,) + shape, jnp.float32) for shape in shapes[1:]),
         in_specs=[smem] * 5 + [anywhere] * 8 + [vmem] * 5,
         out_specs=[anywhere] + [vmem] * 8,
         scratch_shapes=[

time: 111 us -> 117 us (1.054)
  starting transfers between devices: 56.4 us -> 64.4 us
    all_to_all x1, starting transfers between devices: 6.97 us -> 15.5 us  [on_device(): tiles = lax.all_to_all(tiles, AXES, 0, 0, tiled=True)]
    all_to_all x1, starting transfers between devices: 11.4 us -> 9.19 us  [on_device(): shares = lax.all_to_all(shares, CHIPS, 0, 0, tiled=True)]
    ppermute x14, starting transfers between devices: 38.1 us -> 39.7 us  [permuted(): return lax.ppermute(value, AXES, pairs)]
    all_to_all x1, waiting for transfers between devices: 9.23 us -> 7.65 us  [on_device(): tiles = lax.all_to_all(tiles, AXES, 0, 0, tiled=True)]
    unnamed x36 -> x34, local copies, waits for them, and re-layouts: 4.33 us -> 3.36 us
where the time goes in v6:
time: 117 us
  starting transfers between devices  64.4 us (55%)
  waiting for transfers between devices  30.3 us (26%)
  Pallas kernels  13.1 us (11%)
  local copies, waits for them, and re-layouts  4.42 us (4%)
  other arithmetic  3.3 us (3%)
  between operations  1.62 us (1%)
    ppermute x14, starting transfers between devices, permuted(): return lax.ppermute(value, AXES, pairs)  39.7 us
    ppermute x14, waiting for transfers between devices, permuted(): return lax.ppermute(value, AXES, pairs)  16.1 us
    all_to_all x1, starting transfers between devices, on_device(): tiles = lax.all_to_all(tiles, AXES, 0, 0, tiled=True)  15.5 us
    all_to_all x1, starting transfers between devices, on_device(): shares = lax.all_to_all(shares, CHIPS, 0, 0, tiled=True)  9.19 us
    all_to_all x1, waiting for transfers between devices, on_device(): tiles = lax.all_to_all(tiles, AXES, 0, 0, tiled=True)  7.65 us
    all_to_all x1, waiting for transfers between devices, on_device(): shares = lax.all_to_all(shares, CHIPS, 0, 0, tiled=True)  6.56 us
    pallas_call x1, Pallas kernels, patches(): pl.pallas_call(patch_kernel, out_shape=(pltpu.HBM((2,) + shapes[0], jnp.f...  5.91 us
    pallas_call x1, Pallas kernels, shrink_object(): pl.pallas_call(haar_kernel, out_shape=jax.ShapeDtypeStruct(shape, jnp.flo...  3.8 us
  transfers between devices with their start and end apart: 16, of which 6 were waited for; matrix products, arithmetic and copies ran while one was open for 1% of the time, Pallas kernels for 5%

profile of v6, /device:TPU:1, one launch (start us, length us, event | category | flops | bytes accessed | tf_op | source)
XLA Modules:
  0.0 117.2 jit_solution(12941394444553832761)
XLA Ops:
  0.6 1.8 %multiply_add_fusion.centre = f32[2,256,512]{2,1,0:T(8,128)S(1)} fusion(f32[2,256,512]{2,1,0:T(8,128)} %param.11, f32[2,256,512]{2,1,0:T(8,128)} %param.12), kind=kLoop, calls=%fused_computation | loop fusion | flops 786432 | bytes 3145728 | tf_op jit(solution)/shard_map/add | solution.py:643
  2.4 1.0 fusion
  3.4 1.3 %collective-permute-start.1 = (f32[2,128,512]{2,1,0:T(8,128)}, f32[2,128,512]{2,1,0:T(8,128)S(1)}, u32[]{:S(2)}, u32[]{:S(2)}) collective-permute-start(f32[2,128,512]{2,1,0:T(8,128)} %get-tuple-element.72), channel_id=1, source_target_pairs={{16,0},{17,1},{18,2},{19,3},{20,4},{21,5},{22,6},{23,7},{24,8},{25... | collective-permute-start | bytes 1572872 | tf_op jit(solution)/shard_map/ppermute | solution.py:623
  4.7 6.1 %collective-permute-start = (f32[2,128,512]{2,1,0:T(8,128)}, f32[2,128,512]{2,1,0:T(8,128)S(1)}, u32[]{:S(2)}, u32[]{:S(2)}) collective-permute-start(f32[2,128,512]{2,1,0:T(8,128)} %get-tuple-element.73), channel_id=1, source_target_pairs={{0,16},{1,17},{2,18},{3,19},{4,20},{5,21},{6,22},{7,23},{8,24},{9,... | collective-permute-start | bytes 1572872 | tf_op jit(solution)/shard_map/ppermute | solution.py:623
  10.9 0.7 slice_select_fusion.1
  11.6 4.4 %collective-permute-start.5 = (f32[2,256,128]{2,1,0:T(8,128)S(1)}, f32[2,256,128]{2,1,0:T(8,128)S(1)}, u32[]{:S(2)}, u32[]{:S(2)}) collective-permute-start(f32[2,256,128]{2,1,0:T(8,128)S(1)} %get-tuple-element.70), channel_id=1, source_target_pairs={{1,2},{2,1},{3,4},{4,3},{5,6},{6,5},{7,8},{8,7},{9,10},{10,9},{11,... | collective-permute-start | bytes 786440 | tf_op jit(solution)/shard_map/ppermute | solution.py:623
  16.1 4.1 %collective-permute-start.3 = (f32[2,128,128]{2,1,0:T(8,128)S(1)}, f32[2,128,128]{2,1,0:T(8,128)S(1)}, u32[]{:S(2)}, u32[]{:S(2)}) collective-permute-start(f32[2,128,128]{2,1,0:T(8,128)S(1)} %get-tuple-element.75), channel_id=1, source_target_pairs={{1,18},{2,17},{3,20},{4,19},{5,22},{6,21},{7,24},{8,23},{9,26},{10... | collective-permute-start | bytes 393224 | tf_op jit(solution)/shard_map/ppermute | solution.py:623
  20.2 1.3 %collective-permute-start.4 = (f32[2,128,128]{2,1,0:T(8,128)S(1)}, f32[2,128,128]{2,1,0:T(8,128)S(1)}, u32[]{:S(2)}, u32[]{:S(2)}) collective-permute-start(f32[2,128,128]{2,1,0:T(8,128)S(1)} %get-tuple-element.74), channel_id=1, source_target_pairs={{17,2},{18,1},{19,4},{20,3},{21,6},{22,5},{23,8},{24,7},{25,10},{2... | collective-permute-start | bytes 393224 | tf_op jit(solution)/shard_map/ppermute | solution.py:623
  21.5 0.0 collective-permute-done.1.bottom
  21.5 1.8 %collective-permute-start.2 = (f32[2,256,128]{2,1,0:T(8,128)}, f32[2,256,128]{2,1,0:T(8,128)S(1)}, u32[]{:S(2)}, u32[]{:S(2)}) collective-permute-start(f32[2,256,128]{2,1,0:T(8,128)} %get-tuple-element.71), channel_id=1, source_target_pairs={{0,1},{1,0},{2,3},{3,2},{4,5},{5,4},{6,7},{7,6},{8,9},{9,8},{10,11... | collective-permute-start | bytes 786440 | tf_op jit(solution)/shard_map/ppermute | solution.py:623
  23.3 0.0 copy-start.3
  23.3 0.0 collective-permute-done.top
  23.4 0.7 pad_maximum_fusion
  24.1 1.0 collective-permute-done.3.far_top
  25.1 0.7 copy-done.7
  25.7 12.4 %collective-permute-done.4.far_bottom = f32[2,128,128]{2,1,0:T(8,128)S(1)} collective-permute-done((f32[2,128,128]{2,1,0:T(8,128)S(1)}, f32[2,128,128]{2,1,0:T(8,128)S(1)}, u32[]{:S(2)}, u32[]{:S(2)}) %collective-permute-start.4) | collective-permute-done | bytes 131104 | tf_op jit(solution)/shard_map/ppermute | solution.py:623
  38.2 0.7 copy-done.9
  38.8 0.0 collective-permute-done.5.far_mid
  38.8 0.0 collective-permute-start.6
  39.5 0.0 copy-done.3
  39.5 0.0 copy-start.2
  39.5 1.2 %copy-done.2 = f32[1,1,4,256,256]{4,3,2,1,0:T(8,128)S(1)} copy-done((f32[1,1,4,256,256]{4,3,2,1,0:T(8,128)S(1)}, f32[1,1,4,256,256]{4,3,2,1,0:T(8,128)}, u32[]{:S(2)}) %copy-start.2) | copy-done | bytes 1048600
  40.7 0.0 copy-start.8
  40.7 0.0 copy-start.10
  40.7 0.7 ordered_amplitude.1.amplitude
  41.4 0.0 collective-permute-done.2.near_mid
  41.4 0.0 collective-permute-done.6.near_corner
  41.5 0.0 copy-start.11
  41.5 0.0 copy-start.12
  41.5 0.3 copy-done
  41.8 0.1 copy-done.4
  41.9 0.1 copy-done.5
  42.0 0.1 copy-done.6
  42.1 0.0 copy-done.8
  42.1 0.0 copy-done.10
  42.1 0.1 copy-done.11
  42.2 0.0 copy-done.12
  42.3 5.9 %patches.1 = (f32[2,256,512]{2,1,0:T(8,128)}, f32[2,128,512]{2,1,0:T(8,128)S(1)}, f32[2,128,512]{2,1,0:T(8,128)S(1)}, f32[2,256,128]{2,1,0:T(8,128)S(1)}, f32[2,...) custom-call(s32[1]{0:T(128)} %bitcast.10.counts, ...), custom_call_target="tpu_custom_call" | custom-call | tf_op jit(solution)/shard_map/patches/pallas_call | solution.py:382
  48.2 0.0 copy-start.13
  48.2 0.0 copy-start.15
  48.2 1.6 %collective-permute-start.7 = (f32[2,512,128]{2,1,0:T(8,128)S(1)}, f32[2,512,128]{2,1,0:T(8,128)S(1)}, u32[]{:S(2)}, u32[]{:S(2)}) collective-permute-start(f32[2,512,128]{2,1,0:T(8,128)S(1)} %get-tuple-element.43), channel_id=1, source_target_pairs={{0,1},{1,0},{2,3},{3,2},{4,5},{5,4},{6,7},{7,6},{8,9},{9,8},{10,11... | collective-permute-start | bytes 1572872 | tf_op jit(solution)/shard_map/ppermute | solution.py:623
  49.8 1.5 %collective-permute-done.7.given = f32[2,512,128]{2,1,0:T(8,128)S(1)} collective-permute-done((f32[2,512,128]{2,1,0:T(8,128)S(1)}, f32[2,512,128]{2,1,0:T(8,128)S(1)}, u32[]{:S(2)}, u32[]{:S(2)}) %collective-permute-start.7) | collective-permute-done | bytes 524320 | tf_op jit(solution)/shard_map/ppermute | solution.py:623
  51.4 1.0 joined.1
  52.4 7.1 %collective-permute-start.8 = (f32[2,128,512]{2,1,0:T(8,128)S(1)}, f32[2,128,512]{2,1,0:T(8,128)S(1)}, u32[]{:S(2)}, u32[]{:S(2)}) collective-permute-start(f32[2,128,512]{2,1,0:T(8,128)S(1)} %get-tuple-element.53), channel_id=1, source_target_pairs={{0,16},{1,17},{2,18},{3,19},{4,20},{5,21},{6,22},{7,23},{8,24},{9,... | collective-permute-start | bytes 1572872 | tf_op jit(solution)/shard_map/ppermute | solution.py:623
  59.5 1.3 %collective-permute-start.10 = (f32[2,128,128]{2,1,0:T(8,128)}, f32[2,128,128]{2,1,0:T(8,128)S(1)}, u32[]{:S(2)}, u32[]{:S(2)}) collective-permute-start(f32[2,128,128]{2,1,0:T(8,128)} %copy-done.16), channel_id=1, source_target_pairs={{17,2},{18,1},{19,4},{20,3},{21,6},{22,5},{23,8},{24,7},{25,10},{2... | collective-permute-start | bytes 393224 | tf_op jit(solution)/shard_map/ppermute | solution.py:623
  60.7 5.5 %collective-permute-start.11 = (f32[2,128,128]{2,1,0:T(8,128)}, f32[2,128,128]{2,1,0:T(8,128)S(1)}, u32[]{:S(2)}, u32[]{:S(2)}) collective-permute-start(f32[2,128,128]{2,1,0:T(8,128)} %copy-done.15), channel_id=1, source_target_pairs={{1,18},{2,17},{3,20},{4,19},{5,22},{6,21},{7,24},{8,23},{9,26},{10... | collective-permute-start | bytes 393224 | tf_op jit(solution)/shard_map/ppermute | solution.py:623
  66.2 9.2 %all-to-all-start = ((f32[64,8,128]{2,1,0:T(8,128)}), f32[64,8,128]{2,1,0:T(8,128)S(1)}, u32[]{:S(2)}, u32[]{:S(2)}) async-start(f32[64,8,128]{2,1,0:T(8,128)} %get-tuple-element.67), calls=%async_computation | async-start | bytes 524288 | tf_op jit(solution)/shard_map/all_to_all | solution.py:707
  75.4 0.0 collective-permute-done.8.first
  75.4 0.7 collective-permute-start.9
  76.2 0.0 copy-start.1
  76.2 0.0 collective-permute-done.10.far_bottom
  76.2 0.0 collective-permute-done.11.far_top
  76.2 3.2 %collective-permute-start.12 = (f32[2,256,128]{2,1,0:T(8,128)}, f32[2,256,128]{2,1,0:T(8,128)S(1)}, u32[]{:S(2)}, u32[]{:S(2)}) collective-permute-start(f32[2,256,128]{2,1,0:T(8,128)} %get-tuple-element.60), channel_id=1, source_target_pairs={{1,2},{2,1},{3,4},{4,3},{5,6},{6,5},{7,8},{8,7},{9,10},{10,9},{11,... | collective-permute-start | bytes 786440 | tf_op jit(solution)/shard_map/ppermute | solution.py:623
  79.5 6.6 %all-to-all-done.parts = f32[64,8,128]{2,1,0:T(8,128)S(1)} async-done(((f32[64,8,128]{2,1,0:T(8,128)}), f32[64,8,128]{2,1,0:T(8,128)S(1)}, u32[]{:S(2)}, u32[]{:S(2)}) %all-to-all-start) | async-done | bytes 262176 | tf_op jit(solution)/shard_map/all_to_all | solution.py:707
  86.0 0.9 summed.1
  86.9 15.5 %all-to-all-start.1 = ((f32[128,8,128]{2,1,0:T(8,128)}), f32[128,8,128]{2,1,0:T(8,128)S(1)}, u32[]{:S(2)}, u32[]{:S(2)}) async-start(f32[128,8,128]{2,1,0:T(8,128)} %summed.1), calls=%async_computation.1 | async-start | bytes 1048576 | tf_op jit(solution)/shard_map/all_to_all | solution.py:712
  102.4 0.0 collective-permute-done.12.far_mid
  102.4 0.0 collective-permute-done.9.second
  102.5 1.3 %collective-permute-start.13 = (f32[2,256,128]{2,1,0:T(8,128)S(1)}, f32[2,256,128]{2,1,0:T(8,128)S(1)}, u32[]{:S(2)}, u32[]{:S(2)}) collective-permute-start(f32[2,256,128]{2,1,0:T(8,128)S(1)} %copy-done.14), channel_id=1, source_target_pairs={{0,1},{1,0},{2,3},{3,2},{4,5},{5,4},{6,7},{7,6},{8,9},{9,8},{10,11... | collective-permute-start | bytes 786440 | tf_op jit(solution)/shard_map/ppermute | solution.py:623
  103.8 1.2 collective-permute-done.13.near_mid
  104.9 0.0 copy-done.1
  104.9 3.8 %haar.1 = f32[2,256,512]{2,1,0:T(8,128)} custom-call(s32[1]{0:T(128)} %bitcast.core_of, s32[1]{0:T(128)} %bitcast.1.odd_of, f32[2,256,512]{2,1,0:T(8,128)S(1)} %copy-done.1, f32[2,128,512]{2,1,0:T(8,128)S(1)} %collective-permute-done.8.first, f32[2,128,512]{2,1,0:T(8,128)S(1)} %collective-permute-done.9.second, ...), custom_call_target="tpu_custom_call" | custom-call | tf_op jit(solution)/shard_map/haar/pallas_call | solution.py:535
  108.7 7.6 %all-to-all-done.1 = f32[128,8,128]{2,1,0:T(8,128)S(1)} async-done(((f32[128,8,128]{2,1,0:T(8,128)}), f32[128,8,128]{2,1,0:T(8,128)S(1)}, u32[]{:S(2)}, u32[]{:S(2)}) %all-to-all-start.1) | async-done | bytes 524320 | tf_op jit(solution)/shard_map/all_to_all | solution.py:712
  116.4 0.8 laid_out.1
  (17 shorter events, 0.1 us)
Async XLA Ops:
  3.4 18.0 %collective-permute-start.1 = (f32[2,128,512]{2,1,0:T(8,128)}, f32[2,128,512]{2,1,0:T(8,128)S(1)}, u32[]{:S(2)}, u32[]{:S(2)}) collective-permute-start(f32[2,128,512]{2,1,0:T(8,128)} %get-tuple-element.72), channel_id=1, source_target_pairs={{16,0},{17,1},{18,2},{19,3},{20,4},{21,5},{22,6},{23,7},{24,8},{25... | collective-permute-start | bytes 1572872 | tf_op jit(solution)/shard_map/ppermute | solution.py:623
  4.7 18.6 %collective-permute-start = (f32[2,128,512]{2,1,0:T(8,128)}, f32[2,128,512]{2,1,0:T(8,128)S(1)}, u32[]{:S(2)}, u32[]{:S(2)}) collective-permute-start(f32[2,128,512]{2,1,0:T(8,128)} %get-tuple-element.73), channel_id=1, source_target_pairs={{0,16},{1,17},{2,18},{3,19},{4,20},{5,21},{6,22},{7,23},{8,24},{9,... | collective-permute-start | bytes 1572872 | tf_op jit(solution)/shard_map/ppermute | solution.py:623
  11.6 27.2 %collective-permute-start.5 = (f32[2,256,128]{2,1,0:T(8,128)S(1)}, f32[2,256,128]{2,1,0:T(8,128)S(1)}, u32[]{:S(2)}, u32[]{:S(2)}) collective-permute-start(f32[2,256,128]{2,1,0:T(8,128)S(1)} %get-tuple-element.70), channel_id=1, source_target_pairs={{1,2},{2,1},{3,4},{4,3},{5,6},{6,5},{7,8},{8,7},{9,10},{10,9},{11,... | collective-permute-start | bytes 786440 | tf_op jit(solution)/shard_map/ppermute | solution.py:623
  16.1 9.0 %collective-permute-start.3 = (f32[2,128,128]{2,1,0:T(8,128)S(1)}, f32[2,128,128]{2,1,0:T(8,128)S(1)}, u32[]{:S(2)}, u32[]{:S(2)}) collective-permute-start(f32[2,128,128]{2,1,0:T(8,128)S(1)} %get-tuple-element.75), channel_id=1, source_target_pairs={{1,18},{2,17},{3,20},{4,19},{5,22},{6,21},{7,24},{8,23},{9,26},{10... | collective-permute-start | bytes 393224 | tf_op jit(solution)/shard_map/ppermute | solution.py:623
  20.2 18.0 %collective-permute-start.4 = (f32[2,128,128]{2,1,0:T(8,128)S(1)}, f32[2,128,128]{2,1,0:T(8,128)S(1)}, u32[]{:S(2)}, u32[]{:S(2)}) collective-permute-start(f32[2,128,128]{2,1,0:T(8,128)S(1)} %get-tuple-element.74), channel_id=1, source_target_pairs={{17,2},{18,1},{19,4},{20,3},{21,6},{22,5},{23,8},{24,7},{25,10},{2... | collective-permute-start | bytes 393224 | tf_op jit(solution)/shard_map/ppermute | solution.py:623
  21.5 20.0 %collective-permute-start.2 = (f32[2,256,128]{2,1,0:T(8,128)}, f32[2,256,128]{2,1,0:T(8,128)S(1)}, u32[]{:S(2)}, u32[]{:S(2)}) collective-permute-start(f32[2,256,128]{2,1,0:T(8,128)} %get-tuple-element.71), channel_id=1, source_target_pairs={{0,1},{1,0},{2,3},{3,2},{4,5},{5,4},{6,7},{7,6},{8,9},{9,8},{10,11... | collective-permute-start | bytes 786440 | tf_op jit(solution)/shard_map/ppermute | solution.py:623
  23.3 16.2 %copy-start.3 = (bf16[768,256]{1,0:T(8,128)(2,1)S(1)}, bf16[768,256]{1,0:T(8,128)(2,1)}, u32[]{:S(2)}) copy-start(bf16[768,256]{1,0:T(8,128)(2,1)} %constant.42.clone.table) | copy-start | bytes 1179652
  25.1 0.7 copy-start.7
  38.2 0.7 copy-start.9
  38.8 2.6 %collective-permute-start.6 = (f32[2,256,128]{2,1,0:T(8,128)}, f32[2,256,128]{2,1,0:T(8,128)}, u32[]{:S(2)}, u32[]{:S(2)}) collective-permute-start(f32[2,256,128]{2,1,0:T(8,128)} %pad_maximum_fusion), channel_id=1, source_target_pairs={{0,1},{1,0},{2,3},{3,2},{4,5},{5,4},{6,7},{7,6},{8,9},{9,8},{10,11... | collective-permute-start | bytes 786440 | tf_op jit(solution)/shard_map/ppermute | solution.py:623
  39.5 1.2 %copy-start.2 = (f32[1,1,4,256,256]{4,3,2,1,0:T(8,128)S(1)}, f32[1,1,4,256,256]{4,3,2,1,0:T(8,128)}, u32[]{:S(2)}) copy-start(f32[1,1,4,256,256]{4,3,2,1,0:T(8,128)} %param.14) | copy-start | bytes 3145732
  40.7 1.0 copy-start
  40.7 1.2 copy-start.4
  40.7 1.3 %copy-start.5 = (bf16[768,256]{1,0:T(8,128)(2,1)S(1)}, bf16[768,256]{1,0:T(8,128)(2,1)}, u32[]{:S(2)}) copy-start(bf16[768,256]{1,0:T(8,128)(2,1)} %constant.44.clone.right_table) | copy-start | bytes 1179652
  40.7 1.3 %copy-start.6 = (f32[4,128,128]{2,1,0:T(8,128)S(1)}, f32[4,128,128]{2,1,0:T(8,128)}, u32[]{:S(2)}) copy-start(f32[4,128,128]{2,1,0:T(8,128)} %constant.45.clone.twiddle_table) | copy-start | bytes 786436
  40.7 1.4 %copy-start.8 = (f32[2,128,128]{2,1,0:T(8,128)S(1)}, f32[2,128,128]{2,1,0:T(8,128)}, u32[]{:S(2)}) copy-start(f32[2,128,128]{2,1,0:T(8,128)} %copy-done.7) | copy-start | bytes 393220
  40.7 1.4 %copy-start.10 = (f32[2,128,128]{2,1,0:T(8,128)S(1)}, f32[2,128,128]{2,1,0:T(8,128)}, u32[]{:S(2)}) copy-start(f32[2,128,128]{2,1,0:T(8,128)} %copy-done.9) | copy-start | bytes 393220
  41.5 0.8 copy-start.11
  41.5 0.8 copy-start.12
  48.2 4.2 %copy-start.13 = (f32[2,256,128]{2,1,0:T(8,128)}, f32[2,256,128]{2,1,0:T(8,128)S(1)}, u32[]{:S(2)}) copy-start(f32[2,256,128]{2,1,0:T(8,128)S(1)} %get-tuple-element.63) | copy-start | bytes 786436
  48.2 4.2 %copy-start.15 = (f32[2,128,128]{2,1,0:T(8,128)}, f32[2,128,128]{2,1,0:T(8,128)S(1)}, u32[]{:S(2)}) copy-start(f32[2,128,128]{2,1,0:T(8,128)S(1)} %get-tuple-element.59) | copy-start | bytes 393220
  48.2 4.2 %copy-start.16 = (f32[2,128,128]{2,1,0:T(8,128)}, f32[2,128,128]{2,1,0:T(8,128)S(1)}, u32[]{:S(2)}) copy-start(f32[2,128,128]{2,1,0:T(8,128)S(1)} %get-tuple-element.58) | copy-start | bytes 393220
  48.2 3.1 %collective-permute-start.7 = (f32[2,512,128]{2,1,0:T(8,128)S(1)}, f32[2,512,128]{2,1,0:T(8,128)S(1)}, u32[]{:S(2)}, u32[]{:S(2)}) collective-permute-start(f32[2,512,128]{2,1,0:T(8,128)S(1)} %get-tuple-element.43), channel_id=1, source_target_pairs={{0,1},{1,0},{2,3},{3,2},{4,5},{5,4},{6,7},{7,6},{8,9},{9,8},{10,11... | collective-permute-start | bytes 1572872 | tf_op jit(solution)/shard_map/ppermute | solution.py:623
  52.4 23.1 %collective-permute-start.8 = (f32[2,128,512]{2,1,0:T(8,128)S(1)}, f32[2,128,512]{2,1,0:T(8,128)S(1)}, u32[]{:S(2)}, u32[]{:S(2)}) collective-permute-start(f32[2,128,512]{2,1,0:T(8,128)S(1)} %get-tuple-element.53), channel_id=1, source_target_pairs={{0,16},{1,17},{2,18},{3,19},{4,20},{5,21},{6,22},{7,23},{8,24},{9,... | collective-permute-start | bytes 1572872 | tf_op jit(solution)/shard_map/ppermute | solution.py:623
  59.5 16.7 %collective-permute-start.10 = (f32[2,128,128]{2,1,0:T(8,128)}, f32[2,128,128]{2,1,0:T(8,128)S(1)}, u32[]{:S(2)}, u32[]{:S(2)}) collective-permute-start(f32[2,128,128]{2,1,0:T(8,128)} %copy-done.16), channel_id=1, source_target_pairs={{17,2},{18,1},{19,4},{20,3},{21,6},{22,5},{23,8},{24,7},{25,10},{2... | collective-permute-start | bytes 393224 | tf_op jit(solution)/shard_map/ppermute | solution.py:623
  60.7 15.5 %collective-permute-start.11 = (f32[2,128,128]{2,1,0:T(8,128)}, f32[2,128,128]{2,1,0:T(8,128)S(1)}, u32[]{:S(2)}, u32[]{:S(2)}) collective-permute-start(f32[2,128,128]{2,1,0:T(8,128)} %copy-done.15), channel_id=1, source_target_pairs={{1,18},{2,17},{3,20},{4,19},{5,22},{6,21},{7,24},{8,23},{9,26},{10... | collective-permute-start | bytes 393224 | tf_op jit(solution)/shard_map/ppermute | solution.py:623
  66.2 19.8 %all-to-all-start = ((f32[64,8,128]{2,1,0:T(8,128)}), f32[64,8,128]{2,1,0:T(8,128)S(1)}, u32[]{:S(2)}, u32[]{:S(2)}) async-start(f32[64,8,128]{2,1,0:T(8,128)} %get-tuple-element.67), calls=%async_computation | async-start | bytes 524288 | tf_op jit(solution)/shard_map/all_to_all | solution.py:707
  75.4 27.0 %collective-permute-start.9 = (f32[2,128,512]{2,1,0:T(8,128)}, f32[2,128,512]{2,1,0:T(8,128)S(1)}, u32[]{:S(2)}, u32[]{:S(2)}) collective-permute-start(f32[2,128,512]{2,1,0:T(8,128)} %get-tuple-element.56), channel_id=1, source_target_pairs={{16,32},{17,33},{18,34},{19,35},{20,36},{21,37},{22,38},{23,39},{2... | collective-permute-start | bytes 1572872 | tf_op jit(solution)/shard_map/ppermute | solution.py:623
  76.2 28.8 %copy-start.1 = (f32[2,256,512]{2,1,0:T(8,128)S(1)}, f32[2,256,512]{2,1,0:T(8,128)}, u32[]{:S(2)}) copy-start(f32[2,256,512]{2,1,0:T(8,128)} %get-tuple-element.40.inner) | copy-start | bytes 3145732
  76.2 26.2 %collective-permute-start.12 = (f32[2,256,128]{2,1,0:T(8,128)}, f32[2,256,128]{2,1,0:T(8,128)S(1)}, u32[]{:S(2)}, u32[]{:S(2)}) collective-permute-start(f32[2,256,128]{2,1,0:T(8,128)} %get-tuple-element.60), channel_id=1, source_target_pairs={{1,2},{2,1},{3,4},{4,3},{5,6},{6,5},{7,8},{8,7},{9,10},{10,9},{11,... | collective-permute-start | bytes 786440 | tf_op jit(solution)/shard_map/ppermute | solution.py:623
  86.9 15.5 %copy-start.14 = (f32[2,256,128]{2,1,0:T(8,128)S(1)}, f32[2,256,128]{2,1,0:T(8,128)}, u32[]{:S(2)}) copy-start(f32[2,256,128]{2,1,0:T(8,128)} %copy-done.13) | copy-start | bytes 786436
  86.9 29.5 %all-to-all-start.1 = ((f32[128,8,128]{2,1,0:T(8,128)}), f32[128,8,128]{2,1,0:T(8,128)S(1)}, u32[]{:S(2)}, u32[]{:S(2)}) async-start(f32[128,8,128]{2,1,0:T(8,128)} %summed.1), calls=%async_computation.1 | async-start | bytes 1048576 | tf_op jit(solution)/shard_map/all_to_all | solution.py:712
  102.5 2.5 %collective-permute-start.13 = (f32[2,256,128]{2,1,0:T(8,128)S(1)}, f32[2,256,128]{2,1,0:T(8,128)S(1)}, u32[]{:S(2)}, u32[]{:S(2)}) collective-permute-start(f32[2,256,128]{2,1,0:T(8,128)S(1)} %copy-done.14), channel_id=1, source_target_pairs={{0,1},{1,0},{2,3},{3,2},{4,5},{5,4},{6,7},{7,6},{8,9},{9,8},{10,11... | collective-permute-start | bytes 786440 | tf_op jit(solution)/shard_map/ppermute | solution.py:623
